TPU v7x, 32 devices: a whole 2x2x4 slice. The times are simulated.
32 devices in a mesh: dp: 8 (over y, x, core), head: 4 (over z).
Axes of the slice: x: 2, y: 2, z: 4, core: 2. Of those that a mesh axis runs over, the one named last changes fastest.
Arguments:
- patch_observations: bfloat16 [4096, 32], P(('dp', 'head')), may hold values from -6 to 6
- sequence_labels: int32 [32, 128], P(('dp', 'head')), may hold values from 0 to 41, never falling along the last dimension, each value on 1 to 64 neighbouring positions
- leading_filler_count: int32 [32, 42], P(('dp', 'head')), may hold values from 0 to 32
- intake_latent_matrix: bfloat16 [64, 1280], replicated, may hold values from -0.75 to 0.75
- intake_latent_offset: float32 [1280], replicated, may hold values from -3 to 3
- intake_emit_matrix: bfloat16 [1280, 1280], replicated, may hold values from -0.15625 to 0.15625
- intake_emit_offset: float32 [1280], replicated, may hold values from -2 to 2
- intake_shortcut_matrix: bfloat16 [64, 1280], replicated, may hold values from -0.75 to 0.75
- attention_entry_matrices: bfloat16 [2, 1280, 3840], P(None, ('dp', 'head')), may hold values from -0.15625 to 0.15625
- attention_merge_matrix: bfloat16 [2, 1280, 1280], P(None, ('dp', 'head')), may hold values from -0.3125 to 0.3125
- feedforward_widen_matrix: bfloat16 [2, 1280, 1280], P(None, ('dp', 'head')), may hold values from -0.15625 to 0.15625
- feedforward_shrink_matrix: bfloat16 [2, 1280, 1280], P(None, ('dp', 'head')), may hold values from -0.15625 to 0.15625
- layer_scale_factors: bfloat16 [2, 2, 1280], P(None, None, ('dp', 'head')), may hold values from 0.5 to 1.5
- readout_latent_matrix: bfloat16 [1280, 1280], P(None, 'head'), may hold values from -0.15625 to 0.15625
- readout_latent_offset: float32 [1280], P('head'), may hold values from -3 to 3
- readout_emit_matrix: bfloat16 [1280, 1280], P(None, 'head'), may hold values from -0.15625 to 0.15625
- readout_emit_offset: float32 [1280], P('head'), may hold values from -2 to 2
- readout_shortcut_matrix: bfloat16 [1280, 1280], P(None, 'head'), may hold values from -0.15625 to 0.15625
- loss_sensitivity: bfloat16 [4096, 1280], P('dp', 'head'), may hold values from -6 to 6
Outputs:
- token_predictions: bfloat16 [4096, 1280], P('dp', 'head')
- values_grad: float32 [4096, 32], P(('dp', 'head'))
- entry_inner_grad: float32 [64, 1280], replicated
- entry_inner_bias_grad: float32 [1280], replicated
- entry_outer_grad: float32 [1280, 1280], replicated
- entry_outer_bias_grad: float32 [1280], replicated
- entry_skip_grad: float32 [64, 1280], replicated
- qkv_weight_grad: float32 [2, 1280, 3840], P(None, ('dp', 'head'))
- out_weight_grad: float32 [2, 1280, 1280], P(None, ('dp', 'head'))
- up_weight_grad: float32 [2, 1280, 1280], P(None, ('dp', 'head'))
- down_weight_grad: float32 [2, 1280, 1280], P(None, ('dp', 'head'))
- norm_gains_grad: float32 [2, 2, 1280], P(None, None, ('dp', 'head'))
- head_inner_grad: float32 [1280, 1280], P(None, 'head')
- head_inner_bias_grad: float32 [1280], P('head')
- head_outer_grad: float32 [1280, 1280], P(None, 'head')
- head_outer_bias_grad: float32 [1280], P('head')
- head_skip_grad: float32 [1280, 1280], P(None, 'head')
Inputs may be any that keep to these rules, and one draw needn't show every extreme that they name: `sequence_labels`: each row lists the series numbers of one device's 128 tokens in order, rising by one from series to series and starting at 0; each series has 1 to 64 tokens and one series of every device has exactly 64.
All inputs are finite; a program needn't handle non-finite values.
Results may differ from a plain program's by a relative error of at most 0.023.
Values may be sent and summed in bfloat16 or wider, within the bound.
No kernel may reach another device: no remote copies, remote signals or barrier semaphores. Data moves between devices by JAX's collectives and lax.ppermute only.
A program may use at most 192 MiB of HBM per device.

v0:
```python
from functools import partial
import math

import jax
import jax.numpy as jnp
from jax import lax
from jax.experimental import pallas as pl
from jax.experimental.pallas import tpu as pltpu
from jax.sharding import PartitionSpec as P

MODEL_WIDTH = 1280
HEADS = 16
HEAD_DIM = 80


EPS = 1e-06
SMALL_COST = pl.CostEstimate(flops=1, bytes_accessed=1, transcendentals=0)
ROPE_BASE = 10000.0


def layout_rows(series_row, pad_row, patch_len):
    count = series_row.shape[0]
    order = jnp.arange(count, dtype=jnp.int32)
    same_series = series_row[:, None] == series_row[None, :]
    earlier = order[None, :] < order[:, None]
    position = jnp.sum(jnp.logical_and(same_series, earlier).astype(jnp.int32), axis=1)
    numbers = jnp.arange(pad_row.shape[0], dtype=jnp.int32)
    series_pad = jnp.sum(
        jnp.where(series_row[:, None] == numbers[None, :], pad_row[None, :], 0), axis=1
    )
    pad_count = jnp.where(position == 0, series_pad, 0)
    padded = pad_count == patch_len
    diagonal = order[:, None] == order[None, :]
    reach = jnp.logical_or(jnp.logical_and(earlier, jnp.logical_not(padded)[None, :]), diagonal)
    allowed = jnp.logical_and(same_series, reach)
    keep_rows = jnp.where(padded, 0.0, 1.0).astype(jnp.float32)
    return (position, pad_count, allowed, keep_rows)


def rotary_tables(position, head_dim):
    half = head_dim // 2
    steps = jnp.arange(half, dtype=jnp.float32) / half
    inverse = jnp.exp(-math.log(ROPE_BASE) * steps)
    angles = position.astype(jnp.float32)[:, None] * inverse[None, :]
    return (jnp.cos(angles)[:, None, :], jnp.sin(angles)[:, None, :])


def rotate(heads_rows, cosine, sine):
    half = heads_rows.shape[-1] // 2
    first = heads_rows[..., :half]
    second = heads_rows[..., half:]
    return jnp.concatenate(
        [first * cosine - second * sine, second * cosine + first * sine], axis=-1
    )


def unrotate(grad_rows, cosine, sine):
    half = grad_rows.shape[-1] // 2
    first = grad_rows[..., :half]
    second = grad_rows[..., half:]
    return jnp.concatenate(
        [first * cosine + second * sine, second * cosine - first * sine], axis=-1
    )


def norm_apply(resid, gain):
    return resid * lax.rsqrt(jnp.mean(resid * resid, axis=-1, keepdims=True) + EPS) * gain


def dyadic_accumulation(left, right):
    return lax.dot_general(
        left, right, (((0,), (0,)), ((), ())), preferred_element_type=jnp.float32
    )


def reverse_matmul_answer(grad_rows, weight):
    return lax.dot_general(
        grad_rows, weight, (((1,), (1,)), ((), ())), preferred_element_type=jnp.float32
    )


def masked_scores(query_rows, key_rows, allowed):
    scale = 1.0 / math.sqrt(query_rows.shape[-1])
    scores = (
        jnp.einsum("qhd,khd->hqk", query_rows, key_rows, preferred_element_type=jnp.float32) * scale
    )
    return jnp.where(allowed[None], scores, -1e30)


def attend_forward(query_rows, key_rows, value_rows, allowed):
    scores = masked_scores(query_rows, key_rows, allowed)
    peak = jnp.max(scores, axis=-1, keepdims=True)
    weights = jnp.exp(scores - peak)
    total = jnp.sum(weights, axis=-1, keepdims=True)
    probs = (weights / total).astype(jnp.bfloat16)
    mixed = jnp.einsum("hqk,khd->qhd", probs, value_rows, preferred_element_type=jnp.float32)
    return (mixed, peak + jnp.log(total))


def attend_backward(query_rows, key_rows, value_rows, allowed, log_total, grad_mixed):
    scale = 1.0 / math.sqrt(query_rows.shape[-1])
    scores = masked_scores(query_rows, key_rows, allowed)
    probs = jnp.where(allowed[None], jnp.exp(scores - log_total), 0.0)
    grad_probs = jnp.einsum(
        "qhd,khd->hqk", grad_mixed, value_rows, preferred_element_type=jnp.float32
    )
    grad_values = jnp.einsum(
        "hqk,qhd->khd", probs.astype(jnp.bfloat16), grad_mixed, preferred_element_type=jnp.float32
    )
    center = jnp.sum(grad_probs * probs, axis=-1, keepdims=True)
    grad_scores = (probs * (grad_probs - center)).astype(jnp.bfloat16)
    grad_query = (
        jnp.einsum("hqk,khd->qhd", grad_scores, key_rows, preferred_element_type=jnp.float32)
        * scale
    )
    grad_keys = (
        jnp.einsum("hqk,qhd->khd", grad_scores, query_rows, preferred_element_type=jnp.float32)
        * scale
    )
    return (grad_query, grad_keys, grad_values)


def after(value, *earlier):
    return lax.optimization_barrier((value, *earlier))[0]


def swap(v, bit):
    size = lax.axis_size("dp")
    return lax.ppermute(v, "dp", [(i, i ^ (1 << bit)) for i in range(size)])


def outer_groups():
    size = lax.axis_size("dp")
    return [[j + 8 * o for o in range(size // 8)] for j in range(8)]


def place_kernel(plan, piece_count, out_count, me_ref, *refs):
    pieces = refs[:piece_count]
    outs = refs[piece_count : piece_count + out_count]
    held = refs[piece_count + out_count : piece_count + 2 * out_count]
    in_sems, out_sems = refs[piece_count + 2 * out_count :]
    inward, outward = [], []
    for n, (piece, rel, row, out, column) in enumerate(plan):
        source = pieces[piece]
        width = held[out].shape[-1]
        if width != source.shape[-1]:
            source = source.at[:, :, pl.ds(column, width)]
        spot = (slice(None), me_ref[0] ^ rel, pl.ds(row, source.shape[1]), slice(None))
        inward.append(pltpu.make_async_copy(source, held[out].at[spot], in_sems.at[n]))
        outward.append(
            pltpu.make_async_copy(held[out].at[spot], outs[out].at[spot], out_sems.at[n])
        )
    for copy in inward:
        copy.start()
    for copy, onward in zip(inward, outward):
        copy.wait()
        onward.start()
    for onward in outward:
        onward.wait()


def place(me, pieces, widths, first=0):
    plan = []
    for n, (rel, row, _) in enumerate(pieces):
        column = first
        for out, width in enumerate(widths):
            plan.append((n, rel, row, out, column))
            column += width
    arrays = [array for _, _, array in pieces]
    lead, rows, _ = arrays[0].shape
    kind = arrays[0].dtype
    total = sum(8 * lead * rows * -(-w // 128) * 128 for w in widths) * 2
    outs = pl.pallas_call(
        partial(place_kernel, plan, len(arrays), len(widths)),
        out_shape=[jax.ShapeDtypeStruct((lead, 8, rows, w), kind) for w in widths],
        in_specs=[pl.BlockSpec(memory_space=pltpu.SMEM)]
        + [pl.BlockSpec(memory_space=pl.ANY)] * len(arrays),
        out_specs=[pl.BlockSpec(memory_space=pl.ANY)] * len(widths),
        scratch_shapes=[pltpu.VMEM((lead, 8, rows, w), kind) for w in widths]
        + [pltpu.SemaphoreType.DMA((len(plan),))] * 2,
        compiler_params=pltpu.CompilerParams(vmem_limit_bytes=total + (4 << 20)),
        cost_estimate=SMALL_COST,
    )(me, *arrays)
    outer = lax.axis_size("dp") // 8
    return [o.reshape(-1, outer * 8 * rows, o.shape[-1]) for o in outs]


def row_half(rows):
    return rows // 32 * 16 if rows >= 32 else rows // 2


def second_step(held, from_x, from_y):
    half = row_half(held.shape[1])
    return from_y[:, :half], from_x[:, half:]


def all_pieces(near, far, near_met, far_met):
    half = far[0].shape[1]
    places = ((0, 0), (2, 0), (4, 0), (6, 0), (6, half))
    pieces = []
    for (rel, row), array, met in zip(places, (*near, *far), (*near_met, *far_met), strict=True):
        pieces += [(rel, row, array), (rel | 1, row, met)]
    return pieces


def spread_rows(held):
    near = (held, swap(held, 1), swap(held, 2))
    onward_x, onward_y = second_step(*near)
    far = (swap(onward_x, 1), swap(onward_y, 2))
    return all_pieces(near, far, [swap(part, 0) for part in near], [swap(part, 0) for part in far])


def gather_head(own):
    held = lax.all_gather(own, "head", axis=0, tiled=True)[None]
    if lax.axis_size("dp") > 8:
        held = lax.all_gather(
            held, "dp", axis=0, tiled=True, axis_index_groups=outer_groups()
        )
    return held


def product_kernel(count, outer, me_ref, *refs):
    lefts, rights, met_lefts, met_rights = (refs[n * count : (n + 1) * count] for n in range(4))
    to_x, to_y, later, own, right_pair, turned = refs[4 * count :]
    rows, width = own.shape[1] // outer, own.shape[-1]
    tokens = lefts[0].shape[0]
    half = width // 2
    tile = half if half <= 640 else 640
    odd = me_ref[0] & 1 == 1
    chip = me_ref[0] >> 1

    def store(rel, n, span, side, columns, total):
        if rel == 0:
            own[n, span, slice(side * half + columns.start, side * half + columns.stop)] = total
        elif rel == 1 and side == 0:
            to_x[1, n, span, columns] = total
        elif rel == 1:
            later[1, n, span, columns] = total
        elif rel == 2 and side == 0:
            later[0, n, span, columns] = total
        elif rel == 2:
            to_y[1, n, span, columns] = total
        elif side == 0:
            to_x[0, n, span, columns] = total
        else:
            to_y[0, n, span, columns] = total

    for n in range(count):
        right_pair[:tokens] = rights[n][...]
        right_pair[tokens:] = met_rights[n][...]
        for part in range(outer):
            span = slice(part * rows, (part + 1) * rows)
            for place in range(4):
                first = (part * 8 + 2 * place) * rows
                near, far = slice(first, first + rows), slice(first + rows, first + 2 * rows)
                left_pair = jnp.concatenate(
                    [
                        jnp.where(odd, side[n][:, far], side[n][:, near]).astype(jnp.float32)
                        for side in (lefts, met_lefts)
                    ],
                    axis=0,
                )
                turned[place] = left_pair.T.astype(own.dtype)
            every = turned[...].reshape(4 * rows, 2 * tokens)
            for side in range(2):
                for at in range(0, half, tile):
                    total = jnp.dot(
                        every,
                        right_pair[:, side * half + at : side * half + at + tile],
                        preferred_element_type=jnp.float32,
                    ).astype(own.dtype)
                    for place in range(4):
                        for rel in range(4):
                            pl.when(chip ^ place == rel)(
                                partial(
                                    store,
                                    rel,
                                    n,
                                    span,
                                    side,
                                    slice(at, at + tile),
                                    total[place * rows : (place + 1) * rows],
                                )
                            )


def exchange(pairs):
    met = {}
    for pair in pairs:
        for rows in pair:
            if id(rows) not in met:
                met[id(rows)] = swap(rows, 0)
    return [(left, right, met[id(left)], met[id(right)]) for left, right in pairs]


def pair_products(me, both):
    outer = lax.axis_size("dp") // 8
    count = len(both)
    left, right = both[0][:2]
    block, width = left.shape[1] // 8, right.shape[1]
    low = jnp.bfloat16
    return pl.pallas_call(
        partial(product_kernel, count, outer),
        out_shape=[
            jax.ShapeDtypeStruct((2, count, block, width // 2), low),
            jax.ShapeDtypeStruct((2, count, block, width // 2), low),
            jax.ShapeDtypeStruct((2, count, block, width // 2), low),
            jax.ShapeDtypeStruct((count, block, width), low),
        ],
        in_specs=[pl.BlockSpec(memory_space=pltpu.SMEM)]
        + [pl.BlockSpec(memory_space=pltpu.VMEM)] * (4 * count),
        out_specs=[pl.BlockSpec(memory_space=pltpu.VMEM)] * 4,
        scratch_shapes=[
            pltpu.VMEM((2 * left.shape[0], width), low),
            pltpu.VMEM((4, block // outer, 2 * left.shape[0]), low),
        ],
        compiler_params=pltpu.CompilerParams(vmem_limit_bytes=44 << 20),
        cost_estimate=SMALL_COST,
    )((me & 7).reshape(1), *[part for parts in zip(*both, strict=True) for part in parts])


def low_sum(*parts):
    total = parts[0].astype(jnp.float32)
    for part in parts[1:]:
        total = total + part.astype(jnp.float32)
    return total.astype(jnp.bfloat16)


class RowSums:
    def __init__(self, to_x, to_y, later, own):
        self.sent, self.later, self.own = (to_x, to_y), later, own

    def first(self):
        return swap(self.sent[0], 1), swap(self.sent[1], 2)

    def last(self):
        return (
            swap(low_sum(self.later[0], self.met[0][0]), 2),
            swap(low_sum(self.later[1], self.met[1][0]), 1),
        )

    def total(self):
        half = self.own.shape[-1] // 2
        return jnp.concatenate(
            [
                low_sum(self.own[..., :half], self.met[0][1], self.last_met[0]),
                low_sum(self.own[..., half:], self.met[1][1], self.last_met[1]),
            ],
            axis=-1,
        )


def sum_group(total):
    outer = lax.axis_size("dp") // 8
    group = lax.axis_size("head")
    lead = total.shape[:-2]
    rows, columns = total.shape[-2:]
    if outer > 1:
        total = lax.psum_scatter(
            total.reshape(*lead, outer, rows // outer, columns),
            "dp",
            scatter_dimension=len(lead),
            tiled=True,
            axis_index_groups=outer_groups(),
        )
    total = total.reshape(*lead, rows // outer, columns)
    return lax.psum_scatter(total, "head", scatter_dimension=len(lead), tiled=True)


def sum_group_at_once(total):
    outer = lax.axis_size("dp") // 8
    group = lax.axis_size("head")
    if outer > 1:
        return sum_group(total).astype(jnp.float32)
    lead = total.shape[:-2]
    rows, columns = total.shape[-2:]
    total = total.reshape(*lead, group, rows // group, columns)
    axis = len(lead)
    met = lax.all_to_all(total, "head", split_axis=axis, concat_axis=axis, tiled=True)
    return jnp.sum(met.astype(jnp.float32), axis=axis)


def sum_columns(total):
    group = lax.axis_size("head")
    if lax.axis_size("dp") > 8:
        total = lax.psum(total, "dp", axis_index_groups=outer_groups())
    count, rows, columns = total.shape
    total = jnp.moveaxis(total.reshape(count, rows, group, columns // group), 2, 0)
    return lax.psum_scatter(total, "head", scatter_dimension=0, tiled=True)[0]


def gather_blocks(me, summed):
    outer = lax.axis_size("dp") // 8
    count, rows, columns = summed.shape
    if outer == 1:
        whole = lax.all_gather(summed, "dp", axis=0)
        return [whole[:, n].reshape(8 * rows, columns) for n in range(count)]
    held = summed.reshape(count * outer, rows // outer, columns)
    return place((me & 7).reshape(1), spread_rows(held), [columns])[0]


EXTRA_ROWS = 8


def entry_products(me, main, extra):
    group = lax.axis_size("head")
    outer = lax.axis_size("dp") // 8
    devices = 8 * outer * group
    columns = main.shape[1]
    own = main.shape[0] // devices
    extra = jnp.pad(extra, ((0, EXTRA_ROWS * devices - extra.shape[0]), (0, 0)))
    rows = jnp.concatenate(
        [main.reshape(devices, own, columns), extra.reshape(devices, EXTRA_ROWS, columns)], axis=1
    ).astype(jnp.bfloat16)
    view = rows.reshape(outer, 4, 2, group * (own + EXTRA_ROWS), columns)
    core = me & 1
    other = lax.dynamic_index_in_dim(view, 1 - core, 2, keepdims=False)
    pair = low_sum(lax.dynamic_index_in_dim(view, core, 2, keepdims=False), swap(other, 0))
    chip = (me & 7) >> 1
    half = columns // 2

    def picked(rel):
        return lax.dynamic_index_in_dim(pair, chip ^ rel, 1, keepdims=False).reshape(-1, columns)

    own_rows, at_x, at_y, far = (picked(rel) for rel in range(4))
    return RowSums(
        jnp.stack([far[:, :half], at_x[:, :half]]),
        jnp.stack([far[:, half:], at_y[:, half:]]),
        (at_y[:, :half], at_x[:, half:]),
        own_rows,
    )


def silu_parts(x):
    gate = 1.0 / (1.0 + jnp.exp(-x))
    return x * gate, gate * (1.0 + x * (1.0 - gate))


def output_kernel(
    plan, me_ref, top_ref, keep_ref, latent_offset, emit_offset, sensitivity, *refs
):
    pieces = refs[: len(plan)]
    hidden_ref, forecast_ref, pre_low_ref, grad_ref, bias_ref = refs[len(plan) : len(plan) + 5]
    whole, pre, skips, sent, both, sems = refs[len(plan) + 5 :]
    group, width, _ = whole.shape
    each = sensitivity.shape[2]
    two = 2 * each
    rows = width // 8
    copies = []
    for part in range(group):
        copies.append([])
        for n, (rel, row, count) in enumerate(plan):
            first = pl.multiple_of((me_ref[0] ^ rel) * rows + row, 16)
            spot = whole.at[part, pl.ds(first, count), :]
            sem = sems.at[part * len(plan) + n]
            copies[part].append(pltpu.make_async_copy(pieces[n].at[part], spot, sem))
            copies[part][n].start()
    top = top_ref[...]
    keep = keep_ref[...]
    for part in range(group):
        arrive(copies[part])
        both[...] = jnp.dot(top, whole[part, :, :two], preferred_element_type=jnp.float32)
        pre[:, part * each : (part + 1) * each] = both[:, :each] + latent_offset[part : part + 1]
        skips[part] = both[:, each:two] + emit_offset[part : part + 1]
    hidden, slope = silu_parts(pre[...])
    hidden = hidden.astype(jnp.bfloat16)
    hidden_ref[...] = hidden
    for part in range(group):
        emitted = jnp.dot(hidden, whole[part, :, two:], preferred_element_type=jnp.float32)
        forecast_ref[part] = ((emitted + skips[part]) * keep).astype(jnp.bfloat16)

    def back_hidden(n, _):
        at = pl.multiple_of(n * 256, 256)
        total = reverse_matmul_answer(whole[0, pl.ds(at, 256), two:], sensitivity[0])
        for part in range(1, group):
            total += reverse_matmul_answer(whole[part, pl.ds(at, 256), two:], sensitivity[part])
        grad_ref[:, pl.ds(at, 256)] = total.T
        return 0

    lax.fori_loop(0, width // 256, back_hidden, 0)
    pre[...] = grad_ref[...] * slope
    pre_low_ref[...] = pre[...].astype(jnp.bfloat16)
    bias_ref[...] = jnp.sum(pre_low_ref[...].astype(jnp.float32), axis=0, keepdims=True)
    for part in range(group):
        both[:, :each] = pre[:, part * each : (part + 1) * each]
        both[:, each:] = sensitivity[part].astype(jnp.float32)
        sent[part] = both[...].astype(jnp.bfloat16)

    def back_top(n, _):
        at = pl.multiple_of(n * 256, 256)
        total = reverse_matmul_answer(whole[0, pl.ds(at, 256), :two], sent[0])
        for part in range(1, group):
            total += reverse_matmul_answer(whole[part, pl.ds(at, 256), :two], sent[part])
        grad_ref[:, pl.ds(at, 256)] = total.T
        return 0

    lax.fori_loop(0, width // 256, back_top, 0)


def output_block(me, pieces, top, keep, latent_offsets, emit_offsets, grad_forecast):
    plan = [(rel, row, array.shape[1]) for rel, row, array in pieces]
    group, rows, each = grad_forecast.shape
    width = top.shape[1]
    vmem = pl.BlockSpec(memory_space=pltpu.VMEM)
    return pl.pallas_call(
        partial(output_kernel, plan),
        out_shape=[
            jax.ShapeDtypeStruct((rows, width), LOW),
            jax.ShapeDtypeStruct((group, rows, each), LOW),
            jax.ShapeDtypeStruct((rows, width), LOW),
            jax.ShapeDtypeStruct((rows, width), FULL),
            jax.ShapeDtypeStruct((1, width), FULL),
        ],
        in_specs=[pl.BlockSpec(memory_space=pltpu.SMEM)]
        + [vmem] * 5
        + [pl.BlockSpec(memory_space=pl.ANY)] * len(pieces),
        out_specs=[vmem] * 5,
        scratch_shapes=[
            pltpu.VMEM((group, width, 3 * each), LOW),
            pltpu.VMEM((rows, width), FULL),
            pltpu.VMEM((group, rows, each), FULL),
            pltpu.VMEM((group, rows, 2 * each), LOW),
            pltpu.VMEM((rows, 2 * each), FULL),
            pltpu.SemaphoreType.DMA((group * len(pieces),)),
        ],
        compiler_params=pltpu.CompilerParams(vmem_limit_bytes=44 << 20),
        cost_estimate=SMALL_COST,
    )(
        me,
        top,
        keep,
        latent_offsets,
        emit_offsets,
        grad_forecast,
        *[array for _, _, array in pieces],
    )


def output_plain(head_whole, top, keep, latent_offsets, emit_offsets, grad_forecast):
    group, _, each = grad_forecast.shape
    two = 2 * each
    inner_parts = [
        jnp.dot(top, head_whole[part][:, :two], preferred_element_type=jnp.float32)
        for part in range(group)
    ]
    head_pre = jnp.concatenate(
        [inner_parts[part][:, :each] + latent_offsets[part] for part in range(group)], axis=1
    )
    hidden, slope = silu_parts(head_pre)
    hidden = hidden.astype(jnp.bfloat16)
    forecast = jnp.stack(
        [
            (
                jnp.dot(hidden, head_whole[part][:, two:], preferred_element_type=jnp.float32)
                + emit_offsets[part]
                + inner_parts[part][:, each:]
            )
            * keep
            for part in range(group)
        ]
    ).astype(jnp.bfloat16)
    grad_hidden = sum(
        reverse_matmul_answer(grad_forecast[part], head_whole[part][:, two:])
        for part in range(group)
    )
    pre_low = (grad_hidden * slope).astype(jnp.bfloat16)
    grad_top = sum(
        reverse_matmul_answer(
            jnp.concatenate(
                [pre_low[:, part * each : (part + 1) * each], grad_forecast[part]], axis=1
            ),
            head_whole[part][:, :two],
        )
        for part in range(group)
    )
    return hidden, forecast, pre_low, grad_top, jnp.sum(pre_low.astype(FULL), axis=0, keepdims=True)


def input_back_kernel(
    grad_ref, pre_ref, emit_ref, latent_ref, shortcut_ref, low_ref, pre_low_ref, sent_ref, bias_ref, wide
):
    low = grad_ref[...].astype(jnp.bfloat16)
    low_ref[...] = low
    rows_times_turned(low, emit_ref, 0, emit_ref.shape[1], wide, 256)
    pre = pre_ref[...]
    gate = 1.0 / (1.0 + jnp.exp(-pre))
    pre_low = (wide[...] * (gate * (1.0 + pre * (1.0 - gate)))).astype(jnp.bfloat16)
    pre_low_ref[...] = pre_low
    sent_ref[...] = reverse_matmul_answer(pre_low, latent_ref[...]) + reverse_matmul_answer(
        low, shortcut_ref[...]
    )
    bias_ref[0:1] = jnp.sum(pre_low.astype(jnp.float32), axis=0, keepdims=True)
    bias_ref[1:2] = jnp.sum(low.astype(jnp.float32), axis=0, keepdims=True)


def input_products_kernel(group, me_ref, *refs):
    hidden, met_hidden, low, met_low, pre_low, met_pre_low, features, met_features = refs[:8]
    vectors, met_vectors, to_x, to_y, later, own = refs[8:14]
    turned, low_pair, extras, block = refs[14:]
    tokens = hidden.shape[0]
    columns = low.shape[1]
    half = columns // 2
    core, chip = me_ref[0] & 1, me_ref[0] >> 1
    turned[:, :tokens] = hidden[...].astype(jnp.float32).T.astype(jnp.bfloat16)
    turned[:, tokens:] = met_hidden[...].astype(jnp.float32).T.astype(jnp.bfloat16)
    low_pair[:tokens] = low[...]
    low_pair[tokens:] = met_low[...]
    wide = features.shape[1]
    extras[...] = jnp.zeros_like(extras)
    extras[:wide] = dyadic_accumulation(features[...], pre_low[...]) + dyadic_accumulation(
        met_features[...], met_pre_low[...]
    )
    extras[wide : 2 * wide] = dyadic_accumulation(features[...], low[...]) + dyadic_accumulation(
        met_features[...], met_low[...]
    )
    extras[2 * wide : 2 * wide + vectors.shape[0]] = vectors[...] + met_vectors[...]
    rows = hidden.shape[1] // 8
    each = rows // group
    span = each + EXTRA_ROWS

    def store(rel, total):
        if rel == 0:
            own[0] = total
        elif rel == 1:
            to_x[1, 0] = total[:, :half]
            later[1, 0] = total[:, half:]
        elif rel == 2:
            later[0, 0] = total[:, :half]
            to_y[1, 0] = total[:, half:]
        else:
            to_x[0, 0] = total[:, :half]
            to_y[0, 0] = total[:, half:]

    for place in range(4):
        number = 2 * place + core
        first = pl.multiple_of(number * rows, rows)
        outer = jnp.dot(
            turned[pl.ds(first, rows), :], low_pair[...], preferred_element_type=jnp.float32
        )
        first = pl.multiple_of(number * group * EXTRA_ROWS, group * EXTRA_ROWS)
        extra = extras[pl.ds(first, group * EXTRA_ROWS), :]
        for member in range(group):
            block[member * span : member * span + each] = outer[member * each : (member + 1) * each]
            block[member * span + each : (member + 1) * span] = extra[
                member * EXTRA_ROWS : (member + 1) * EXTRA_ROWS
            ]
        total = block[...].astype(own.dtype)
        for rel in range(4):
            pl.when(chip ^ place == rel)(partial(store, rel, total))


def input_back(grad, pre, emit, latent, shortcut):
    rows, columns = grad.shape
    vmem = pl.BlockSpec(memory_space=pltpu.VMEM)
    return pl.pallas_call(
        input_back_kernel,
        out_shape=[
            jax.ShapeDtypeStruct((rows, columns), LOW),
            jax.ShapeDtypeStruct((rows, columns), LOW),
            jax.ShapeDtypeStruct((rows, latent.shape[0]), FULL),
            jax.ShapeDtypeStruct((2, columns), FULL),
        ],
        in_specs=[vmem] * 5,
        out_specs=[vmem] * 4,
        scratch_shapes=[pltpu.VMEM((rows, columns), FULL)],
        compiler_params=pltpu.CompilerParams(vmem_limit_bytes=32 << 20),
        cost_estimate=SMALL_COST,
    )(grad, pre, emit, latent, shortcut)


def input_products(me, operands):
    group = lax.axis_size("head")
    tokens, columns = operands[2].shape
    width = operands[0].shape[1]
    block = width // 8 + group * EXTRA_ROWS
    pair = jax.ShapeDtypeStruct((2, 1, block, columns // 2), LOW)
    return RowSums(
        *pl.pallas_call(
            partial(input_products_kernel, group),
            out_shape=[pair, pair, pair, jax.ShapeDtypeStruct((1, block, columns), LOW)],
            in_specs=[pl.BlockSpec(memory_space=pltpu.SMEM)]
            + [pl.BlockSpec(memory_space=pltpu.VMEM)] * len(operands),
            out_specs=[pl.BlockSpec(memory_space=pltpu.VMEM)] * 4,
            scratch_shapes=[
                pltpu.VMEM((width, 2 * tokens), LOW),
                pltpu.VMEM((2 * tokens, columns), LOW),
                pltpu.VMEM((8 * group * EXTRA_ROWS, columns), FULL),
                pltpu.VMEM((block, columns), FULL),
            ],
            compiler_params=pltpu.CompilerParams(vmem_limit_bytes=32 << 20),
            cost_estimate=SMALL_COST,
        )((me & 7).reshape(1), *operands)
    )


def entry_kernel(plan, own, me_ref, *refs):
    pieces = refs[: len(plan)]
    main_ref, extra_ref, held, sems = refs[len(plan) :]
    copies = []
    for n, (rel, row, rows) in enumerate(plan):
        spot = held.at[me_ref[0] ^ rel, pl.ds(row, rows)]
        copies.append(pltpu.make_async_copy(pieces[n].at[0], spot, sems.at[n]))
    for copy in copies:
        copy.start()
    for copy in copies:
        copy.wait()
    span = own + EXTRA_ROWS
    group = held.shape[1] // span
    for block in range(8):
        rows = held[block].astype(jnp.float32)
        for member in range(group):
            main_ref[block * group + member] = rows[member * span : member * span + own]
            extra_ref[block * group + member] = rows[member * span + own : (member + 1) * span]


def entry_sums_of_group(total):
    total = total.reshape(-1, total.shape[-1])
    return sum_group_at_once(total).astype(total.dtype)


def entry_everywhere(me, summed, own, count):
    columns = summed.shape[-1]
    group = lax.axis_size("head")
    if lax.axis_size("dp") > 8:
        held = gather_head(summed)
    else:
        every = jnp.broadcast_to(summed[None], (group, *summed.shape))
        held = lax.all_to_all(every, "head", split_axis=0, concat_axis=0, tiled=True)
        held = held.reshape(1, -1, columns)
    pieces = spread_rows(held)
    places = (me & 7).reshape(1)
    span = own + EXTRA_ROWS
    if held.shape[0] > 1 or own % 8 or not in_kernel(pieces):
        (whole,) = place(places, pieces, [columns])
        whole = whole.reshape(-1, span, columns).astype(jnp.float32)
        return whole[:, :own].reshape(-1, columns), whole[:, own:].reshape(-1, columns)[:count], held
    rows = held.shape[1]
    blocks = 8 * rows // span
    plan = [(rel, row, array.shape[1]) for rel, row, array in pieces]
    vmem = pl.BlockSpec(memory_space=pltpu.VMEM)
    main, extra = pl.pallas_call(
        partial(entry_kernel, plan, own),
        out_shape=[
            jax.ShapeDtypeStruct((blocks, own, columns), jnp.float32),
            jax.ShapeDtypeStruct((blocks, EXTRA_ROWS, columns), jnp.float32),
        ],
        in_specs=[pl.BlockSpec(memory_space=pltpu.SMEM)]
        + [pl.BlockSpec(memory_space=pl.ANY)] * len(pieces),
        out_specs=[vmem, vmem],
        scratch_shapes=[
            pltpu.VMEM((8, rows, columns), held.dtype),
            pltpu.SemaphoreType.DMA((len(pieces),)),
        ],
        compiler_params=pltpu.CompilerParams(vmem_limit_bytes=44 << 20),
        cost_estimate=SMALL_COST,
    )(places, *[array for _, _, array in pieces])
    return main.reshape(-1, columns), extra.reshape(-1, columns)[:count], held


def fetch(plan, me, pieces, whole, sems):
    groups = []
    for group in range(whole.shape[1] // MODEL_WIDTH):
        columns = pl.ds(group * MODEL_WIDTH, MODEL_WIDTH)
        copies = []
        for n, (rel, row, rows) in enumerate(plan):
            first = pl.multiple_of((me ^ rel) * (whole.shape[0] // 8) + row, 16)
            copies.append(
                pltpu.make_async_copy(
                    pieces[n].at[0, :, columns],
                    whole.at[pl.ds(first, rows), columns],
                    sems.at[group * len(plan) + n],
                )
            )
        for copy in copies:
            copy.start()
        groups.append(copies)
    return groups


def arrive(copies):
    for copy in copies:
        copy.wait()


def rows_times(left, whole, first, out, tile):
    def step(n, _):
        at = pl.multiple_of(n * tile, 128)
        out[:, pl.ds(at, tile)] = jnp.dot(
            left, whole[:, pl.ds(first + at, tile)], preferred_element_type=jnp.float32
        )
        return 0

    lax.fori_loop(0, out.shape[1] // tile, step, 0)


def rows_times_turned(left, whole, first, width, out, tile):
    def step(n, _):
        at = pl.multiple_of(n * tile, 128)
        part = reverse_matmul_answer(whole[pl.ds(at, tile), pl.ds(first, width)], left)
        out[:, pl.ds(at, tile)] = part.T
        return 0

    lax.fori_loop(0, out.shape[1] // tile, step, 0)


def inverse_norm(rows):
    return lax.rsqrt(jnp.mean(rows * rows, axis=-1, keepdims=True) + EPS)


def other_half(rows):
    half = HEAD_DIM // 2
    lane = lax.broadcasted_iota(jnp.int32, rows.shape, 1) % HEAD_DIM
    ahead = pltpu.roll(rows, rows.shape[1] - half, 1)
    behind = pltpu.roll(rows, half, 1)
    return jnp.where(lane < half, ahead, behind)


def head_window(head, width):
    first = head * HEAD_DIM // 128 * 128
    last = min(-(-(head + 1) * HEAD_DIM // 128) * 128, width)
    start = head * HEAD_DIM - first
    lane = lax.broadcasted_iota(jnp.int32, (1, last - first), 1)
    return slice(first, last), jnp.logical_and(lane >= start, lane < start + HEAD_DIM)


def entry_forward_kernel(plan, me_ref, resid_ref, gain_ref, cosine_ref, sine_ref, allowed_ref, *refs):
    pieces = refs[: len(plan)]
    normed_ref, query_ref, key_ref, value_ref, total_ref, mixed_ref = refs[len(plan) : len(plan) + 6]
    whole, wide, sems = refs[len(plan) + 6 :]
    groups = fetch(plan, me_ref[0], pieces, whole, sems)
    resid = resid_ref[...]
    normed = (resid * inverse_norm(resid) * gain_ref[...]).astype(jnp.bfloat16)
    normed_ref[...] = normed
    for group, out in enumerate((query_ref, key_ref, value_ref)):
        arrive(groups[group])
        rows_times(normed, whole, group * MODEL_WIDTH, wide, 256)
        rows = wide[...]
        if group < 2:
            rows = rows * cosine_ref[...] + other_half(rows) * sine_ref[...]
        out[...] = rows.astype(jnp.bfloat16)
    scale = 1.0 / math.sqrt(HEAD_DIM)
    allowed = allowed_ref[...] > 0.0
    wide[...] = jnp.zeros_like(wide)
    totals = jnp.zeros(total_ref.shape, jnp.float32)
    head_lane = lax.broadcasted_iota(jnp.int32, total_ref.shape, 1)
    for head in range(HEADS):
        window, inside = head_window(head, MODEL_WIDTH)
        query = jnp.where(inside, query_ref[:, window], 0)
        scores = reverse_matmul_answer(query, key_ref[:, window]) * scale
        scores = jnp.where(allowed, scores, -1e30)
        peak = jnp.max(scores, axis=-1, keepdims=True)
        weights = jnp.exp(scores - peak)
        total = jnp.sum(weights, axis=-1, keepdims=True)
        probs = (weights / total).astype(jnp.bfloat16)
        mixed = jnp.dot(probs, value_ref[:, window], preferred_element_type=jnp.float32)
        wide[:, window] += jnp.where(inside, mixed, 0.0)
        totals = jnp.where(head_lane == head, peak + jnp.log(total), totals)
    total_ref[...] = totals
    mixed_ref[...] = wide[...].astype(jnp.bfloat16)


def gelu_parts(x):
    root = math.sqrt(2.0 / math.pi)
    bend = jnp.tanh(root * (x + 0.044715 * (x * x * x)))
    slope = 0.5 * (1.0 + bend) + 0.5 * x * (1.0 - bend * bend) * root * (
        1.0 + 3.0 * 0.044715 * (x * x)
    )
    return 0.5 * x * (1.0 + bend), slope


def rest_forward_kernel(plan, me_ref, resid_ref, mixed_ref, gain_ref, *refs):
    pieces = refs[: len(plan)]
    result_ref, middle_ref, normed_ref, pre_ref = refs[len(plan) : len(plan) + 4]
    whole, sems = refs[len(plan) + 4 :]
    groups = fetch(plan, me_ref[0], pieces, whole, sems)
    arrive(groups[0])
    rows_times(mixed_ref[...], whole, 0, middle_ref, 256)
    middle = resid_ref[...] + middle_ref[...]
    middle_ref[...] = middle
    normed = (middle * inverse_norm(middle) * gain_ref[...]).astype(jnp.bfloat16)
    normed_ref[...] = normed
    arrive(groups[1])
    rows_times(normed, whole, MODEL_WIDTH, pre_ref, 256)
    act = gelu_parts(pre_ref[...])[0].astype(jnp.bfloat16)
    arrive(groups[2])
    rows_times(act, whole, 2 * MODEL_WIDTH, result_ref, 256)
    result_ref[...] += middle_ref[...]


def norm_back(rows, gain, grad):
    inverse = inverse_norm(rows)
    scaled = grad * gain
    mean = jnp.mean(rows * scaled, axis=-1, keepdims=True)
    sent = inverse * scaled - rows * (inverse * inverse * inverse * mean)
    return sent, jnp.sum(grad * rows * inverse, axis=0, keepdims=True)


def rest_backward_kernel(plan, me_ref, grad_ref, middle_ref, pre_ref, gain_ref, *refs):
    pieces = refs[: len(plan)]
    outs = refs[len(plan) : len(plan) + 7]
    grad_middle_ref, mixed_ref, attn_ref, grad_pre_ref, branch_ref, act_ref, gain_grad_ref = outs
    whole, wide, sems = refs[len(plan) + 7 :]
    groups = fetch(plan, me_ref[0], pieces, whole, sems)
    grad = grad_ref[...]
    branch = grad.astype(jnp.bfloat16)
    branch_ref[...] = branch
    arrive(groups[2])
    rows_times_turned(branch, whole, 2 * MODEL_WIDTH, MODEL_WIDTH, wide, 256)
    act, slope = gelu_parts(pre_ref[...])
    act_ref[...] = act.astype(jnp.bfloat16)
    grad_pre = (wide[...] * slope).astype(jnp.bfloat16)
    grad_pre_ref[...] = grad_pre
    arrive(groups[1])
    rows_times_turned(grad_pre, whole, MODEL_WIDTH, MODEL_WIDTH, wide, 256)
    sent, gain_grad_ref[...] = norm_back(middle_ref[...], gain_ref[...], wide[...])
    grad_middle = grad + sent
    grad_middle_ref[...] = grad_middle
    attn = grad_middle.astype(jnp.bfloat16)
    attn_ref[...] = attn
    arrive(groups[0])
    rows_times_turned(attn, whole, 0, MODEL_WIDTH, wide, 256)
    mixed_ref[...] = wide[...].astype(jnp.bfloat16)


def entry_backward_kernel(
    plan,
    me_ref,
    grad_middle_ref,
    grad_mixed_ref,
    resid_ref,
    query_ref,
    key_ref,
    value_ref,
    total_ref,
    gain_ref,
    cosine_ref,
    sine_ref,
    allowed_ref,
    *refs,
):
    pieces = refs[: len(plan)]
    grad_resid_ref, projected_ref, gain_grad_ref = refs[len(plan) : len(plan) + 3]
    whole, grad_query, grad_key, grad_value, sems = refs[len(plan) + 3 :]
    groups = fetch(plan, me_ref[0], pieces, whole, sems)
    scale = 1.0 / math.sqrt(HEAD_DIM)
    allowed = allowed_ref[...] > 0.0
    totals = total_ref[...]
    grad_query[...] = jnp.zeros_like(grad_query)
    grad_key[...] = jnp.zeros_like(grad_key)
    grad_value[...] = jnp.zeros_like(grad_value)
    for head in range(HEADS):
        window, inside = head_window(head, MODEL_WIDTH)
        query = jnp.where(inside, query_ref[:, window], 0)
        keys = key_ref[:, window]
        grad_mixed = jnp.where(inside, grad_mixed_ref[:, window], 0)
        scores = reverse_matmul_answer(query, keys) * scale
        probs = jnp.where(allowed, jnp.exp(scores - totals[:, head : head + 1]), 0.0)
        grad_probs = reverse_matmul_answer(grad_mixed, value_ref[:, window])
        grad_value[:, window] += dyadic_accumulation(probs.astype(jnp.bfloat16), grad_mixed)
        center = jnp.sum(grad_probs * probs, axis=-1, keepdims=True)
        grad_scores = (probs * (grad_probs - center)).astype(jnp.bfloat16)
        along = jnp.dot(grad_scores, keys, preferred_element_type=jnp.float32)
        grad_query[:, window] += jnp.where(inside, along * scale, 0.0)
        grad_key[:, window] += dyadic_accumulation(grad_scores, query) * scale
    for group, part in enumerate((grad_query, grad_key, grad_value)):
        rows = part[...]
        if group < 2:
            rows = rows * cosine_ref[...] - other_half(rows) * sine_ref[...]
        projected_ref[:, group * MODEL_WIDTH : (group + 1) * MODEL_WIDTH] = rows.astype(jnp.bfloat16)
    for copies in groups:
        arrive(copies)
    rows_times_turned(projected_ref[...], whole, 0, 3 * MODEL_WIDTH, grad_query, 256)
    sent, gain_grad_ref[...] = norm_back(resid_ref[...], gain_ref[...], grad_query[...])
    grad_resid_ref[...] = grad_middle_ref[...] + sent


def whole_call(kernel, me, pieces, inputs, outs, wides):
    rows = inputs[0].shape[0]
    plan = [(rel, row, array.shape[1]) for rel, row, array in pieces]
    blocks = 8 * pieces[0][2].shape[1]
    columns = 3 * MODEL_WIDTH
    vmem = pl.BlockSpec(memory_space=pltpu.VMEM)
    return pl.pallas_call(
        partial(kernel, plan),
        out_shape=[jax.ShapeDtypeStruct(shape, kind) for shape, kind in outs],
        in_specs=[pl.BlockSpec(memory_space=pltpu.SMEM)]
        + [vmem] * len(inputs)
        + [pl.BlockSpec(memory_space=pl.ANY)] * len(pieces),
        out_specs=[vmem] * len(outs),
        scratch_shapes=[pltpu.VMEM((blocks, columns), jnp.bfloat16)]
        + [pltpu.VMEM((rows, MODEL_WIDTH), jnp.float32)] * wides
        + [pltpu.SemaphoreType.DMA((3 * len(pieces),))],
        compiler_params=pltpu.CompilerParams(vmem_limit_bytes=44 << 20),
        cost_estimate=SMALL_COST,
    )(me, *inputs, *[array for _, _, array in pieces])


def in_kernel(pieces):
    lead, rows, _ = pieces[0][2].shape
    return lead == 1 and rows % 32 == 0


LOW, FULL = jnp.bfloat16, jnp.float32


class Layer:
    def __init__(self, places, entry_pieces, gains, tables, allowed):
        self.places, self.entry_pieces, self.gains = places, entry_pieces, gains
        self.tables, self.allowed = tables, allowed
        self.fetched = in_kernel(entry_pieces)
        if not self.fetched:
            self.entry_whole = place(places, entry_pieces, [3 * MODEL_WIDTH])[0][0]

    def add_rest(self, rest_pieces):
        self.rest_pieces = rest_pieces
        if not self.fetched:
            self.rest_whole = [part[0] for part in place(self.places, rest_pieces, [MODEL_WIDTH] * 3)]

    def shapes(self, *kinds):
        rows = self.allowed.shape[0]
        return [((rows, width), kind) for width, kind in kinds]

    def entry_forward(self, resid):
        if not self.fetched:
            self.saved = entry_forward(
                resid, self.entry_whole, self.gains, *self.tables[:2], self.allowed
            )
            return self.saved[6]
        wide = (MODEL_WIDTH, LOW)
        self.resid = resid
        outs = whole_call(
            entry_forward_kernel,
            self.places,
            self.entry_pieces,
            (resid, self.gains[:1].astype(FULL), *self.tables[2:], self.allowed.astype(FULL)),
            self.shapes(wide, wide, wide, wide, (128, FULL), wide),
            1,
        )
        self.normed_first, self.heads = outs[0], outs[1:5]
        return outs[5]

    def rest_forward(self, mixed):
        if not self.fetched:
            result, self.saved = rest_forward(
                (*self.saved[:6], mixed), *self.rest_whole, self.gains
            )
            return result
        self.mixed = mixed
        result, self.middle, self.normed_second, self.hidden_pre = whole_call(
            rest_forward_kernel,
            self.places,
            self.rest_pieces,
            (self.resid, mixed, self.gains[1:].astype(FULL)),
            self.shapes(
                (MODEL_WIDTH, FULL), (MODEL_WIDTH, FULL), (MODEL_WIDTH, LOW), (MODEL_WIDTH, FULL)
            ),
            0,
        )
        return result

    def rest_backward(self, grad):
        if not self.fetched:
            weights = (self.entry_whole, *self.rest_whole, self.gains)
            return rest_backward(self.saved, weights, grad)
        wide = (MODEL_WIDTH, LOW)
        grad_middle, grad_mixed, grad_attn, grad_pre, branch, act, gain_grad = whole_call(
            rest_backward_kernel,
            self.places,
            self.rest_pieces,
            (grad, self.middle, self.hidden_pre, self.gains[1:].astype(FULL)),
            self.shapes((MODEL_WIDTH, FULL), wide, wide, wide, wide, wide)
            + [((1, MODEL_WIDTH), FULL)],
            1,
        )
        lefts = (self.mixed, self.normed_second, act)
        return grad_middle, grad_mixed, lefts, (grad_attn, grad_pre, branch), gain_grad[0]

    def entry_backward(self, grad_middle, grad_mixed):
        if not self.fetched:
            weights = (self.entry_whole, *self.rest_whole, self.gains)
            return entry_backward(
                self.saved, weights, *self.tables[:2], self.allowed, grad_middle, grad_mixed
            )
        grad_resid, projected, gain_grad = whole_call(
            entry_backward_kernel,
            self.places,
            self.entry_pieces,
            (
                grad_middle,
                grad_mixed,
                self.resid,
                *self.heads,
                self.gains[:1].astype(FULL),
                *self.tables[2:],
                self.allowed.astype(FULL),
            ),
            self.shapes((MODEL_WIDTH, FULL), (3 * MODEL_WIDTH, LOW)) + [((1, MODEL_WIDTH), FULL)],
            3,
        )
        return grad_resid, self.normed_first, projected, gain_grad[0]


def entry_forward(resid, qkv_full, gain_pair, cosine, sine, allowed):
    gains = gain_pair.astype(jnp.float32)
    rows = resid.shape[0]
    normed_first = norm_apply(resid, gains[0]).astype(jnp.bfloat16)
    projected = jnp.dot(normed_first, qkv_full, preferred_element_type=jnp.float32)
    query_rows = rotate(
        projected[:, :MODEL_WIDTH].reshape(rows, HEADS, HEAD_DIM), cosine, sine
    ).astype(jnp.bfloat16)
    key_rows = rotate(
        projected[:, MODEL_WIDTH : 2 * MODEL_WIDTH].reshape(rows, HEADS, HEAD_DIM), cosine, sine
    ).astype(jnp.bfloat16)
    value_rows = projected[:, 2 * MODEL_WIDTH :].reshape(rows, HEADS, HEAD_DIM).astype(jnp.bfloat16)

    mixed, log_total = attend_forward(query_rows, key_rows, value_rows, allowed)
    mixed_low = mixed.reshape(rows, MODEL_WIDTH).astype(jnp.bfloat16)
    return (resid, normed_first, query_rows, key_rows, value_rows, log_total, mixed_low)


def rest_forward(saved, out_full, up_full, down_full, gain_pair):
    gains = gain_pair.astype(jnp.float32)
    resid, mixed_low = saved[0], saved[6]
    middle = resid + jnp.dot(mixed_low, out_full, preferred_element_type=jnp.float32)
    normed_second = norm_apply(middle, gains[1]).astype(jnp.bfloat16)
    hidden_pre = jnp.dot(normed_second, up_full, preferred_element_type=jnp.float32)
    hidden_act = jax.nn.gelu(hidden_pre, approximate=True).astype(jnp.bfloat16)
    result = middle + jnp.dot(hidden_act, down_full, preferred_element_type=jnp.float32)
    return (result, (*saved, middle, normed_second, hidden_pre))


def rest_backward(saved, weights, grad_result):
    mixed_low, middle, normed_second, hidden_pre = saved[6:]
    _, out_full, up_full, down_full, gain_pair = weights
    gains = gain_pair.astype(jnp.float32)
    grad_branch = grad_result.astype(jnp.bfloat16)
    hidden_act, gelu_pull = jax.vjp(partial(jax.nn.gelu, approximate=True), hidden_pre)
    hidden_low = hidden_act.astype(jnp.bfloat16)
    grad_act = reverse_matmul_answer(grad_branch, down_full)
    grad_pre = gelu_pull(grad_act)[0].astype(jnp.bfloat16)
    grad_normed_second = reverse_matmul_answer(grad_pre, up_full)
    unused_second, second_pull = jax.vjp(norm_apply, middle, gains[1])
    grad_middle_norm, grad_gain_second = second_pull(grad_normed_second)
    grad_middle = grad_result + grad_middle_norm
    grad_attn = grad_middle.astype(jnp.bfloat16)
    grad_mixed = reverse_matmul_answer(grad_attn, out_full).astype(jnp.bfloat16)
    left_rows = (mixed_low, normed_second, hidden_low)
    right_rows = (grad_attn, grad_pre, grad_branch)
    return (grad_middle, grad_mixed, left_rows, right_rows, grad_gain_second)


def entry_backward(saved, weights, cosine, sine, allowed, grad_middle, grad_mixed):
    resid, normed_first, query_rows, key_rows, value_rows, log_total = saved[:6]
    qkv_full = weights[0]
    gains = weights[4].astype(jnp.float32)
    rows = resid.shape[0]
    grad_query, grad_keys, grad_values = attend_backward(
        query_rows,
        key_rows,
        value_rows,
        allowed,
        log_total,
        grad_mixed.reshape(rows, HEADS, HEAD_DIM),
    )
    grad_query = unrotate(grad_query, cosine, sine).reshape(rows, MODEL_WIDTH)
    grad_keys = unrotate(grad_keys, cosine, sine).reshape(rows, MODEL_WIDTH)
    grad_values = grad_values.reshape(rows, MODEL_WIDTH)
    grad_projected = jnp.concatenate([grad_query, grad_keys, grad_values], axis=1).astype(
        jnp.bfloat16
    )
    grad_normed_first = reverse_matmul_answer(grad_projected, qkv_full)
    unused_first, first_pull = jax.vjp(norm_apply, resid, gains[0])
    grad_resid_norm, grad_gain_first = first_pull(grad_normed_first)
    return (grad_middle + grad_resid_norm, normed_first, grad_projected, grad_gain_first)


def body(
    patch_observations,
    sequence_labels,
    leading_filler_count,
    intake_latent_matrix,
    intake_latent_offset,
    intake_emit_matrix,
    intake_emit_offset,
    intake_shortcut_matrix,
    attention_entry_matrices,
    attention_merge_matrix,
    feedforward_widen_matrix,
    feedforward_shrink_matrix,
    layer_scale_factors,
    readout_latent_matrix,
    readout_latent_offset,
    readout_emit_matrix,
    readout_emit_offset,
    readout_shortcut_matrix,
    loss_sensitivity,
):
    patch_len = patch_observations.shape[1]
    position, pad_count, allowed, keep_rows = layout_rows(
        sequence_labels[0], leading_filler_count[0], patch_len
    )
    cosine, sine = rotary_tables(position, HEAD_DIM)
    columns = jnp.arange(patch_len, dtype=jnp.int32)
    pad_mask = columns[None, :] < pad_count[:, None]
    features = jnp.concatenate(
        [
            jnp.where(pad_mask, jnp.zeros_like(patch_observations), patch_observations),
            pad_mask.astype(jnp.bfloat16),
        ],
        axis=1,
    )
    entry_pre = (
        jnp.dot(features, intake_latent_matrix, preferred_element_type=jnp.float32)
        + intake_latent_offset
    )
    entry_hidden = jax.nn.silu(entry_pre).astype(jnp.bfloat16)
    resid = (
        jnp.dot(entry_hidden, intake_emit_matrix, preferred_element_type=jnp.float32)
        + intake_emit_offset
        + jnp.dot(features, intake_shortcut_matrix, preferred_element_type=jnp.float32)
    )
    layer_count = attention_entry_matrices.shape[0]
    group = lax.axis_size("head")
    group_place = lax.axis_index("head")
    outer = lax.axis_size("dp") // 8
    me = lax.axis_index("dp").astype(jnp.int32)
    places = (me & 7).reshape(1)
    own_count = layer_scale_factors.shape[2]
    rows = patch_observations.shape[0]

    group_width = readout_latent_offset.shape[0]
    offsets = jnp.stack([readout_latent_offset, readout_emit_offset])
    coarse = lax.reduce_precision(offsets, 8, 7)
    offset_rows = jnp.concatenate([coarse, offsets - coarse], axis=0).astype(jnp.bfloat16)
    offset_rows = jnp.pad(offset_rows, ((0, 12), (0, 0)))
    sent = jnp.concatenate(
        [
            loss_sensitivity.reshape(group, rows, group_width),
            jnp.broadcast_to(offset_rows[None], (group, 16, group_width)),
        ],
        axis=1,
    )
    gain_columns = layer_scale_factors.reshape(2 * layer_count, own_count).T
    gain_columns = jnp.pad(gain_columns, ((0, 0), (0, 128 - 2 * layer_count)))
    chunks = []
    for layer_index in range(layer_count):
        entry_own = attention_entry_matrices[layer_index]
        if layer_index == 0:
            entry_own = jnp.concatenate([entry_own, gain_columns], axis=1)
        chunks.append(entry_own)
        rest_own = jnp.concatenate(
            [
                attention_merge_matrix[layer_index],
                feedforward_widen_matrix[layer_index],
                feedforward_shrink_matrix[layer_index],
            ],
            axis=1,
        )
        chunks.append(rest_own)
    head_own = jnp.concatenate(
        [
            lax.dynamic_index_in_dim(
                matrix.reshape(outer, 8, -1, group_width), me % 8, 1, keepdims=False
            )
            for matrix in (readout_latent_matrix, readout_shortcut_matrix, readout_emit_matrix)
        ],
        axis=2,
    )
    chunks.append(head_own)
    count = len(chunks)

    def gather_chunk(number, own):
        if number < count - 1:
            return gather_head(own)
        return lax.all_gather(own, "head", axis=0, tiled=True)

    held = gather_chunk(0, chunks[0])
    cosine_wide = jnp.tile(jnp.concatenate([cosine[:, 0], cosine[:, 0]], axis=1), (1, HEADS))
    sine_wide = jnp.tile(jnp.concatenate([-sine[:, 0], sine[:, 0]], axis=1), (1, HEADS))
    tables = (cosine, sine, cosine_wide, sine_wide)
    nears, fars, near_mets = [], [], []
    layers = []
    onward = None
    for number in range(count + 1):
        step = {}
        if number < count:
            step["x"], step["y"] = swap(held, 1), swap(held, 2)
        if number + 1 < count:
            step["next"] = gather_chunk(number + 1, chunks[number + 1])
        if number == count - 1:
            step["met"] = lax.all_to_all(
                after(sent, held), "head", split_axis=0, concat_axis=0, tiled=True
            )
        if number == 0:
            step["resid"] = resid
        else:
            step["far"] = (swap(onward[0], 1), swap(onward[1], 2))
            near_mets.append([swap(part, 0) for part in after(nears[number - 1], onward)])
        if number > 1:
            chunk = number - 2
            far_met = [swap(part, 0) for part in after(fars[chunk], onward)]
            pieces = all_pieces(nears[chunk], fars[chunk], near_mets[chunk], far_met)
            if chunk == 0:
                gain_rows = place(places, pieces, [128], 3 * MODEL_WIDTH)[0][0]
                gain_rows = gain_rows[:, : 2 * layer_count].T.reshape(layer_count, 2, -1)
            if chunk % 2 == 0:
                layers.append(Layer(places, pieces, gain_rows[chunk // 2], tables, allowed))
                step["mixed"] = layers[-1].entry_forward(resid)
            else:
                layers[-1].add_rest(pieces)
                step["resid"] = layers[-1].rest_forward(mixed)
        step["own"] = chunks[number + 2 :]
        step = lax.optimization_barrier(step)
        chunks[number + 2 :] = step["own"]
        if number < count:
            nears.append((held, step["x"], step["y"]))
            onward = second_step(*nears[-1])
        held = step.get("next")
        if number > 0:
            fars.append(step["far"])
        resid = step.get("resid", resid)
        mixed = step.get("mixed")
        if "met" in step:
            met = step["met"]
    head_far_met = [swap(part, 0) for part in fars[-1]]
    head_pieces = all_pieces(nears[-1], fars[-1], near_mets[-1], head_far_met)
    sensitivity = met[:, :rows]
    head_offsets = met[:, rows : rows + 4].astype(jnp.float32)
    latent_offsets = head_offsets[:, 0] + head_offsets[:, 2]
    emit_offsets = head_offsets[:, 1] + head_offsets[:, 3]

    top = resid.astype(jnp.bfloat16)
    keep_column = keep_rows[:, None]
    grad_forecast = (sensitivity.astype(jnp.float32) * keep_column).astype(jnp.bfloat16)
    grad_forecast_rows = jnp.concatenate([grad_forecast[part] for part in range(group)], axis=1)
    head_inputs = (top, keep_column, latent_offsets, emit_offsets, grad_forecast)
    if layers[0].fetched:
        outs = output_block(places, head_pieces, *head_inputs)
    else:
        head_whole = place(places, head_pieces, [3 * group_width])[0]
        outs = output_plain(head_whole, *head_inputs)
    head_hidden, forecast, grad_head_pre, grad_resid, pre_sums = outs
    token_predictions = lax.all_to_all(
        forecast, "head", split_axis=0, concat_axis=0, tiled=True
    ).reshape(group * rows, group_width)
    head_bias_rows = (pre_sums[0], jnp.sum(grad_forecast_rows.astype(jnp.float32), axis=0))
    head_both = exchange(
        [
            (top, grad_head_pre),
            (top, grad_forecast_rows),
            (head_hidden, grad_forecast_rows),
        ]
    )
    gain_sums = [[None, None] for _ in range(layer_count)]

    def rest_stage(layer_index, carry):
        outs = layers[layer_index].rest_backward(carry["grad"])
        gain_sums[layer_index][1] = outs[4]
        both = exchange(list(zip(outs[2], outs[3], strict=True)))
        return {"middle": outs[0], "mixed": outs[1]}, both

    def entry_stage(layer_index, carry):
        outs = layers[layer_index].entry_backward(carry["middle"], carry["mixed"])
        gain_sums[layer_index][0] = outs[3]
        return {"grad": outs[0]}, exchange([(outs[1], outs[2])])

    def input_stage(carry):
        head_rows = [row[None] for row in head_bias_rows]
        gain_rows = [row[None] for pair in gain_sums for row in pair]
        if layers[0].fetched and 2 + len(head_rows) + len(gain_rows) == EXTRA_ROWS:
            low, pre_low, grad_features, bias_rows = input_back(
                carry["grad"],
                entry_pre,
                intake_emit_matrix,
                intake_latent_matrix,
                intake_shortcut_matrix,
            )
            values_grad = jnp.where(pad_mask, 0.0, grad_features[:, :patch_len])
            vectors = jnp.concatenate([bias_rows, *head_rows, *gain_rows], axis=0)
            operands = []
            for part in (entry_hidden, low, pre_low, features, vectors):
                operands += [part, swap(part, 0)]
            return values_grad, 4 * patch_len + EXTRA_ROWS, operands
        grad_entry = carry["grad"].astype(jnp.bfloat16)
        grad_entry_outer = dyadic_accumulation(entry_hidden, grad_entry)
        grad_entry_outer_bias = jnp.sum(grad_entry.astype(jnp.float32), axis=0)
        grad_entry_skip = dyadic_accumulation(features, grad_entry)
        unused_entry, entry_pull = jax.vjp(jax.nn.silu, entry_pre)
        grad_entry_pre = entry_pull(reverse_matmul_answer(grad_entry, intake_emit_matrix))[0].astype(
            jnp.bfloat16
        )
        grad_entry_inner = dyadic_accumulation(features, grad_entry_pre)
        grad_entry_inner_bias = jnp.sum(grad_entry_pre.astype(jnp.float32), axis=0)
        grad_features = reverse_matmul_answer(
            grad_entry_pre, intake_latent_matrix
        ) + reverse_matmul_answer(grad_entry, intake_shortcut_matrix)
        values_grad = jnp.where(pad_mask, 0.0, grad_features[:, :patch_len])
        extra_rows = jnp.concatenate(
            [
                grad_entry_inner,
                grad_entry_skip,
                grad_entry_inner_bias[None],
                grad_entry_outer_bias[None],
            ]
            + head_rows
            + [row[None] for pair in gain_sums for row in pair],
            axis=0,
        )
        plain = entry_products(me, grad_entry_outer, extra_rows)
        return values_grad, extra_rows.shape[0], (plain.sent, plain.later, plain.own)

    stages = []
    for layer_index in reversed(range(layer_count)):
        stages += [(rest_stage, layer_index), (entry_stage, layer_index)]
    stage_count = len(stages)
    carry = {"grad": grad_resid}
    boths = {0: head_both}
    sums = {0: RowSums(*pair_products(me, head_both))}
    totals, finished = {}, {}
    entry_chunk = None
    done = 0

    def close(**step):
        step["sent"] = {n: (sums[n].sent, sums[n].later, sums[n].own) for n in sums}
        step["boths"] = boths
        step["carry"] = carry
        step = lax.optimization_barrier(step)
        for n, parts in step.pop("sent").items():
            sums[n].sent, sums[n].later, sums[n].own = parts
        return step

    step = close()
    for number in range(stage_count + 1):
        carry, boths = step["carry"], step["boths"]
        parts = {"first": sums[number].first()}
        if number >= 1:
            totals[number - 1] = sums.pop(number - 1).total()
            if number == 1:
                finished[0] = sum_columns(totals[0])
            else:
                finished[number - 1] = sum_group(totals[number - 1])
        if number >= 2:
            parts["finished"] = finished[number - 2]
        until = number + 1 if number == 0 else number + 2
        while done < min(until, stage_count):
            stage, layer_index = stages[done]
            carry, boths[done + 1] = stage(layer_index, carry)
            done += 1
        if number == stage_count - 2:
            values_grad, extra_count, parts["entry"] = input_stage(carry)
        if number == stage_count - 1:
            entry_chunk.met = entry_chunk.first()
        if number == stage_count:
            entry_summed = entry_sums_of_group(entry_chunk.total())
        step = close(**parts)
        sums[number].met = step["first"]
        if number >= 2:
            finished[number - 2] = step["finished"]
        carry, boths = step["carry"], step["boths"]
        parts = {"last": sums[number].last()}
        if number == stage_count - 2:
            if layers[0].fetched:
                entry_chunk = input_products(me, step["entry"])
            else:
                (to_x, to_y), later, own = step["entry"]
                entry_chunk = RowSums(to_x, to_y, later, own)
            parts["entry"] = (entry_chunk.sent, entry_chunk.later, entry_chunk.own)
        if number == stage_count - 1:
            parts["entry"] = entry_chunk.last()
        if number < stage_count:
            sums[number + 1] = RowSums(*pair_products(me, boths.pop(number + 1)))
            step = close(**parts)
        else:
            step = parts
        sums[number].last_met = step["last"]
        if number == stage_count - 2:
            entry_chunk.sent, entry_chunk.later, entry_chunk.own = step["entry"]
        if number == stage_count - 1:
            entry_chunk.last_met = step["entry"]
    finished[stage_count] = sum_group_at_once(sums[stage_count].total())
    entry_main, entry_extra, entry_held = entry_everywhere(
        me, entry_summed, own_count, extra_count
    )
    head_rows = gather_blocks(me, finished[0])
    head_sums = [after(head_rows[n], entry_held).astype(jnp.float32) for n in range(3)]
    layer_sums = [None] * layer_count
    for member, layer_index in enumerate(reversed(range(layer_count))):
        rest = finished[1 + 2 * member].astype(jnp.float32)
        entry = finished[2 + 2 * member].astype(jnp.float32)
        layer_sums[layer_index] = (entry[0], rest[0], rest[1], rest[2])
    inner_rows = 2 * patch_len
    last = 2 * inner_rows
    entry_sums = (
        entry_extra[:inner_rows],
        entry_extra[last],
        entry_main,
        entry_extra[last + 1],
        entry_extra[inner_rows:last],
    )
    head_bias_sums = lax.dynamic_slice_in_dim(
        entry_extra[last + 2 : last + 4], group_place * group_width, group_width, 1
    )
    own_place = (me * group + group_place) * own_count
    gains_grad = lax.dynamic_slice_in_dim(
        entry_extra[last + 4 : last + 4 + 2 * layer_count], own_place, own_count, 1
    ).reshape(layer_count, 2, own_count)
    qkv_grad = jnp.stack([layer_sums[member][0] for member in range(layer_count)])
    out_grad = jnp.stack([layer_sums[member][1] for member in range(layer_count)])
    up_grad = jnp.stack([layer_sums[member][2] for member in range(layer_count)])
    down_grad = jnp.stack([layer_sums[member][3] for member in range(layer_count)])
    return (
        token_predictions,
        values_grad,
        entry_sums[0],
        entry_sums[1],
        entry_sums[2],
        entry_sums[3],
        entry_sums[4],
        qkv_grad,
        out_grad,
        up_grad,
        down_grad,
        gains_grad,
        head_sums[0],
        head_bias_sums[0],
        head_sums[2],
        head_bias_sums[1],
        head_sums[1],
    )


def solution(mesh):
    return jax.shard_map(
        body,
        mesh=mesh,
        in_specs=(
            P(("dp", "head"), None),
            P(("dp", "head"), None),
            P(("dp", "head"), None),
            P(),
            P(),
            P(),
            P(),
            P(),
            P(None, ("dp", "head"), None),
            P(None, ("dp", "head"), None),
            P(None, ("dp", "head"), None),
            P(None, ("dp", "head"), None),
            P(None, None, ("dp", "head")),
            P(None, "head"),
            P("head"),
            P(None, "head"),
            P("head"),
            P(None, "head"),
            P("dp", "head"),
        ),
        out_specs=(
            P("dp", "head"),
            P(("dp", "head"), None),
            P(),
            P(),
            P(),
            P(),
            P(),
            P(None, ("dp", "head"), None),
            P(None, ("dp", "head"), None),
            P(None, ("dp", "head"), None),
            P(None, ("dp", "head"), None),
            P(None, None, ("dp", "head")),
            P(None, "head"),
            P("head"),
            P(None, "head"),
            P("head"),
            P(None, "head"),
        ),
        check_vma=False,
    )
```

profile of v0, /device:TPU:0, one launch (start us, length us, event | category | flops | bytes accessed | tf_op | source)
XLA Modules:
  0.0 636.1 jit_solution(5900353750468289693)
XLA Ops:
  16.9 28.0 %all-gather.10.cloned.1.call-done = bf16[160,3968]{1,0:T(8,128)(2,1)} async-done(((bf16[40,3968]{1,0:T(8,128)(2,1)}), bf16[160,3968]{1,0:T(8,128)(2,1)}) %all-gather.10.cloned.1.call-update) | async-done | bytes 1269776 | tf_op jit(solution)/shard_map/all_gather | solution.py:214
  51.8 25.7 %all-gather.8.cloned.1.call-done = bf16[160,3840]{1,0:T(8,128)(2,1)} async-done(((bf16[40,3840]{1,0:T(8,128)(2,1)}), bf16[160,3840]{1,0:T(8,128)(2,1)}) %all-gather.8.cloned.1.call-update) | async-done | bytes 1228816 | tf_op jit(solution)/shard_map/all_gather | solution.py:214
  82.6 12.3 %collective-permute-done.2.refs_6_ = bf16[1,80,3968]{2,1,0:T(8,128)(2,1)S(1)} collective-permute-done((bf16[1,80,3968]{2,1,0:T(8,128)(2,1)S(1)}, bf16[1,80,3968]{2,1,0:T(8,128)(2,1)S(1)}, u32[]{:S(2)}, u32[]{:S(2)}) %collective-permute-start.2) | collective-permute-done | bytes 634912 | tf_op jit(solution)/shard_map/ppermute | solution.py:129
  96.5 23.0 %collective-permute-done.4.refs_2_ = bf16[1,160,3840]{2,1,0:T(8,128)(2,1)} collective-permute-done((bf16[1,160,3840]{2,1,0:T(8,128)(2,1)S(1)}, bf16[1,160,3840]{2,1,0:T(8,128)(2,1)}, u32[]{:S(2)}, u32[]{:S(2)}) %collective-permute-start.4) | collective-permute-done | bytes 1228832 | tf_op jit(solution)/shard_map/ppermute | solution.py:129
  129.4 10.5 %collective-permute-done.6.refs_6_ = bf16[1,80,3840]{2,1,0:T(8,128)(2,1)} collective-permute-done((bf16[1,80,3840]{2,1,0:T(8,128)(2,1)}, bf16[1,80,3840]{2,1,0:T(8,128)(2,1)}, u32[]{:S(2)}, u32[]{:S(2)}) %collective-permute-start.6) | collective-permute-done | bytes 614432 | tf_op jit(solution)/shard_map/ppermute | solution.py:129
  154.3 10.2 %shard_map.315 = (bf16[128,1280]{1,0:T(8,128)(2,1)S(1)}, bf16[128,1280]{1,0:T(8,128)(2,1)S(1)}, bf16[128,1280]{1,0:T(8,128)(2,1)S(1)}, bf16[128,1280]{1,0:T(8,12...) custom-call(s32[1]{0:T(128)} %bitcast.me_ref, f32[128,1280]{1,0:T(8,128)S(1)} %fusion.resid_ref, ...), custom_call_target="tpu_custom_call" | custom-call | flops 1 | bytes 1 | tf_op jit(solution)/shard_map/pallas_call | solution.py:983
  176.2 11.6 %collective-permute-done.15.refs_6_ = bf16[1,80,3840]{2,1,0:T(8,128)(2,1)} collective-permute-done((bf16[1,80,3840]{2,1,0:T(8,128)(2,1)}, bf16[1,80,3840]{2,1,0:T(8,128)(2,1)}, u32[]{:S(2)}, u32[]{:S(2)}) %collective-permute-start.15) | collective-permute-done | bytes 614432 | tf_op jit(solution)/shard_map/ppermute | solution.py:129
  187.8 3.0 collective-permute-done.16.refs_8_
  193.8 6.6 %shard_map.316 = (f32[128,1280]{1,0:T(8,128)S(1)}, f32[128,1280]{1,0:T(8,128)S(1)}, bf16[128,1280]{1,0:T(8,128)(2,1)S(1)}, f32[128,1280]{1,0:T(8,128)S(1)}) custom-call(s32[1]{0:T(128)} %bitcast.me_ref, f32[128,1280]{1,0:T(8,128)S(1)} %fusion.resid_ref, bf16[128,1280]{1,0:T(8,128)(2,1)S(1)} %copy-done.47, f32[1,1280]{1,0:T(1,128)S(1)} %get-tuple-element.723.gain_ref, ...), custom_call_target="tpu_custom_call" | custom-call | flops 1 | bytes 1 | tf_op jit(solution)/shard_map/pallas_call | solution.py:983
  203.8 10.0 %collective-permute-done.22.refs_2_ = bf16[1,160,3840]{2,1,0:T(8,128)(2,1)S(1)} collective-permute-done((bf16[1,160,3840]{2,1,0:T(8,128)(2,1)}, bf16[1,160,3840]{2,1,0:T(8,128)(2,1)S(1)}, u32[]{:S(2)}, u32[]{:S(2)}) %collective-permute-start.22) | collective-permute-done | bytes 1228832 | tf_op jit(solution)/shard_map/ppermute | solution.py:129
  213.8 2.6 collective-permute-done.23.refs_4_
  221.7 12.7 %collective-permute-done.24.refs_6_ = bf16[1,80,3840]{2,1,0:T(8,128)(2,1)S(1)} collective-permute-done((bf16[1,80,3840]{2,1,0:T(8,128)(2,1)S(1)}, bf16[1,80,3840]{2,1,0:T(8,128)(2,1)S(1)}, u32[]{:S(2)}, u32[]{:S(2)}) %collective-permute-start.24) | collective-permute-done | bytes 614432 | tf_op jit(solution)/shard_map/ppermute | solution.py:129
  241.2 4.1 all-to-all-start
  249.0 10.3 %shard_map.317 = (bf16[128,1280]{1,0:T(8,128)(2,1)S(1)}, bf16[128,1280]{1,0:T(8,128)(2,1)S(1)}, bf16[128,1280]{1,0:T(8,128)(2,1)S(1)}, bf16[128,1280]{1,0:T(8,12...) custom-call(s32[1]{0:T(128)} %bitcast.me_ref, f32[128,1280]{1,0:T(8,128)S(1)} %copy-done.7, ...), custom_call_target="tpu_custom_call" | custom-call | flops 1 | bytes 1 | tf_op jit(solution)/shard_map/pallas_call | solution.py:983
  279.7 6.4 %shard_map.318 = (f32[128,1280]{1,0:T(8,128)S(1)}, f32[128,1280]{1,0:T(8,128)S(1)}, bf16[128,1280]{1,0:T(8,128)(2,1)S(1)}, f32[128,1280]{1,0:T(8,128)S(1)}) custom-call(s32[1]{0:T(128)} %bitcast.me_ref, f32[128,1280]{1,0:T(8,128)S(1)} %copy-done.8, bf16[128,1280]{1,0:T(8,128)(2,1)S(1)} %copy-done.50, f32[1,1280]{1,0:T(1,128)S(1)} %get-tuple-element.721.gain_ref, ...), custom_call_target="tpu_custom_call" | custom-call | flops 1 | bytes 1 | tf_op jit(solution)/shard_map/pallas_call | solution.py:983
  290.8 11.3 %shard_map.319 = (bf16[128,1280]{1,0:T(8,128)(2,1)S(1)}, bf16[4,128,320]{2,1,0:T(8,128)(2,1)S(1)}, bf16[128,1280]{1,0:T(8,128)(2,1)S(1)}, f32[128,1280]{1,0:T(8,128)S(1)}, f32[1,1280]{1,0:T(1,128)S(1)}) custom-call(s32[1]{0:T(128)} %bitcast.me_ref, bf16[128,1280]{1,0:T(8,128)(2,1)S(1)} %convert_element_type.630.top_ref.refs_0_.refs_1_, ...), custom_call_target="tpu_custom_call" | custom-call | flops 1 | bytes 1 | tf_op jit(solution)/shard_map/pallas_call | solution.py:505
  305.0 6.0 shard_map.320
  314.2 10.5 %shard_map.321 = (f32[128,1280]{1,0:T(8,128)S(1)}, bf16[128,1280]{1,0:T(8,128)(2,1)S(1)}, bf16[128,1280]{1,0:T(8,128)(2,1)S(1)}, bf16[128,1280]{1,0:T(8,128)(2,1...) custom-call(s32[1]{0:T(128)} %bitcast.me_ref, ...), custom_call_target="tpu_custom_call" | custom-call | flops 1 | bytes 1 | tf_op jit(solution)/shard_map/pallas_call | solution.py:983
  328.7 11.8 %collective-permute-done.55 = bf16[2,3,160,640]{3,2,1,0:T(8,128)(2,1)} collective-permute-done((bf16[2,3,160,640]{3,2,1,0:T(8,128)(2,1)S(1)}, bf16[2,3,160,640]{3,2,1,0:T(8,128)(2,1)}, u32[]{:S(2)}, u32[]{:S(2)}) %collective-permute-start.55) | collective-permute-done | bytes 1228832 | tf_op jit(solution)/shard_map/ppermute | solution.py:129
  341.4 2.5 fusion.23
  345.8 7.3 %shard_map.322 = (bf16[2,3,160,640]{3,2,1,0:T(8,128)(2,1)}, bf16[2,3,160,640]{3,2,1,0:T(8,128)(2,1)}, bf16[2,3,160,640]{3,2,1,0:T(8,128)(2,1)S(1)}, bf16[3,160,1280]{2,1,0:T(8,128)(2,1)S(1)}) custom-call(s32[1]{0:T(128)} %bitcast.me_ref, bf16[128,1280]{1,0:T(8,128)(2,1)S(1)} %copy-done.51, bf16[128,1280]{1,0:T(8,128)(2,1)S(1)} %copy-done.112, ...), custom_call_target="tpu_custom_call" | custom-call | flops 1 | bytes 1 | tf_op jit(solution)/shard_map/pallas_call | solution.py:302
  355.2 3.9 collective-permute-done.57
  362.2 11.2 %shard_map.323 = (f32[128,1280]{1,0:T(8,128)S(1)}, bf16[128,3840]{1,0:T(8,128)(2,1)}, f32[1,1280]{1,0:T(1,128)S(1)}) custom-call(s32[1]{0:T(128)} %bitcast.me_ref, f32[128,1280]{1,0:T(8,128)S(1)} %get-tuple-element.408.grad_middle_ref, bf16[128,1280]{1,0:T(8,128)(2,1)S(1)} %copy-done.114, f32[128,1280]{1,0:T(8,128)S(1)} %copy-done.9, ...), custom_call_target="tpu_custom_call" | custom-call | flops 1 | bytes 1 | tf_op jit(solution)/shard_map/pallas_call | solution.py:983
  376.1 10.8 %shard_map.324 = (f32[128,1280]{1,0:T(8,128)S(1)}, bf16[128,1280]{1,0:T(8,128)(2,1)S(1)}, bf16[128,1280]{1,0:T(8,128)(2,1)}, bf16[128,1280]{1,0:T(8,128)(2,1)}, ...) custom-call(s32[1]{0:T(128)} %bitcast.me_ref, ...), custom_call_target="tpu_custom_call" | custom-call | flops 1 | bytes 1 | tf_op jit(solution)/shard_map/pallas_call | solution.py:983
  392.9 4.2 reshape.508
  397.2 2.7 copy.172
  408.2 7.8 %shard_map.325 = (bf16[2,1,160,1920]{3,2,1,0:T(8,128)(2,1)}, bf16[2,1,160,1920]{3,2,1,0:T(8,128)(2,1)}, bf16[2,1,160,1920]{3,2,1,0:T(8,128)(2,1)S(1)}, bf16[1,160,3840]{2,1,0:T(8,128)(2,1)S(1)}) custom-call(s32[1]{0:T(128)} %bitcast.me_ref, bf16[128,1280]{1,0:T(8,128)(2,1)S(1)} %copy-done.122, bf16[128,3840]{1,0:T(8,128)(2,1)} %get-tuple-element.448.refs_1_, ...), custom_call_target="tpu_custom_call" | custom-call | flops 1 | bytes 1 | tf_op jit(solution)/shard_map/pallas_call | solution.py:302
  418.2 3.5 collective-permute-done.69
  425.3 10.8 %shard_map.326 = (f32[128,1280]{1,0:T(8,128)S(1)}, bf16[128,3840]{1,0:T(8,128)(2,1)}, f32[1,1280]{1,0:T(1,128)S(1)}) custom-call(s32[1]{0:T(128)} %bitcast.me_ref, f32[128,1280]{1,0:T(8,128)S(1)} %copy-done.65, bf16[128,1280]{1,0:T(8,128)(2,1)S(1)} %copy-done.88, f32[128,1280]{1,0:T(8,128)S(1)} %fusion.resid_ref, bf16[128,1280]{1,0:T(8,128)(2,1)S(1)} %copy-done.82, ...), custom_call_target="tpu_custom_call" | custom-call | flops 1 | bytes 1 | tf_op jit(solution)/shard_map/pallas_call | solution.py:983
  436.3 2.5 shard_map.327
  446.1 5.1 collective-permute-done.78
  456.5 2.7 shard_map.328
  461.6 7.1 %shard_map.329 = (bf16[2,3,160,640]{3,2,1,0:T(8,128)(2,1)S(1)}, bf16[2,3,160,640]{3,2,1,0:T(8,128)(2,1)S(1)}, bf16[2,3,160,640]{3,2,1,0:T(8,128)(2,1)S(1)}, bf16[3,160,1280]{2,1,0:T(8,128)(2,1)S(1)}) custom-call(s32[1]{0:T(128)} %bitcast.me_ref, bf16[128,1280]{1,0:T(8,128)(2,1)S(1)} %copy-done.48, bf16[128,1280]{1,0:T(8,128)(2,1)S(1)} %copy-done.91, ...), custom_call_target="tpu_custom_call" | custom-call | flops 1 | bytes 1 | tf_op jit(solution)/shard_map/pallas_call | solution.py:302
  468.8 2.6 fusion.12
  481.1 22.6 %collective-permute-done.86 = bf16[2,3,160,640]{3,2,1,0:T(8,128)(2,1)} collective-permute-done((bf16[2,3,160,640]{3,2,1,0:T(8,128)(2,1)}, bf16[2,3,160,640]{3,2,1,0:T(8,128)(2,1)}, u32[]{:S(2)}, u32[]{:S(2)}) %collective-permute-start.86) | collective-permute-done | bytes 1228832 | tf_op jit(solution)/shard_map/ppermute | solution.py:129
  504.7 2.6 fusion.29
  509.3 5.9 collective-permute-done.84
  520.1 5.2 all-to-all-start.1
  525.3 7.6 %shard_map.330 = (bf16[2,1,160,1920]{3,2,1,0:T(8,128)(2,1)}, bf16[2,1,160,1920]{3,2,1,0:T(8,128)(2,1)}, bf16[2,1,160,1920]{3,2,1,0:T(8,128)(2,1)S(1)}, bf16[1,160,3840]{2,1,0:T(8,128)(2,1)S(1)}) custom-call(s32[1]{0:T(128)} %bitcast.me_ref, bf16[128,1280]{1,0:T(8,128)(2,1)S(1)} %copy-done.119, bf16[128,3840]{1,0:T(8,128)(2,1)} %get-tuple-element.550.refs_1_, ...), custom_call_target="tpu_custom_call" | custom-call | flops 1 | bytes 1 | tf_op jit(solution)/shard_map/pallas_call | solution.py:302
  538.2 5.1 all-to-all-start.2
  548.4 4.7 all-to-all-done.2
  554.1 3.5 all-to-all-start.3
  557.7 9.9 %collective-permute-done.99 = bf16[2,1,160,1920]{3,2,1,0:T(8,128)(2,1)} collective-permute-done((bf16[2,1,160,1920]{3,2,1,0:T(8,128)(2,1)}, bf16[2,1,160,1920]{3,2,1,0:T(8,128)(2,1)}, u32[]{:S(2)}, u32[]{:S(2)}) %collective-permute-start.99) | collective-permute-done | bytes 1228832 | tf_op jit(solution)/shard_map/ppermute | solution.py:129
  568.2 2.6 fusion.30
  577.4 10.6 %collective-permute-done.101 = bf16[1,160,1920]{2,1,0:T(8,128)(2,1)} collective-permute-done((bf16[1,160,1920]{2,1,0:T(8,128)(2,1)}, bf16[1,160,1920]{2,1,0:T(8,128)(2,1)}, u32[]{:S(2)}, u32[]{:S(2)}) %collective-permute-start.101) | collective-permute-done | bytes 614432 | tf_op jit(solution)/shard_map/ppermute | solution.py:129
  592.5 5.0 all-to-all-start.4
  600.5 3.4 fusion.50
  616.6 6.8 %shard_map.331 = (f32[32,40,1280]{2,1,0:T(8,128)}, f32[32,8,1280]{2,1,0:T(8,128)S(1)}) custom-call(s32[1]{0:T(128)} %bitcast.me_ref, bf16[1,192,1280]{2,1,0:T(8,128)(2,1)S(1)} %bitcast.180, bf16[1,192,1280]{2,1,0:T(8,128)(2,1)S(1)} %collective-permute-done.90.refs_1_, bf16[1,192,1280]{2,1,0:T(8,128)(2,1)S(1)} %collective-permute-done.91.refs_2_, ...), custom_call_target="tpu_custom_call" | custom-call | flops 1 | bytes 1 | tf_op jit(solution)/shard_map/pallas_call | solution.py:741
  (686 shorter events, 223.1 us)
Async XLA Ops:
  7.2 37.7 %all-gather.10.cloned.1.call-start = ((), (), s32[]{:S(2)}) async-start(), calls=%async_computation.10 | async-start | bytes 1587200 | tf_op jit(solution)/shard_map/all_gather | solution.py:214
  10.1 67.3 %all-gather.8.cloned.1.call-start = ((), (), s32[]{:S(2)}) async-start(), calls=%async_computation.9 | async-start | bytes 1536000 | tf_op jit(solution)/shard_map/all_gather | solution.py:214
  12.3 108.5 %all-gather.12.cloned.1.call-start = ((), (), s32[]{:S(2)}) async-start(), calls=%async_computation.11 | async-start | bytes 1536000 | tf_op jit(solution)/shard_map/all_gather | solution.py:214
  44.9 32.5 %collective-permute-start = (bf16[1,160,3968]{2,1,0:T(8,128)(2,1)}, bf16[1,160,3968]{2,1,0:T(8,128)(2,1)S(1)}, u32[]{:S(2)}, u32[]{:S(2)}) collective-permute-start(bf16[1,160,3968]{2,1,0:T(8,128)(2,1)} %bitcast.20.refs_0_), channel_id=1, source_target_pairs={{0,8},{4,12},{8,0},{12,4},{16,24},{20,28},{24,16},{28,20},{1,9},{5... | collective-permute-start | bytes 3809288 | tf_op jit(solution)/shard_map/ppermute | solution.py:129
  46.4 31.0 %collective-permute-start.1 = (bf16[1,160,3968]{2,1,0:T(8,128)(2,1)}, bf16[1,160,3968]{2,1,0:T(8,128)(2,1)S(1)}, u32[]{:S(2)}, u32[]{:S(2)}) collective-permute-start(bf16[1,160,3968]{2,1,0:T(8,128)(2,1)} %bitcast.20.refs_0_), channel_id=1, source_target_pairs={{0,16},{4,20},{8,24},{12,28},{16,0},{20,4},{24,8},{28,12},{1,17},{... | collective-permute-start | bytes 3809288 | tf_op jit(solution)/shard_map/ppermute | solution.py:129
  77.5 91.4 %all-gather.14.cloned.1.call-start = ((), (), s32[]{:S(2)}) async-start(), calls=%async_computation.12 | async-start | bytes 1536000 | tf_op jit(solution)/shard_map/all_gather | solution.py:214
  80.7 38.8 %collective-permute-start.4 = (bf16[1,160,3840]{2,1,0:T(8,128)(2,1)S(1)}, bf16[1,160,3840]{2,1,0:T(8,128)(2,1)}, u32[]{:S(2)}, u32[]{:S(2)}) collective-permute-start(bf16[1,160,3840]{2,1,0:T(8,128)(2,1)S(1)} %bitcast.168), channel_id=1, source_target_pairs={{0,8},{4,12},{8,0},{12,4},{16,24},{20,28},{24,16},{28,20},{1,9},{5... | collective-permute-start | bytes 3686408 | tf_op jit(solution)/shard_map/ppermute | solution.py:129
  81.3 39.6 %collective-permute-start.5 = (bf16[1,160,3840]{2,1,0:T(8,128)(2,1)S(1)}, bf16[1,160,3840]{2,1,0:T(8,128)(2,1)}, u32[]{:S(2)}, u32[]{:S(2)}) collective-permute-start(bf16[1,160,3840]{2,1,0:T(8,128)(2,1)S(1)} %bitcast.169), channel_id=1, source_target_pairs={{0,16},{4,20},{8,24},{12,28},{16,0},{20,4},{24,8},{28,12},{1,17},{... | collective-permute-start | bytes 3686408 | tf_op jit(solution)/shard_map/ppermute | solution.py:129
  82.6 44.7 %collective-permute-start.8 = (bf16[1,160,3968]{2,1,0:T(8,128)(2,1)}, bf16[1,160,3968]{2,1,0:T(8,128)(2,1)}, u32[]{:S(2)}, u32[]{:S(2)}) collective-permute-start(bf16[1,160,3968]{2,1,0:T(8,128)(2,1)} %bitcast.20.refs_0_), channel_id=1, source_target_pairs={{0,4},{4,0},{8,12},{12,8},{16,20},{20,16},{24,28},{28,24},{1,5},{5... | collective-permute-start | bytes 3809288 | tf_op jit(solution)/shard_map/ppermute | solution.py:129
  94.9 32.5 %collective-permute-start.9 = (bf16[1,160,3968]{2,1,0:T(8,128)(2,1)S(1)}, bf16[1,160,3968]{2,1,0:T(8,128)(2,1)}, u32[]{:S(2)}, u32[]{:S(2)}) collective-permute-start(bf16[1,160,3968]{2,1,0:T(8,128)(2,1)S(1)} %collective-permute-done.refs_2_), channel_id=1, source_target_pairs={{0,4},{4,0},{8,12},{12,8},{16,20},{20,16},{24,28},{28,24},{1,5},{5... | collective-permute-start | bytes 3809288 | tf_op jit(solution)/shard_map/ppermute | solution.py:129
  96.5 31.4 %collective-permute-start.10 = (bf16[1,160,3968]{2,1,0:T(8,128)(2,1)S(1)}, bf16[1,160,3968]{2,1,0:T(8,128)(2,1)}, u32[]{:S(2)}, u32[]{:S(2)}) collective-permute-start(bf16[1,160,3968]{2,1,0:T(8,128)(2,1)S(1)} %collective-permute-done.1.refs_4_), channel_id=1, source_target_pairs={{0,4},{4,0},{8,12},{12,8},{16,20},{20,16},{24,28},{28,24},{1,5},{5... | collective-permute-start | bytes 3809288 | tf_op jit(solution)/shard_map/ppermute | solution.py:129
  123.3 93.0 %all-gather.16.cloned.1.call-start = ((), (), s32[]{:S(2)}) async-start(), calls=%async_computation.13 | async-start | bytes 1638400 | tf_op jit(solution)/shard_map/all_gather | solution.py:1275
  127.9 41.0 %collective-permute-start.13 = (bf16[1,160,3840]{2,1,0:T(8,128)(2,1)}, bf16[1,160,3840]{2,1,0:T(8,128)(2,1)}, u32[]{:S(2)}, u32[]{:S(2)}) collective-permute-start(bf16[1,160,3840]{2,1,0:T(8,128)(2,1)} %bitcast.172), channel_id=1, source_target_pairs={{0,8},{4,12},{8,0},{12,4},{16,24},{20,28},{24,16},{28,20},{1,9},{5... | collective-permute-start | bytes 3686408 | tf_op jit(solution)/shard_map/ppermute | solution.py:129
  139.9 29.0 %collective-permute-start.14 = (bf16[1,160,3840]{2,1,0:T(8,128)(2,1)}, bf16[1,160,3840]{2,1,0:T(8,128)(2,1)}, u32[]{:S(2)}, u32[]{:S(2)}) collective-permute-start(bf16[1,160,3840]{2,1,0:T(8,128)(2,1)} %bitcast.173), channel_id=1, source_target_pairs={{0,16},{4,20},{8,24},{12,28},{16,0},{20,4},{24,8},{28,12},{1,17},{... | collective-permute-start | bytes 3686408 | tf_op jit(solution)/shard_map/ppermute | solution.py:129
  142.4 33.1 %collective-permute-start.17 = (bf16[1,160,3840]{2,1,0:T(8,128)(2,1)}, bf16[1,160,3840]{2,1,0:T(8,128)(2,1)}, u32[]{:S(2)}, u32[]{:S(2)}) collective-permute-start(bf16[1,160,3840]{2,1,0:T(8,128)(2,1)} %bitcast.167), channel_id=1, source_target_pairs={{0,4},{4,0},{8,12},{12,8},{16,20},{20,16},{24,28},{28,24},{1,5},{5... | collective-permute-start | bytes 3686408 | tf_op jit(solution)/shard_map/ppermute | solution.py:129
  144.6 30.9 %collective-permute-start.18 = (bf16[1,160,3840]{2,1,0:T(8,128)(2,1)}, bf16[1,160,3840]{2,1,0:T(8,128)(2,1)}, u32[]{:S(2)}, u32[]{:S(2)}) collective-permute-start(bf16[1,160,3840]{2,1,0:T(8,128)(2,1)} %collective-permute-done.4.refs_2_), channel_id=1, source_target_pairs={{0,4},{4,0},{8,12},{12,8},{16,20},{20,16},{24,28},{28,24},{1,5},{5... | collective-permute-start | bytes 3686408 | tf_op jit(solution)/shard_map/ppermute | solution.py:129
  145.2 30.5 %collective-permute-start.19 = (bf16[1,160,3840]{2,1,0:T(8,128)(2,1)}, bf16[1,160,3840]{2,1,0:T(8,128)(2,1)}, u32[]{:S(2)}, u32[]{:S(2)}) collective-permute-start(bf16[1,160,3840]{2,1,0:T(8,128)(2,1)} %collective-permute-done.5.refs_4_), channel_id=1, source_target_pairs={{0,4},{4,0},{8,12},{12,8},{16,20},{20,16},{24,28},{28,24},{1,5},{5... | collective-permute-start | bytes 3686408 | tf_op jit(solution)/shard_map/ppermute | solution.py:129
  175.5 38.3 %collective-permute-start.22 = (bf16[1,160,3840]{2,1,0:T(8,128)(2,1)}, bf16[1,160,3840]{2,1,0:T(8,128)(2,1)S(1)}, u32[]{:S(2)}, u32[]{:S(2)}) collective-permute-start(bf16[1,160,3840]{2,1,0:T(8,128)(2,1)} %bitcast.26.refs_0_), channel_id=1, source_target_pairs={{0,8},{4,12},{8,0},{12,4},{16,24},{20,28},{24,16},{28,20},{1,9},{5... | collective-permute-start | bytes 3686408 | tf_op jit(solution)/shard_map/ppermute | solution.py:129
  175.7 40.7 %collective-permute-start.23 = (bf16[1,160,3840]{2,1,0:T(8,128)(2,1)}, bf16[1,160,3840]{2,1,0:T(8,128)(2,1)}, u32[]{:S(2)}, u32[]{:S(2)}) collective-permute-start(bf16[1,160,3840]{2,1,0:T(8,128)(2,1)} %bitcast.26.refs_0_), channel_id=1, source_target_pairs={{0,16},{4,20},{8,24},{12,28},{16,0},{20,4},{24,8},{28,12},{1,17},{... | collective-permute-start | bytes 3686408 | tf_op jit(solution)/shard_map/ppermute | solution.py:129
  190.8 28.6 %collective-permute-start.26 = (bf16[1,160,3840]{2,1,0:T(8,128)(2,1)}, bf16[1,160,3840]{2,1,0:T(8,128)(2,1)}, u32[]{:S(2)}, u32[]{:S(2)}) collective-permute-start(bf16[1,160,3840]{2,1,0:T(8,128)(2,1)} %bitcast.174), channel_id=1, source_target_pairs={{0,4},{4,0},{8,12},{12,8},{16,20},{20,16},{24,28},{28,24},{1,5},{5... | collective-permute-start | bytes 3686408 | tf_op jit(solution)/shard_map/ppermute | solution.py:129
  190.8 28.6 %collective-permute-start.27 = (bf16[1,160,3840]{2,1,0:T(8,128)(2,1)}, bf16[1,160,3840]{2,1,0:T(8,128)(2,1)}, u32[]{:S(2)}, u32[]{:S(2)}) collective-permute-start(bf16[1,160,3840]{2,1,0:T(8,128)(2,1)} %collective-permute-done.13.refs_2_), channel_id=1, source_target_pairs={{0,4},{4,0},{8,12},{12,8},{16,20},{20,16},{24,28},{28,24},{1,5},{5... | collective-permute-start | bytes 3686408 | tf_op jit(solution)/shard_map/ppermute | solution.py:129
  191.3 28.6 %collective-permute-start.28 = (bf16[1,160,3840]{2,1,0:T(8,128)(2,1)}, bf16[1,160,3840]{2,1,0:T(8,128)(2,1)}, u32[]{:S(2)}, u32[]{:S(2)}) collective-permute-start(bf16[1,160,3840]{2,1,0:T(8,128)(2,1)} %collective-permute-done.14.refs_4_), channel_id=1, source_target_pairs={{0,4},{4,0},{8,12},{12,8},{16,20},{20,16},{24,28},{28,24},{1,5},{5... | collective-permute-start | bytes 3686408 | tf_op jit(solution)/shard_map/ppermute | solution.py:129
  220.0 43.6 %collective-permute-start.31 = (bf16[4,160,960]{2,1,0:T(8,128)(2,1)}, bf16[4,160,960]{2,1,0:T(8,128)(2,1)}, u32[]{:S(2)}, u32[]{:S(2)}) collective-permute-start(bf16[4,160,960]{2,1,0:T(8,128)(2,1)} %all-gather.16.cloned.1.call-done.refs_0_), channel_id=1, source_target_pairs={{0,8},{4,12},{8,0},{12,4},{16,24},{20,28},{24,16},{28,20},{1,9},{5... | collective-permute-start | bytes 3686408 | tf_op jit(solution)/shard_map/ppermute | solution.py:129
  234.4 29.1 %collective-permute-start.32 = (bf16[4,160,960]{2,1,0:T(8,128)(2,1)}, bf16[4,160,960]{2,1,0:T(8,128)(2,1)}, u32[]{:S(2)}, u32[]{:S(2)}) collective-permute-start(bf16[4,160,960]{2,1,0:T(8,128)(2,1)} %all-gather.16.cloned.1.call-done.refs_0_), channel_id=1, source_target_pairs={{0,16},{4,20},{8,24},{12,28},{16,0},{20,4},{24,8},{28,12},{1,17},{... | collective-permute-start | bytes 3686408 | tf_op jit(solution)/shard_map/ppermute | solution.py:129
  235.9 32.2 %collective-permute-start.35 = (bf16[1,160,3840]{2,1,0:T(8,128)(2,1)}, bf16[1,160,3840]{2,1,0:T(8,128)(2,1)}, u32[]{:S(2)}, u32[]{:S(2)}) collective-permute-start(bf16[1,160,3840]{2,1,0:T(8,128)(2,1)} %bitcast.26.refs_0_), channel_id=1, source_target_pairs={{0,4},{4,0},{8,12},{12,8},{16,20},{20,16},{24,28},{28,24},{1,5},{5... | collective-permute-start | bytes 3686408 | tf_op jit(solution)/shard_map/ppermute | solution.py:129
  236.9 31.5 %collective-permute-start.36 = (bf16[1,160,3840]{2,1,0:T(8,128)(2,1)S(1)}, bf16[1,160,3840]{2,1,0:T(8,128)(2,1)}, u32[]{:S(2)}, u32[]{:S(2)}) collective-permute-start(bf16[1,160,3840]{2,1,0:T(8,128)(2,1)S(1)} %collective-permute-done.22.refs_2_), channel_id=1, source_target_pairs={{0,4},{4,0},{8,12},{12,8},{16,20},{20,16},{24,28},{28,24},{1,5},{5... | collective-permute-start | bytes 3686408 | tf_op jit(solution)/shard_map/ppermute | solution.py:129
  239.2 29.9 %collective-permute-start.37 = (bf16[1,160,3840]{2,1,0:T(8,128)(2,1)}, bf16[1,160,3840]{2,1,0:T(8,128)(2,1)}, u32[]{:S(2)}, u32[]{:S(2)}) collective-permute-start(bf16[1,160,3840]{2,1,0:T(8,128)(2,1)} %collective-permute-done.23.refs_4_), channel_id=1, source_target_pairs={{0,4},{4,0},{8,12},{12,8},{16,20},{20,16},{24,28},{28,24},{1,5},{5... | collective-permute-start | bytes 3686408 | tf_op jit(solution)/shard_map/ppermute | solution.py:129
  245.3 200.8 %reduce-scatter.9.cloned.1.call-start = ((), (), s32[]{:S(2)}) async-start(), calls=%async_computation.14 | async-start | bytes 1843200 | tf_op jit(solution)/shard_map/reduce_scatter | solution.py:389
  311.0 29.5 %collective-permute-start.55 = (bf16[2,3,160,640]{3,2,1,0:T(8,128)(2,1)S(1)}, bf16[2,3,160,640]{3,2,1,0:T(8,128)(2,1)}, u32[]{:S(2)}, u32[]{:S(2)}) collective-permute-start(bf16[2,3,160,640]{3,2,1,0:T(8,128)(2,1)S(1)} %get-tuple-element.382), channel_id=1, source_target_pairs={{0,8},{4,12},{8,0},{12,4},{16,24},{20,28},{24,16},{28,20},{1,9},{5... | collective-permute-start | bytes 3686408 | tf_op jit(solution)/shard_map/ppermute | solution.py:129
  312.3 29.1 %collective-permute-start.56 = (bf16[2,3,160,640]{3,2,1,0:T(8,128)(2,1)S(1)}, bf16[2,3,160,640]{3,2,1,0:T(8,128)(2,1)}, u32[]{:S(2)}, u32[]{:S(2)}) collective-permute-start(bf16[2,3,160,640]{3,2,1,0:T(8,128)(2,1)S(1)} %get-tuple-element.383), channel_id=1, source_target_pairs={{0,16},{4,20},{8,24},{12,28},{16,0},{20,4},{24,8},{28,12},{1,17},{... | collective-permute-start | bytes 3686408 | tf_op jit(solution)/shard_map/ppermute | solution.py:129
  360.2 43.1 %collective-permute-start.67 = (bf16[2,3,160,640]{3,2,1,0:T(8,128)(2,1)}, bf16[2,3,160,640]{3,2,1,0:T(8,128)(2,1)}, u32[]{:S(2)}, u32[]{:S(2)}) collective-permute-start(bf16[2,3,160,640]{3,2,1,0:T(8,128)(2,1)} %get-tuple-element.425), channel_id=1, source_target_pairs={{0,8},{4,12},{8,0},{12,4},{16,24},{20,28},{24,16},{28,20},{1,9},{5... | collective-permute-start | bytes 3686408 | tf_op jit(solution)/shard_map/ppermute | solution.py:129
  360.8 42.5 %collective-permute-start.68 = (bf16[2,3,160,640]{3,2,1,0:T(8,128)(2,1)}, bf16[2,3,160,640]{3,2,1,0:T(8,128)(2,1)}, u32[]{:S(2)}, u32[]{:S(2)}) collective-permute-start(bf16[2,3,160,640]{3,2,1,0:T(8,128)(2,1)} %get-tuple-element.426), channel_id=1, source_target_pairs={{0,16},{4,20},{8,24},{12,28},{16,0},{20,4},{24,8},{28,12},{1,17},{... | collective-permute-start | bytes 3686408 | tf_op jit(solution)/shard_map/ppermute | solution.py:129
  361.6 28.9 %collective-permute-start.63 = (bf16[128,1280]{1,0:T(8,128)(2,1)S(1)}, bf16[128,1280]{1,0:T(8,128)(2,1)S(1)}, u32[]{:S(2)}, u32[]{:S(2)}) collective-permute-start(bf16[128,1280]{1,0:T(8,128)(2,1)S(1)} %copy-done.90), channel_id=1, source_target_pairs={{0,4},{4,0},{8,12},{12,8},{16,20},{20,16},{24,28},{28,24},{1,5},{5... | collective-permute-start | bytes 983048 | tf_op jit(solution)/shard_map/ppermute | solution.py:129
  361.6 29.3 %collective-permute-start.59 = (bf16[128,1280]{1,0:T(8,128)(2,1)S(1)}, bf16[128,1280]{1,0:T(8,128)(2,1)S(1)}, u32[]{:S(2)}, u32[]{:S(2)}) collective-permute-start(bf16[128,1280]{1,0:T(8,128)(2,1)S(1)} %copy-done.121), channel_id=1, source_target_pairs={{0,4},{4,0},{8,12},{12,8},{16,20},{20,16},{24,28},{28,24},{1,5},{5... | collective-permute-start | bytes 983048 | tf_op jit(solution)/shard_map/ppermute | solution.py:129
  373.5 29.8 %collective-permute-start.60 = (bf16[128,3840]{1,0:T(8,128)(2,1)}, bf16[128,3840]{1,0:T(8,128)(2,1)}, u32[]{:S(2)}, u32[]{:S(2)}) collective-permute-start(bf16[128,3840]{1,0:T(8,128)(2,1)} %get-tuple-element.448.refs_1_), channel_id=1, source_target_pairs={{0,4},{4,0},{8,12},{12,8},{16,20},{20,16},{24,28},{28,24},{1,5},{5... | collective-permute-start | bytes 2949128 | tf_op jit(solution)/shard_map/ppermute | solution.py:129
  399.9 77.6 %reduce-scatter.13.cloned.1.call-start = ((), (), s32[]{:S(2)}) async-start(), calls=%async_computation.17 | async-start | bytes 1536000
  422.6 28.6 %collective-permute-start.78 = (bf16[2,1,160,1920]{3,2,1,0:T(8,128)(2,1)}, bf16[2,1,160,1920]{3,2,1,0:T(8,128)(2,1)}, u32[]{:S(2)}, u32[]{:S(2)}) collective-permute-start(bf16[2,1,160,1920]{3,2,1,0:T(8,128)(2,1)} %get-tuple-element.488), channel_id=1, source_target_pairs={{0,8},{4,12},{8,0},{12,4},{16,24},{20,28},{24,16},{28,20},{1,9},{5... | collective-permute-start | bytes 3686408 | tf_op jit(solution)/shard_map/ppermute | solution.py:129
  446.0 111.6 %reduce-scatter.11.cloned.1.call-start = ((), (), s32[]{:S(2)}) async-start(), calls=%async_computation.15 | async-start | bytes 1536000 | tf_op jit(solution)/shard_map/reduce_scatter | solution.py:367
  472.6 127.9 %all-gather.18.cloned.1.call-start = ((), (), s32[]{:S(2)}) async-start(), calls=%async_computation.16 | async-start | bytes 3317760 | tf_op jit(solution)/shard_map/all_gather | solution.py:396
  473.4 30.3 %collective-permute-start.86 = (bf16[2,3,160,640]{3,2,1,0:T(8,128)(2,1)}, bf16[2,3,160,640]{3,2,1,0:T(8,128)(2,1)}, u32[]{:S(2)}, u32[]{:S(2)}) collective-permute-start(bf16[2,3,160,640]{3,2,1,0:T(8,128)(2,1)} %copy-done.143), channel_id=1, source_target_pairs={{0,8},{4,12},{8,0},{12,4},{16,24},{20,28},{24,16},{28,20},{1,9},{5... | collective-permute-start | bytes 3686408 | tf_op jit(solution)/shard_map/ppermute | solution.py:129
  474.7 30.1 %collective-permute-start.87 = (bf16[2,3,160,640]{3,2,1,0:T(8,128)(2,1)S(1)}, bf16[2,3,160,640]{3,2,1,0:T(8,128)(2,1)}, u32[]{:S(2)}, u32[]{:S(2)}) collective-permute-start(bf16[2,3,160,640]{3,2,1,0:T(8,128)(2,1)S(1)} %copy-done.142), channel_id=1, source_target_pairs={{0,16},{4,20},{8,24},{12,28},{16,0},{20,4},{24,8},{28,12},{1,17},{... | collective-permute-start | bytes 3686408 | tf_op jit(solution)/shard_map/ppermute | solution.py:129
  476.0 39.2 %collective-permute-start.84 = (bf16[2,1,192,640]{3,2,1,0:T(8,128)(2,1)}, bf16[2,1,192,640]{3,2,1,0:T(8,128)(2,1)}, u32[]{:S(2)}, u32[]{:S(2)}) collective-permute-start(bf16[2,1,192,640]{3,2,1,0:T(8,128)(2,1)} %copy-done.146), channel_id=1, source_target_pairs={{0,16},{4,20},{8,24},{12,28},{16,0},{20,4},{24,8},{28,12},{1,17},{... | collective-permute-start | bytes 1474568 | tf_op jit(solution)/shard_map/ppermute | solution.py:129
  476.7 38.6 %collective-permute-start.82 = (bf16[2,1,192,640]{3,2,1,0:T(8,128)(2,1)S(1)}, bf16[2,1,192,640]{3,2,1,0:T(8,128)(2,1)}, u32[]{:S(2)}, u32[]{:S(2)}) collective-permute-start(bf16[2,1,192,640]{3,2,1,0:T(8,128)(2,1)S(1)} %copy-done.145), channel_id=1, source_target_pairs={{0,8},{4,12},{8,0},{12,4},{16,24},{20,28},{24,16},{28,20},{1,9},{5... | collective-permute-start | bytes 1474568 | tf_op jit(solution)/shard_map/ppermute | solution.py:129
  533.9 33.7 %collective-permute-start.99 = (bf16[2,1,160,1920]{3,2,1,0:T(8,128)(2,1)}, bf16[2,1,160,1920]{3,2,1,0:T(8,128)(2,1)}, u32[]{:S(2)}, u32[]{:S(2)}) collective-permute-start(bf16[2,1,160,1920]{3,2,1,0:T(8,128)(2,1)} %get-tuple-element.564), channel_id=1, source_target_pairs={{0,8},{4,12},{8,0},{12,4},{16,24},{20,28},{24,16},{28,20},{1,9},{5... | collective-permute-start | bytes 3686408 | tf_op jit(solution)/shard_map/ppermute | solution.py:129
  534.8 33.4 %collective-permute-start.100 = (bf16[2,1,160,1920]{3,2,1,0:T(8,128)(2,1)}, bf16[2,1,160,1920]{3,2,1,0:T(8,128)(2,1)}, u32[]{:S(2)}, u32[]{:S(2)}) collective-permute-start(bf16[2,1,160,1920]{3,2,1,0:T(8,128)(2,1)} %get-tuple-element.565), channel_id=1, source_target_pairs={{0,16},{4,20},{8,24},{12,28},{16,0},{20,4},{24,8},{28,12},{1,17},{... | collective-permute-start | bytes 3686408 | tf_op jit(solution)/shard_map/ppermute | solution.py:129
  543.2 67.9 %reduce-scatter.15.cloned.1.call-start = ((), (), s32[]{:S(2)}) async-start(), calls=%async_computation.18 | async-start | bytes 1536000
  575.8 40.8 %collective-permute-start.90 = (bf16[1,192,1280]{2,1,0:T(8,128)(2,1)S(1)}, bf16[1,192,1280]{2,1,0:T(8,128)(2,1)S(1)}, u32[]{:S(2)}, u32[]{:S(2)}) collective-permute-start(bf16[1,192,1280]{2,1,0:T(8,128)(2,1)S(1)} %bitcast.177), channel_id=1, source_target_pairs={{0,4},{4,0},{8,12},{12,8},{16,20},{20,16},{24,28},{28,24},{1,5},{5... | collective-permute-start | bytes 1474568 | tf_op jit(solution)/shard_map/ppermute | solution.py:129
  592.5 33.9 %all-to-all-start.4 = ((bf16[1,4,40,3840]{3,2,0,1:T(8,128)(2,1)}), bf16[1,4,40,3840]{3,2,0,1:T(8,128)(2,1)}, u32[]{:S(2)}, u32[]{:S(2)}) async-start(bf16[1,4,40,3840]{3,2,0,1:T(8,128)(2,1)} %bitcast.64), calls=%async_computation.6 | async-start | bytes 2457600 | tf_op jit(solution)/shard_map/all_to_all | solution.py:379
  (245 other events, 2419.3 us)
Sparse Core Ops, SparseCore 0:
  10.2 34.6 all-gather.9
  47.1 30.3 all-gather.7
  79.6 30.3 all-gather.11
  123.5 31.1 all-gather.13
  172.9 31.6 all-gather.15
  400.0 34.8 reduce-scatter.8
  446.1 30.5 reduce-scatter.12
  479.7 28.8 reduce-scatter.10
  510.6 41.4 all-gather.17
  555.0 32.3 reduce-scatter.14
where the time goes:
time: 642 us; the launch traced here: 636 us
  waiting for transfers between devices  235 us (37%)
  Pallas kernels  137 us (21%)
  local copies, waits for them, and re-layouts  113 us (18%)
  starting transfers between devices  87 us (14%)
  other arithmetic  46 us (7%)
  between operations  16.4 us (3%)
    ppermute x103, waiting for transfers between devices, swap(): return lax.ppermute(v, 'dp', [(i, i ^ 1 << bit) for i in range(size)])  176 us
    pallas_call x8, Pallas kernels, whole_call(): pl.pallas_call(partial(kernel, plan), out_shape=[jax.ShapeDtypeStruct(sha...  76.7 us
    unnamed x368, local copies, waits for them, and re-layouts  72.9 us
    ppermute x103, starting transfers between devices, swap(): return lax.ppermute(v, 'dp', [(i, i ^ 1 << bit) for i in range(size)])  63 us
    all_gather x4, waiting for transfers between devices, gather_head(): held = lax.all_gather(own, 'head', axis=0, tiled=True)[None]  53.7 us
    pallas_call x5, Pallas kernels, pair_products(): pl.pallas_call(partial(product_kernel, count, outer), out_shape=[jax.Shap...  35.8 us
    convert_element_type x12, other arithmetic, low_sum(): return total.astype(jnp.bfloat16)  25.6 us
    slice x12, local copies, waits for them, and re-layouts, second_step(): return (from_y[:, :half], from_x[:, half:])  13.7 us
  transfers between devices with their start and end apart: 118, of which 38 were waited for; matrix products, arithmetic and copies ran while one was open for 16% of the time, Pallas kernels for 21%

commit v1 on v0

--- a/solution.py
+++ b/solution.py
@@ -733,7 +733,7 @@
     if held.shape[0] > 1 or own % 8 or not in_kernel(pieces):
         (whole,) = place(places, pieces, [columns])
         whole = whole.reshape(-1, span, columns).astype(jnp.float32)
-        return whole[:, :own].reshape(-1, columns), whole[:, own:].reshape(-1, columns)[:count], held
+        return whole[:, :own].reshape(-1, columns), whole[:, own:].reshape(-1, columns)[:count]
     rows = held.shape[1]
     blocks = 8 * rows // span
     plan = [(rel, row, array.shape[1]) for rel, row, array in pieces]
@@ -754,7 +754,7 @@
         compiler_params=pltpu.CompilerParams(vmem_limit_bytes=44 << 20),
         cost_estimate=SMALL_COST,
     )(places, *[array for _, _, array in pieces])
-    return main.reshape(-1, columns), extra.reshape(-1, columns)[:count], held
+    return main.reshape(-1, columns), extra.reshape(-1, columns)[:count]
 
 
 def fetch(plan, me, pieces, whole, sems):
@@ -1416,7 +1416,7 @@
     carry = {"grad": grad_resid}
     boths = {0: head_both}
     sums = {0: RowSums(*pair_products(me, head_both))}
-    totals, finished = {}, {}
+    finished = {}
     entry_chunk = None
     done = 0
 
@@ -1433,12 +1433,8 @@
     for number in range(stage_count + 1):
         carry, boths = step["carry"], step["boths"]
         parts = {"first": sums[number].first()}
-        if number >= 1:
-            totals[number - 1] = sums.pop(number - 1).total()
-            if number == 1:
-                finished[0] = sum_columns(totals[0])
-            else:
-                finished[number - 1] = sum_group(totals[number - 1])
+        if number >= 2:
+            finished[number - 1] = sum_group(sums.pop(number - 1).total())
         if number >= 2:
             parts["finished"] = finished[number - 2]
         until = number + 1 if number == 0 else number + 2
@@ -1458,6 +1454,8 @@
             finished[number - 2] = step["finished"]
         carry, boths = step["carry"], step["boths"]
         parts = {"last": sums[number].last()}
+        if number == 1:
+            finished[0] = sum_columns(sums.pop(0).total())
         if number == stage_count - 2:
             if layers[0].fetched:
                 entry_chunk = input_products(me, step["entry"])
@@ -1478,11 +1476,9 @@
         if number == stage_count - 1:
             entry_chunk.last_met = step["entry"]
     finished[stage_count] = sum_group_at_once(sums[stage_count].total())
-    entry_main, entry_extra, entry_held = entry_everywhere(
-        me, entry_summed, own_count, extra_count
-    )
+    entry_main, entry_extra = entry_everywhere(me, entry_summed, own_count, extra_count)
     head_rows = gather_blocks(me, finished[0])
-    head_sums = [after(head_rows[n], entry_held).astype(jnp.float32) for n in range(3)]
+    head_sums = [after(head_rows[n], entry_summed).astype(jnp.float32) for n in range(3)]
     layer_sums = [None] * layer_count
     for member, layer_index in enumerate(reversed(range(layer_count))):
         rest = finished[1 + 2 * member].astype(jnp.float32)

time: 642 us -> 639 us (level)
    unnamed x368 -> x378, local copies, waits for them, and re-layouts: 72.9 us -> 69.7 us
  transfers between devices with their start and end apart: 118 -> 118, of which waited for: 38 -> 41; matrix products, arithmetic and copies ran while one was open for 16% -> 14% of each run, Pallas kernels for 21% -> 21%
where the time goes in v1:
time: 639 us; the launch traced here: 633 us
  waiting for transfers between devices  238 us (37%)
  Pallas kernels  136 us (21%)
  local copies, waits for them, and re-layouts  109 us (17%)
  starting transfers between devices  86.4 us (14%)
  other arithmetic  45.5 us (7%)
  between operations  16.5 us (3%)
    ppermute x103, waiting for transfers between devices, swap(): return lax.ppermute(v, 'dp', [(i, i ^ 1 << bit) for i in range(size)])  178 us
    pallas_call x8, Pallas kernels, whole_call(): pl.pallas_call(partial(kernel, plan), out_shape=[jax.ShapeDtypeStruct(sha...  76.7 us
    unnamed x378, local copies, waits for them, and re-layouts  69.7 us
    ppermute x103, starting transfers between devices, swap(): return lax.ppermute(v, 'dp', [(i, i ^ 1 << bit) for i in range(size)])  62.5 us
    all_gather x4, waiting for transfers between devices, gather_head(): held = lax.all_gather(own, 'head', axis=0, tiled=True)[None]  53.7 us
    pallas_call x5, Pallas kernels, pair_products(): pl.pallas_call(partial(product_kernel, count, outer), out_shape=[jax.Shap...  34.9 us
    convert_element_type x12, other arithmetic, low_sum(): return total.astype(jnp.bfloat16)  25.2 us
    slice x12, local copies, waits for them, and re-layouts, second_step(): return (from_y[:, :half], from_x[:, half:])  13.7 us
  transfers between devices with their start and end apart: 118, of which 41 were waited for; matrix products, arithmetic and copies ran while one was open for 14% of the time, Pallas kernels for 21%

profile of v1, /device:TPU:0, one launch (start us, length us, event | category | flops | bytes accessed | tf_op | source)
XLA Modules:
  0.0 633.5 jit_solution(3781570726830204455)
XLA Ops:
  16.9 28.0 %all-gather.10.cloned.1.call-done = bf16[160,3968]{1,0:T(8,128)(2,1)} async-done(((bf16[40,3968]{1,0:T(8,128)(2,1)}), bf16[160,3968]{1,0:T(8,128)(2,1)}) %all-gather.10.cloned.1.call-update) | async-done | bytes 1269776 | tf_op jit(solution)/shard_map/all_gather | solution.py:214
  51.8 25.7 %all-gather.8.cloned.1.call-done = bf16[160,3840]{1,0:T(8,128)(2,1)} async-done(((bf16[40,3840]{1,0:T(8,128)(2,1)}), bf16[160,3840]{1,0:T(8,128)(2,1)}) %all-gather.8.cloned.1.call-update) | async-done | bytes 1228816 | tf_op jit(solution)/shard_map/all_gather | solution.py:214
  82.6 12.3 %collective-permute-done.2.refs_6_ = bf16[1,80,3968]{2,1,0:T(8,128)(2,1)S(1)} collective-permute-done((bf16[1,80,3968]{2,1,0:T(8,128)(2,1)S(1)}, bf16[1,80,3968]{2,1,0:T(8,128)(2,1)S(1)}, u32[]{:S(2)}, u32[]{:S(2)}) %collective-permute-start.2) | collective-permute-done | bytes 634912 | tf_op jit(solution)/shard_map/ppermute | solution.py:129
  96.5 23.0 %collective-permute-done.4.refs_2_ = bf16[1,160,3840]{2,1,0:T(8,128)(2,1)} collective-permute-done((bf16[1,160,3840]{2,1,0:T(8,128)(2,1)S(1)}, bf16[1,160,3840]{2,1,0:T(8,128)(2,1)}, u32[]{:S(2)}, u32[]{:S(2)}) %collective-permute-start.4) | collective-permute-done | bytes 1228832 | tf_op jit(solution)/shard_map/ppermute | solution.py:129
  129.4 10.5 %collective-permute-done.6.refs_6_ = bf16[1,80,3840]{2,1,0:T(8,128)(2,1)} collective-permute-done((bf16[1,80,3840]{2,1,0:T(8,128)(2,1)}, bf16[1,80,3840]{2,1,0:T(8,128)(2,1)}, u32[]{:S(2)}, u32[]{:S(2)}) %collective-permute-start.6) | collective-permute-done | bytes 614432 | tf_op jit(solution)/shard_map/ppermute | solution.py:129
  154.3 10.2 %shard_map.315 = (bf16[128,1280]{1,0:T(8,128)(2,1)S(1)}, bf16[128,1280]{1,0:T(8,128)(2,1)S(1)}, bf16[128,1280]{1,0:T(8,128)(2,1)S(1)}, bf16[128,1280]{1,0:T(8,12...) custom-call(s32[1]{0:T(128)} %bitcast.me_ref, f32[128,1280]{1,0:T(8,128)S(1)} %fusion.resid_ref, ...), custom_call_target="tpu_custom_call" | custom-call | flops 1 | bytes 1 | tf_op jit(solution)/shard_map/pallas_call | solution.py:983
  176.2 11.6 %collective-permute-done.15.refs_6_ = bf16[1,80,3840]{2,1,0:T(8,128)(2,1)} collective-permute-done((bf16[1,80,3840]{2,1,0:T(8,128)(2,1)}, bf16[1,80,3840]{2,1,0:T(8,128)(2,1)}, u32[]{:S(2)}, u32[]{:S(2)}) %collective-permute-start.15) | collective-permute-done | bytes 614432 | tf_op jit(solution)/shard_map/ppermute | solution.py:129
  187.8 3.0 collective-permute-done.16.refs_8_
  193.8 7.0 %shard_map.316 = (f32[128,1280]{1,0:T(8,128)S(1)}, f32[128,1280]{1,0:T(8,128)S(1)}, bf16[128,1280]{1,0:T(8,128)(2,1)}, f32[128,1280]{1,0:T(8,128)S(1)}) custom-call(s32[1]{0:T(128)} %bitcast.me_ref, f32[128,1280]{1,0:T(8,128)S(1)} %fusion.resid_ref, bf16[128,1280]{1,0:T(8,128)(2,1)S(1)} %copy-done.47, f32[1,1280]{1,0:T(1,128)S(1)} %get-tuple-element.725.gain_ref, ...), custom_call_target="tpu_custom_call" | custom-call | flops 1 | bytes 1 | tf_op jit(solution)/shard_map/pallas_call | solution.py:983
  203.4 10.4 %collective-permute-done.22.refs_2_ = bf16[1,160,3840]{2,1,0:T(8,128)(2,1)S(1)} collective-permute-done((bf16[1,160,3840]{2,1,0:T(8,128)(2,1)}, bf16[1,160,3840]{2,1,0:T(8,128)(2,1)S(1)}, u32[]{:S(2)}, u32[]{:S(2)}) %collective-permute-start.22) | collective-permute-done | bytes 1228832 | tf_op jit(solution)/shard_map/ppermute | solution.py:129
  213.7 2.6 collective-permute-done.23.refs_4_
  221.7 12.7 %collective-permute-done.24.refs_6_ = bf16[1,80,3840]{2,1,0:T(8,128)(2,1)S(1)} collective-permute-done((bf16[1,80,3840]{2,1,0:T(8,128)(2,1)S(1)}, bf16[1,80,3840]{2,1,0:T(8,128)(2,1)S(1)}, u32[]{:S(2)}, u32[]{:S(2)}) %collective-permute-start.24) | collective-permute-done | bytes 614432 | tf_op jit(solution)/shard_map/ppermute | solution.py:129
  241.1 4.1 all-to-all-start
  248.9 10.6 %shard_map.317 = (bf16[128,1280]{1,0:T(8,128)(2,1)}, bf16[128,1280]{1,0:T(8,128)(2,1)S(1)}, bf16[128,1280]{1,0:T(8,128)(2,1)S(1)}, bf16[128,1280]{1,0:T(8,128)(2...) custom-call(s32[1]{0:T(128)} %bitcast.me_ref, f32[128,1280]{1,0:T(8,128)S(1)} %copy-done.7, ...), custom_call_target="tpu_custom_call" | custom-call | flops 1 | bytes 1 | tf_op jit(solution)/shard_map/pallas_call | solution.py:983
  279.2 6.5 %shard_map.318 = (f32[128,1280]{1,0:T(8,128)S(1)}, f32[128,1280]{1,0:T(8,128)S(1)}, bf16[128,1280]{1,0:T(8,128)(2,1)S(1)}, f32[128,1280]{1,0:T(8,128)S(1)}) custom-call(s32[1]{0:T(128)} %bitcast.me_ref, f32[128,1280]{1,0:T(8,128)S(1)} %copy-done.8, bf16[128,1280]{1,0:T(8,128)(2,1)S(1)} %copy-done.50, f32[1,1280]{1,0:T(1,128)S(1)} %get-tuple-element.723.gain_ref, ...), custom_call_target="tpu_custom_call" | custom-call | flops 1 | bytes 1 | tf_op jit(solution)/shard_map/pallas_call | solution.py:983
  290.3 11.3 %shard_map.319 = (bf16[128,1280]{1,0:T(8,128)(2,1)S(1)}, bf16[4,128,320]{2,1,0:T(8,128)(2,1)S(1)}, bf16[128,1280]{1,0:T(8,128)(2,1)S(1)}, f32[128,1280]{1,0:T(8,128)S(1)}, f32[1,1280]{1,0:T(1,128)S(1)}) custom-call(s32[1]{0:T(128)} %bitcast.me_ref, bf16[128,1280]{1,0:T(8,128)(2,1)S(1)} %convert_element_type.630.top_ref.refs_0_.refs_1_, ...), custom_call_target="tpu_custom_call" | custom-call | flops 1 | bytes 1 | tf_op jit(solution)/shard_map/pallas_call | solution.py:505
  304.5 6.0 shard_map.320
  313.7 10.5 %shard_map.321 = (f32[128,1280]{1,0:T(8,128)S(1)}, bf16[128,1280]{1,0:T(8,128)(2,1)S(1)}, bf16[128,1280]{1,0:T(8,128)(2,1)S(1)}, bf16[128,1280]{1,0:T(8,128)(2,1...) custom-call(s32[1]{0:T(128)} %bitcast.me_ref, ...), custom_call_target="tpu_custom_call" | custom-call | flops 1 | bytes 1 | tf_op jit(solution)/shard_map/pallas_call | solution.py:983
  328.1 11.8 %collective-permute-done.55 = bf16[2,3,160,640]{3,2,1,0:T(8,128)(2,1)} collective-permute-done((bf16[2,3,160,640]{3,2,1,0:T(8,128)(2,1)S(1)}, bf16[2,3,160,640]{3,2,1,0:T(8,128)(2,1)}, u32[]{:S(2)}, u32[]{:S(2)}) %collective-permute-start.55) | collective-permute-done | bytes 1228832 | tf_op jit(solution)/shard_map/ppermute | solution.py:129
  344.4 7.2 %shard_map.322 = (bf16[2,3,160,640]{3,2,1,0:T(8,128)(2,1)}, bf16[2,3,160,640]{3,2,1,0:T(8,128)(2,1)}, bf16[2,3,160,640]{3,2,1,0:T(8,128)(2,1)S(1)}, bf16[3,160,1280]{2,1,0:T(8,128)(2,1)S(1)}) custom-call(s32[1]{0:T(128)} %bitcast.me_ref, bf16[128,1280]{1,0:T(8,128)(2,1)S(1)} %copy-done.51, bf16[128,1280]{1,0:T(8,128)(2,1)S(1)} %copy-done.120, ...), custom_call_target="tpu_custom_call" | custom-call | flops 1 | bytes 1 | tf_op jit(solution)/shard_map/pallas_call | solution.py:302
  353.7 3.9 collective-permute-done.57
  362.8 10.7 %shard_map.323 = (f32[128,1280]{1,0:T(8,128)S(1)}, bf16[128,3840]{1,0:T(8,128)(2,1)S(1)}, f32[1,1280]{1,0:T(1,128)S(1)}) custom-call(s32[1]{0:T(128)} %bitcast.me_ref, f32[128,1280]{1,0:T(8,128)S(1)} %get-tuple-element.409.grad_middle_ref, bf16[128,1280]{1,0:T(8,128)(2,1)S(1)} %copy-done.122, f32[128,1280]{1,0:T(8,128)S(1)} %copy-done.9, ...), custom_call_target="tpu_custom_call" | custom-call | flops 1 | bytes 1 | tf_op jit(solution)/shard_map/pallas_call | solution.py:983
  375.0 10.5 %shard_map.324 = (f32[128,1280]{1,0:T(8,128)S(1)}, bf16[128,1280]{1,0:T(8,128)(2,1)S(1)}, bf16[128,1280]{1,0:T(8,128)(2,1)S(1)}, bf16[128,1280]{1,0:T(8,128)(2,1...) custom-call(s32[1]{0:T(128)} %bitcast.me_ref, ...), custom_call_target="tpu_custom_call" | custom-call | flops 1 | bytes 1 | tf_op jit(solution)/shard_map/pallas_call | solution.py:983
  391.0 2.4 fusion.20
  394.7 4.2 reshape.508
  398.9 2.7 copy.172
  406.5 7.2 %shard_map.325 = (bf16[2,1,160,1920]{3,2,1,0:T(8,128)(2,1)}, bf16[2,1,160,1920]{3,2,1,0:T(8,128)(2,1)}, bf16[2,1,160,1920]{3,2,1,0:T(8,128)(2,1)S(1)}, bf16[1,160,3840]{2,1,0:T(8,128)(2,1)S(1)}) custom-call(s32[1]{0:T(128)} %bitcast.me_ref, bf16[128,1280]{1,0:T(8,128)(2,1)} %get-tuple-element.449.refs_0_, bf16[128,3840]{1,0:T(8,128)(2,1)S(1)} %copy-done.65, ...), custom_call_target="tpu_custom_call" | custom-call | flops 1 | bytes 1 | tf_op jit(solution)/shard_map/pallas_call | solution.py:302
  416.0 3.8 collective-permute-done.69
  423.4 10.8 %shard_map.326 = (f32[128,1280]{1,0:T(8,128)S(1)}, bf16[128,3840]{1,0:T(8,128)(2,1)}, f32[1,1280]{1,0:T(1,128)S(1)}) custom-call(s32[1]{0:T(128)} %bitcast.me_ref, f32[128,1280]{1,0:T(8,128)S(1)} %copy-done.69, bf16[128,1280]{1,0:T(8,128)(2,1)S(1)} %copy-done.92, f32[128,1280]{1,0:T(8,128)S(1)} %fusion.resid_ref, bf16[128,1280]{1,0:T(8,128)(2,1)S(1)} %copy-done.86, ...), custom_call_target="tpu_custom_call" | custom-call | flops 1 | bytes 1 | tf_op jit(solution)/shard_map/pallas_call | solution.py:983
  434.5 2.6 shard_map.327
  444.3 4.8 collective-permute-done.78
  454.5 2.7 shard_map.328
  459.6 6.8 %shard_map.329 = (bf16[2,3,160,640]{3,2,1,0:T(8,128)(2,1)S(1)}, bf16[2,3,160,640]{3,2,1,0:T(8,128)(2,1)S(1)}, bf16[2,3,160,640]{3,2,1,0:T(8,128)(2,1)S(1)}, bf16[3,160,1280]{2,1,0:T(8,128)(2,1)S(1)}) custom-call(s32[1]{0:T(128)} %bitcast.me_ref, bf16[128,1280]{1,0:T(8,128)(2,1)S(1)} %copy-done.48, bf16[128,1280]{1,0:T(8,128)(2,1)} %get-tuple-element.517.refs_1_, ...), custom_call_target="tpu_custom_call" | custom-call | flops 1 | bytes 1 | tf_op jit(solution)/shard_map/pallas_call | solution.py:302
  466.5 2.7 fusion.12
  478.8 22.6 %collective-permute-done.86 = bf16[2,3,160,640]{3,2,1,0:T(8,128)(2,1)} collective-permute-done((bf16[2,3,160,640]{3,2,1,0:T(8,128)(2,1)}, bf16[2,3,160,640]{3,2,1,0:T(8,128)(2,1)}, u32[]{:S(2)}, u32[]{:S(2)}) %collective-permute-start.86) | collective-permute-done | bytes 1228832 | tf_op jit(solution)/shard_map/ppermute | solution.py:129
  502.5 2.6 fusion.29
  507.0 6.0 collective-permute-done.84
  517.8 5.1 all-to-all-start.1
  522.9 7.6 %shard_map.330 = (bf16[2,1,160,1920]{3,2,1,0:T(8,128)(2,1)}, bf16[2,1,160,1920]{3,2,1,0:T(8,128)(2,1)}, bf16[2,1,160,1920]{3,2,1,0:T(8,128)(2,1)S(1)}, bf16[1,160,3840]{2,1,0:T(8,128)(2,1)S(1)}) custom-call(s32[1]{0:T(128)} %bitcast.me_ref, bf16[128,1280]{1,0:T(8,128)(2,1)S(1)} %copy-done.127, bf16[128,3840]{1,0:T(8,128)(2,1)} %get-tuple-element.552.refs_1_, ...), custom_call_target="tpu_custom_call" | custom-call | flops 1 | bytes 1 | tf_op jit(solution)/shard_map/pallas_call | solution.py:302
  535.6 5.1 all-to-all-start.2
  546.0 4.7 all-to-all-done.2
  551.6 3.5 all-to-all-start.3
  555.2 9.7 %collective-permute-done.99 = bf16[2,1,160,1920]{3,2,1,0:T(8,128)(2,1)} collective-permute-done((bf16[2,1,160,1920]{3,2,1,0:T(8,128)(2,1)}, bf16[2,1,160,1920]{3,2,1,0:T(8,128)(2,1)}, u32[]{:S(2)}, u32[]{:S(2)}) %collective-permute-start.99) | collective-permute-done | bytes 1228832 | tf_op jit(solution)/shard_map/ppermute | solution.py:129
  565.7 2.6 fusion.30
  574.9 10.6 %collective-permute-done.101 = bf16[1,160,1920]{2,1,0:T(8,128)(2,1)} collective-permute-done((bf16[1,160,1920]{2,1,0:T(8,128)(2,1)}, bf16[1,160,1920]{2,1,0:T(8,128)(2,1)}, u32[]{:S(2)}, u32[]{:S(2)}) %collective-permute-start.101) | collective-permute-done | bytes 614432 | tf_op jit(solution)/shard_map/ppermute | solution.py:129
  589.9 5.0 all-to-all-start.4
  597.8 3.4 fusion.50
  614.0 6.8 %shard_map.331 = (f32[32,40,1280]{2,1,0:T(8,128)}, f32[32,8,1280]{2,1,0:T(8,128)S(1)}) custom-call(s32[1]{0:T(128)} %bitcast.me_ref, bf16[1,192,1280]{2,1,0:T(8,128)(2,1)S(1)} %bitcast.180, bf16[1,192,1280]{2,1,0:T(8,128)(2,1)S(1)} %collective-permute-done.90.refs_1_, bf16[1,192,1280]{2,1,0:T(8,128)(2,1)S(1)} %collective-permute-done.91.refs_2_, ...), custom_call_target="tpu_custom_call" | custom-call | flops 1 | bytes 1 | tf_op jit(solution)/shard_map/pallas_call | solution.py:741
  (696 shorter events, 221.1 us)
Async XLA Ops:
  7.2 37.7 %all-gather.10.cloned.1.call-start = ((), (), s32[]{:S(2)}) async-start(), calls=%async_computation.10 | async-start | bytes 1587200 | tf_op jit(solution)/shard_map/all_gather | solution.py:214
  10.1 67.3 %all-gather.8.cloned.1.call-start = ((), (), s32[]{:S(2)}) async-start(), calls=%async_computation.9 | async-start | bytes 1536000 | tf_op jit(solution)/shard_map/all_gather | solution.py:214
  12.3 108.5 %all-gather.12.cloned.1.call-start = ((), (), s32[]{:S(2)}) async-start(), calls=%async_computation.11 | async-start | bytes 1536000 | tf_op jit(solution)/shard_map/all_gather | solution.py:214
  44.9 32.5 %collective-permute-start = (bf16[1,160,3968]{2,1,0:T(8,128)(2,1)}, bf16[1,160,3968]{2,1,0:T(8,128)(2,1)S(1)}, u32[]{:S(2)}, u32[]{:S(2)}) collective-permute-start(bf16[1,160,3968]{2,1,0:T(8,128)(2,1)} %bitcast.20.refs_0_), channel_id=1, source_target_pairs={{0,8},{4,12},{8,0},{12,4},{16,24},{20,28},{24,16},{28,20},{1,9},{5... | collective-permute-start | bytes 3809288 | tf_op jit(solution)/shard_map/ppermute | solution.py:129
  46.4 31.0 %collective-permute-start.1 = (bf16[1,160,3968]{2,1,0:T(8,128)(2,1)}, bf16[1,160,3968]{2,1,0:T(8,128)(2,1)S(1)}, u32[]{:S(2)}, u32[]{:S(2)}) collective-permute-start(bf16[1,160,3968]{2,1,0:T(8,128)(2,1)} %bitcast.20.refs_0_), channel_id=1, source_target_pairs={{0,16},{4,20},{8,24},{12,28},{16,0},{20,4},{24,8},{28,12},{1,17},{... | collective-permute-start | bytes 3809288 | tf_op jit(solution)/shard_map/ppermute | solution.py:129
  77.5 91.3 %all-gather.14.cloned.1.call-start = ((), (), s32[]{:S(2)}) async-start(), calls=%async_computation.12 | async-start | bytes 1536000 | tf_op jit(solution)/shard_map/all_gather | solution.py:214
  80.7 38.8 %collective-permute-start.4 = (bf16[1,160,3840]{2,1,0:T(8,128)(2,1)S(1)}, bf16[1,160,3840]{2,1,0:T(8,128)(2,1)}, u32[]{:S(2)}, u32[]{:S(2)}) collective-permute-start(bf16[1,160,3840]{2,1,0:T(8,128)(2,1)S(1)} %bitcast.168), channel_id=1, source_target_pairs={{0,8},{4,12},{8,0},{12,4},{16,24},{20,28},{24,16},{28,20},{1,9},{5... | collective-permute-start | bytes 3686408 | tf_op jit(solution)/shard_map/ppermute | solution.py:129
  81.3 39.6 %collective-permute-start.5 = (bf16[1,160,3840]{2,1,0:T(8,128)(2,1)S(1)}, bf16[1,160,3840]{2,1,0:T(8,128)(2,1)}, u32[]{:S(2)}, u32[]{:S(2)}) collective-permute-start(bf16[1,160,3840]{2,1,0:T(8,128)(2,1)S(1)} %bitcast.169), channel_id=1, source_target_pairs={{0,16},{4,20},{8,24},{12,28},{16,0},{20,4},{24,8},{28,12},{1,17},{... | collective-permute-start | bytes 3686408 | tf_op jit(solution)/shard_map/ppermute | solution.py:129
  82.6 44.7 %collective-permute-start.8 = (bf16[1,160,3968]{2,1,0:T(8,128)(2,1)}, bf16[1,160,3968]{2,1,0:T(8,128)(2,1)}, u32[]{:S(2)}, u32[]{:S(2)}) collective-permute-start(bf16[1,160,3968]{2,1,0:T(8,128)(2,1)} %bitcast.20.refs_0_), channel_id=1, source_target_pairs={{0,4},{4,0},{8,12},{12,8},{16,20},{20,16},{24,28},{28,24},{1,5},{5... | collective-permute-start | bytes 3809288 | tf_op jit(solution)/shard_map/ppermute | solution.py:129
  94.9 32.5 %collective-permute-start.9 = (bf16[1,160,3968]{2,1,0:T(8,128)(2,1)S(1)}, bf16[1,160,3968]{2,1,0:T(8,128)(2,1)}, u32[]{:S(2)}, u32[]{:S(2)}) collective-permute-start(bf16[1,160,3968]{2,1,0:T(8,128)(2,1)S(1)} %collective-permute-done.refs_2_), channel_id=1, source_target_pairs={{0,4},{4,0},{8,12},{12,8},{16,20},{20,16},{24,28},{28,24},{1,5},{5... | collective-permute-start | bytes 3809288 | tf_op jit(solution)/shard_map/ppermute | solution.py:129
  96.5 31.4 %collective-permute-start.10 = (bf16[1,160,3968]{2,1,0:T(8,128)(2,1)S(1)}, bf16[1,160,3968]{2,1,0:T(8,128)(2,1)}, u32[]{:S(2)}, u32[]{:S(2)}) collective-permute-start(bf16[1,160,3968]{2,1,0:T(8,128)(2,1)S(1)} %collective-permute-done.1.refs_4_), channel_id=1, source_target_pairs={{0,4},{4,0},{8,12},{12,8},{16,20},{20,16},{24,28},{28,24},{1,5},{5... | collective-permute-start | bytes 3809288 | tf_op jit(solution)/shard_map/ppermute | solution.py:129
  123.3 93.0 %all-gather.16.cloned.1.call-start = ((), (), s32[]{:S(2)}) async-start(), calls=%async_computation.13 | async-start | bytes 1638400 | tf_op jit(solution)/shard_map/all_gather | solution.py:1275
  127.9 40.9 %collective-permute-start.13 = (bf16[1,160,3840]{2,1,0:T(8,128)(2,1)}, bf16[1,160,3840]{2,1,0:T(8,128)(2,1)}, u32[]{:S(2)}, u32[]{:S(2)}) collective-permute-start(bf16[1,160,3840]{2,1,0:T(8,128)(2,1)} %bitcast.172), channel_id=1, source_target_pairs={{0,8},{4,12},{8,0},{12,4},{16,24},{20,28},{24,16},{28,20},{1,9},{5... | collective-permute-start | bytes 3686408 | tf_op jit(solution)/shard_map/ppermute | solution.py:129
  139.9 28.9 %collective-permute-start.14 = (bf16[1,160,3840]{2,1,0:T(8,128)(2,1)}, bf16[1,160,3840]{2,1,0:T(8,128)(2,1)}, u32[]{:S(2)}, u32[]{:S(2)}) collective-permute-start(bf16[1,160,3840]{2,1,0:T(8,128)(2,1)} %bitcast.173), channel_id=1, source_target_pairs={{0,16},{4,20},{8,24},{12,28},{16,0},{20,4},{24,8},{28,12},{1,17},{... | collective-permute-start | bytes 3686408 | tf_op jit(solution)/shard_map/ppermute | solution.py:129
  142.4 33.0 %collective-permute-start.17 = (bf16[1,160,3840]{2,1,0:T(8,128)(2,1)}, bf16[1,160,3840]{2,1,0:T(8,128)(2,1)}, u32[]{:S(2)}, u32[]{:S(2)}) collective-permute-start(bf16[1,160,3840]{2,1,0:T(8,128)(2,1)} %bitcast.167), channel_id=1, source_target_pairs={{0,4},{4,0},{8,12},{12,8},{16,20},{20,16},{24,28},{28,24},{1,5},{5... | collective-permute-start | bytes 3686408 | tf_op jit(solution)/shard_map/ppermute | solution.py:129
  144.6 30.8 %collective-permute-start.18 = (bf16[1,160,3840]{2,1,0:T(8,128)(2,1)}, bf16[1,160,3840]{2,1,0:T(8,128)(2,1)}, u32[]{:S(2)}, u32[]{:S(2)}) collective-permute-start(bf16[1,160,3840]{2,1,0:T(8,128)(2,1)} %collective-permute-done.4.refs_2_), channel_id=1, source_target_pairs={{0,4},{4,0},{8,12},{12,8},{16,20},{20,16},{24,28},{28,24},{1,5},{5... | collective-permute-start | bytes 3686408 | tf_op jit(solution)/shard_map/ppermute | solution.py:129
  145.2 30.4 %collective-permute-start.19 = (bf16[1,160,3840]{2,1,0:T(8,128)(2,1)}, bf16[1,160,3840]{2,1,0:T(8,128)(2,1)}, u32[]{:S(2)}, u32[]{:S(2)}) collective-permute-start(bf16[1,160,3840]{2,1,0:T(8,128)(2,1)} %collective-permute-done.5.refs_4_), channel_id=1, source_target_pairs={{0,4},{4,0},{8,12},{12,8},{16,20},{20,16},{24,28},{28,24},{1,5},{5... | collective-permute-start | bytes 3686408 | tf_op jit(solution)/shard_map/ppermute | solution.py:129
  175.5 38.3 %collective-permute-start.22 = (bf16[1,160,3840]{2,1,0:T(8,128)(2,1)}, bf16[1,160,3840]{2,1,0:T(8,128)(2,1)S(1)}, u32[]{:S(2)}, u32[]{:S(2)}) collective-permute-start(bf16[1,160,3840]{2,1,0:T(8,128)(2,1)} %bitcast.26.refs_0_), channel_id=1, source_target_pairs={{0,8},{4,12},{8,0},{12,4},{16,24},{20,28},{24,16},{28,20},{1,9},{5... | collective-permute-start | bytes 3686408 | tf_op jit(solution)/shard_map/ppermute | solution.py:129
  175.6 40.7 %collective-permute-start.23 = (bf16[1,160,3840]{2,1,0:T(8,128)(2,1)}, bf16[1,160,3840]{2,1,0:T(8,128)(2,1)}, u32[]{:S(2)}, u32[]{:S(2)}) collective-permute-start(bf16[1,160,3840]{2,1,0:T(8,128)(2,1)} %bitcast.26.refs_0_), channel_id=1, source_target_pairs={{0,16},{4,20},{8,24},{12,28},{16,0},{20,4},{24,8},{28,12},{1,17},{... | collective-permute-start | bytes 3686408 | tf_op jit(solution)/shard_map/ppermute | solution.py:129
  190.8 28.6 %collective-permute-start.26 = (bf16[1,160,3840]{2,1,0:T(8,128)(2,1)}, bf16[1,160,3840]{2,1,0:T(8,128)(2,1)}, u32[]{:S(2)}, u32[]{:S(2)}) collective-permute-start(bf16[1,160,3840]{2,1,0:T(8,128)(2,1)} %bitcast.174), channel_id=1, source_target_pairs={{0,4},{4,0},{8,12},{12,8},{16,20},{20,16},{24,28},{28,24},{1,5},{5... | collective-permute-start | bytes 3686408 | tf_op jit(solution)/shard_map/ppermute | solution.py:129
  190.8 28.6 %collective-permute-start.27 = (bf16[1,160,3840]{2,1,0:T(8,128)(2,1)}, bf16[1,160,3840]{2,1,0:T(8,128)(2,1)}, u32[]{:S(2)}, u32[]{:S(2)}) collective-permute-start(bf16[1,160,3840]{2,1,0:T(8,128)(2,1)} %collective-permute-done.13.refs_2_), channel_id=1, source_target_pairs={{0,4},{4,0},{8,12},{12,8},{16,20},{20,16},{24,28},{28,24},{1,5},{5... | collective-permute-start | bytes 3686408 | tf_op jit(solution)/shard_map/ppermute | solution.py:129
  191.3 28.6 %collective-permute-start.28 = (bf16[1,160,3840]{2,1,0:T(8,128)(2,1)}, bf16[1,160,3840]{2,1,0:T(8,128)(2,1)}, u32[]{:S(2)}, u32[]{:S(2)}) collective-permute-start(bf16[1,160,3840]{2,1,0:T(8,128)(2,1)} %collective-permute-done.14.refs_4_), channel_id=1, source_target_pairs={{0,4},{4,0},{8,12},{12,8},{16,20},{20,16},{24,28},{28,24},{1,5},{5... | collective-permute-start | bytes 3686408 | tf_op jit(solution)/shard_map/ppermute | solution.py:129
  219.9 43.1 %collective-permute-start.31 = (bf16[4,160,960]{2,1,0:T(8,128)(2,1)}, bf16[4,160,960]{2,1,0:T(8,128)(2,1)}, u32[]{:S(2)}, u32[]{:S(2)}) collective-permute-start(bf16[4,160,960]{2,1,0:T(8,128)(2,1)} %all-gather.16.cloned.1.call-done.refs_0_), channel_id=1, source_target_pairs={{0,8},{4,12},{8,0},{12,4},{16,24},{20,28},{24,16},{28,20},{1,9},{5... | collective-permute-start | bytes 3686408 | tf_op jit(solution)/shard_map/ppermute | solution.py:129
  234.3 28.7 %collective-permute-start.32 = (bf16[4,160,960]{2,1,0:T(8,128)(2,1)}, bf16[4,160,960]{2,1,0:T(8,128)(2,1)}, u32[]{:S(2)}, u32[]{:S(2)}) collective-permute-start(bf16[4,160,960]{2,1,0:T(8,128)(2,1)} %all-gather.16.cloned.1.call-done.refs_0_), channel_id=1, source_target_pairs={{0,16},{4,20},{8,24},{12,28},{16,0},{20,4},{24,8},{28,12},{1,17},{... | collective-permute-start | bytes 3686408 | tf_op jit(solution)/shard_map/ppermute | solution.py:129
  235.9 31.7 %collective-permute-start.35 = (bf16[1,160,3840]{2,1,0:T(8,128)(2,1)}, bf16[1,160,3840]{2,1,0:T(8,128)(2,1)}, u32[]{:S(2)}, u32[]{:S(2)}) collective-permute-start(bf16[1,160,3840]{2,1,0:T(8,128)(2,1)} %bitcast.26.refs_0_), channel_id=1, source_target_pairs={{0,4},{4,0},{8,12},{12,8},{16,20},{20,16},{24,28},{28,24},{1,5},{5... | collective-permute-start | bytes 3686408 | tf_op jit(solution)/shard_map/ppermute | solution.py:129
  236.9 31.0 %collective-permute-start.36 = (bf16[1,160,3840]{2,1,0:T(8,128)(2,1)S(1)}, bf16[1,160,3840]{2,1,0:T(8,128)(2,1)}, u32[]{:S(2)}, u32[]{:S(2)}) collective-permute-start(bf16[1,160,3840]{2,1,0:T(8,128)(2,1)S(1)} %collective-permute-done.22.refs_2_), channel_id=1, source_target_pairs={{0,4},{4,0},{8,12},{12,8},{16,20},{20,16},{24,28},{28,24},{1,5},{5... | collective-permute-start | bytes 3686408 | tf_op jit(solution)/shard_map/ppermute | solution.py:129
  239.2 29.8 %collective-permute-start.37 = (bf16[1,160,3840]{2,1,0:T(8,128)(2,1)}, bf16[1,160,3840]{2,1,0:T(8,128)(2,1)}, u32[]{:S(2)}, u32[]{:S(2)}) collective-permute-start(bf16[1,160,3840]{2,1,0:T(8,128)(2,1)} %collective-permute-done.23.refs_4_), channel_id=1, source_target_pairs={{0,4},{4,0},{8,12},{12,8},{16,20},{20,16},{24,28},{28,24},{1,5},{5... | collective-permute-start | bytes 3686408 | tf_op jit(solution)/shard_map/ppermute | solution.py:129
  245.2 205.0 %reduce-scatter.9.cloned.1.call-start = ((), (), s32[]{:S(2)}) async-start(), calls=%async_computation.14 | async-start | bytes 1843200 | tf_op jit(solution)/shard_map/reduce_scatter | solution.py:389
  310.5 29.5 %collective-permute-start.55 = (bf16[2,3,160,640]{3,2,1,0:T(8,128)(2,1)S(1)}, bf16[2,3,160,640]{3,2,1,0:T(8,128)(2,1)}, u32[]{:S(2)}, u32[]{:S(2)}) collective-permute-start(bf16[2,3,160,640]{3,2,1,0:T(8,128)(2,1)S(1)} %get-tuple-element.383), channel_id=1, source_target_pairs={{0,8},{4,12},{8,0},{12,4},{16,24},{20,28},{24,16},{28,20},{1,9},{5... | collective-permute-start | bytes 3686408 | tf_op jit(solution)/shard_map/ppermute | solution.py:129
  311.8 29.1 %collective-permute-start.56 = (bf16[2,3,160,640]{3,2,1,0:T(8,128)(2,1)S(1)}, bf16[2,3,160,640]{3,2,1,0:T(8,128)(2,1)}, u32[]{:S(2)}, u32[]{:S(2)}) collective-permute-start(bf16[2,3,160,640]{3,2,1,0:T(8,128)(2,1)S(1)} %get-tuple-element.384), channel_id=1, source_target_pairs={{0,16},{4,20},{8,24},{12,28},{16,0},{20,4},{24,8},{28,12},{1,17},{... | collective-permute-start | bytes 3686408 | tf_op jit(solution)/shard_map/ppermute | solution.py:129
  344.4 29.8 %collective-permute-start.61 = (bf16[128,1280]{1,0:T(8,128)(2,1)S(1)}, bf16[128,1280]{1,0:T(8,128)(2,1)S(1)}, u32[]{:S(2)}, u32[]{:S(2)}) collective-permute-start(bf16[128,1280]{1,0:T(8,128)(2,1)S(1)} %copy-done.48), channel_id=1, source_target_pairs={{0,4},{4,0},{8,12},{12,8},{16,20},{20,16},{24,28},{28,24},{1,5},{5... | collective-permute-start | bytes 983048 | tf_op jit(solution)/shard_map/ppermute | solution.py:129
  358.8 32.1 %collective-permute-start.67 = (bf16[2,3,160,640]{3,2,1,0:T(8,128)(2,1)}, bf16[2,3,160,640]{3,2,1,0:T(8,128)(2,1)}, u32[]{:S(2)}, u32[]{:S(2)}) collective-permute-start(bf16[2,3,160,640]{3,2,1,0:T(8,128)(2,1)} %get-tuple-element.426), channel_id=1, source_target_pairs={{0,8},{4,12},{8,0},{12,4},{16,24},{20,28},{24,16},{28,20},{1,9},{5... | collective-permute-start | bytes 3686408 | tf_op jit(solution)/shard_map/ppermute | solution.py:129
  359.4 31.5 %collective-permute-start.68 = (bf16[2,3,160,640]{3,2,1,0:T(8,128)(2,1)}, bf16[2,3,160,640]{3,2,1,0:T(8,128)(2,1)}, u32[]{:S(2)}, u32[]{:S(2)}) collective-permute-start(bf16[2,3,160,640]{3,2,1,0:T(8,128)(2,1)} %get-tuple-element.427), channel_id=1, source_target_pairs={{0,16},{4,20},{8,24},{12,28},{16,0},{20,4},{24,8},{28,12},{1,17},{... | collective-permute-start | bytes 3686408 | tf_op jit(solution)/shard_map/ppermute | solution.py:129
  401.6 73.6 %reduce-scatter.13.cloned.1.call-start = ((), (), s32[]{:S(2)}) async-start(), calls=%async_computation.17 | async-start | bytes 1536000
  420.7 28.3 %collective-permute-start.78 = (bf16[2,1,160,1920]{3,2,1,0:T(8,128)(2,1)}, bf16[2,1,160,1920]{3,2,1,0:T(8,128)(2,1)}, u32[]{:S(2)}, u32[]{:S(2)}) collective-permute-start(bf16[2,1,160,1920]{3,2,1,0:T(8,128)(2,1)} %get-tuple-element.490), channel_id=1, source_target_pairs={{0,8},{4,12},{8,0},{12,4},{16,24},{20,28},{24,16},{28,20},{1,9},{5... | collective-permute-start | bytes 3686408 | tf_op jit(solution)/shard_map/ppermute | solution.py:129
  422.1 28.1 %collective-permute-start.79 = (bf16[2,1,160,1920]{3,2,1,0:T(8,128)(2,1)}, bf16[2,1,160,1920]{3,2,1,0:T(8,128)(2,1)}, u32[]{:S(2)}, u32[]{:S(2)}) collective-permute-start(bf16[2,1,160,1920]{3,2,1,0:T(8,128)(2,1)} %get-tuple-element.491), channel_id=1, source_target_pairs={{0,16},{4,20},{8,24},{12,28},{16,0},{20,4},{24,8},{28,12},{1,17},{... | collective-permute-start | bytes 3686408 | tf_op jit(solution)/shard_map/ppermute | solution.py:129
  444.2 111.0 %reduce-scatter.11.cloned.1.call-start = ((), (), s32[]{:S(2)}) async-start(), calls=%async_computation.15 | async-start | bytes 1536000 | tf_op jit(solution)/shard_map/reduce_scatter | solution.py:367
  470.4 127.5 %all-gather.18.cloned.1.call-start = ((), (), s32[]{:S(2)}) async-start(), calls=%async_computation.16 | async-start | bytes 3317760 | tf_op jit(solution)/shard_map/all_gather | solution.py:396
  471.1 30.3 %collective-permute-start.86 = (bf16[2,3,160,640]{3,2,1,0:T(8,128)(2,1)}, bf16[2,3,160,640]{3,2,1,0:T(8,128)(2,1)}, u32[]{:S(2)}, u32[]{:S(2)}) collective-permute-start(bf16[2,3,160,640]{3,2,1,0:T(8,128)(2,1)} %copy-done.148), channel_id=1, source_target_pairs={{0,8},{4,12},{8,0},{12,4},{16,24},{20,28},{24,16},{28,20},{1,9},{5... | collective-permute-start | bytes 3686408 | tf_op jit(solution)/shard_map/ppermute | solution.py:129
  472.4 30.1 %collective-permute-start.87 = (bf16[2,3,160,640]{3,2,1,0:T(8,128)(2,1)S(1)}, bf16[2,3,160,640]{3,2,1,0:T(8,128)(2,1)}, u32[]{:S(2)}, u32[]{:S(2)}) collective-permute-start(bf16[2,3,160,640]{3,2,1,0:T(8,128)(2,1)S(1)} %copy-done.147), channel_id=1, source_target_pairs={{0,16},{4,20},{8,24},{12,28},{16,0},{20,4},{24,8},{28,12},{1,17},{... | collective-permute-start | bytes 3686408 | tf_op jit(solution)/shard_map/ppermute | solution.py:129
  473.7 39.3 %collective-permute-start.84 = (bf16[2,1,192,640]{3,2,1,0:T(8,128)(2,1)}, bf16[2,1,192,640]{3,2,1,0:T(8,128)(2,1)}, u32[]{:S(2)}, u32[]{:S(2)}) collective-permute-start(bf16[2,1,192,640]{3,2,1,0:T(8,128)(2,1)} %copy-done.151), channel_id=1, source_target_pairs={{0,16},{4,20},{8,24},{12,28},{16,0},{20,4},{24,8},{28,12},{1,17},{... | collective-permute-start | bytes 1474568 | tf_op jit(solution)/shard_map/ppermute | solution.py:129
  474.4 38.6 %collective-permute-start.82 = (bf16[2,1,192,640]{3,2,1,0:T(8,128)(2,1)S(1)}, bf16[2,1,192,640]{3,2,1,0:T(8,128)(2,1)}, u32[]{:S(2)}, u32[]{:S(2)}) collective-permute-start(bf16[2,1,192,640]{3,2,1,0:T(8,128)(2,1)S(1)} %copy-done.150), channel_id=1, source_target_pairs={{0,8},{4,12},{8,0},{12,4},{16,24},{20,28},{24,16},{28,20},{1,9},{5... | collective-permute-start | bytes 1474568 | tf_op jit(solution)/shard_map/ppermute | solution.py:129
  505.1 26.6 %collective-permute-start.88 = (bf16[3,160,640]{2,1,0:T(8,128)(2,1)}, bf16[3,160,640]{2,1,0:T(8,128)(2,1)}, u32[]{:S(2)}, u32[]{:S(2)}) collective-permute-start(bf16[3,160,640]{2,1,0:T(8,128)(2,1)} %get-tuple-element.688), channel_id=1, source_target_pairs={{0,16},{4,20},{8,24},{12,28},{16,0},{20,4},{24,8},{28,12},{1,17},{... | collective-permute-start | bytes 1843208 | tf_op jit(solution)/shard_map/ppermute | solution.py:129
  531.7 33.2 %collective-permute-start.99 = (bf16[2,1,160,1920]{3,2,1,0:T(8,128)(2,1)}, bf16[2,1,160,1920]{3,2,1,0:T(8,128)(2,1)}, u32[]{:S(2)}, u32[]{:S(2)}) collective-permute-start(bf16[2,1,160,1920]{3,2,1,0:T(8,128)(2,1)} %get-tuple-element.566), channel_id=1, source_target_pairs={{0,8},{4,12},{8,0},{12,4},{16,24},{20,28},{24,16},{28,20},{1,9},{5... | collective-permute-start | bytes 3686408 | tf_op jit(solution)/shard_map/ppermute | solution.py:129
  532.4 33.3 %collective-permute-start.100 = (bf16[2,1,160,1920]{3,2,1,0:T(8,128)(2,1)}, bf16[2,1,160,1920]{3,2,1,0:T(8,128)(2,1)}, u32[]{:S(2)}, u32[]{:S(2)}) collective-permute-start(bf16[2,1,160,1920]{3,2,1,0:T(8,128)(2,1)} %get-tuple-element.567), channel_id=1, source_target_pairs={{0,16},{4,20},{8,24},{12,28},{16,0},{20,4},{24,8},{28,12},{1,17},{... | collective-permute-start | bytes 3686408 | tf_op jit(solution)/shard_map/ppermute | solution.py:129
  540.8 67.7 %reduce-scatter.15.cloned.1.call-start = ((), (), s32[]{:S(2)}) async-start(), calls=%async_computation.18 | async-start | bytes 1536000
  573.1 40.9 %collective-permute-start.90 = (bf16[1,192,1280]{2,1,0:T(8,128)(2,1)S(1)}, bf16[1,192,1280]{2,1,0:T(8,128)(2,1)S(1)}, u32[]{:S(2)}, u32[]{:S(2)}) collective-permute-start(bf16[1,192,1280]{2,1,0:T(8,128)(2,1)S(1)} %bitcast.177), channel_id=1, source_target_pairs={{0,4},{4,0},{8,12},{12,8},{16,20},{20,16},{24,28},{28,24},{1,5},{5... | collective-permute-start | bytes 1474568 | tf_op jit(solution)/shard_map/ppermute | solution.py:129
  589.9 33.8 %all-to-all-start.4 = ((bf16[1,4,40,3840]{3,2,0,1:T(8,128)(2,1)}), bf16[1,4,40,3840]{3,2,0,1:T(8,128)(2,1)}, u32[]{:S(2)}, u32[]{:S(2)}) async-start(bf16[1,4,40,3840]{3,2,0,1:T(8,128)(2,1)} %bitcast.64), calls=%async_computation.6 | async-start | bytes 2457600 | tf_op jit(solution)/shard_map/all_to_all | solution.py:379
  (250 other events, 2466.0 us)
Sparse Core Ops, SparseCore 0:
  10.2 34.6 all-gather.9
  47.1 30.3 all-gather.7
  79.6 30.3 all-gather.11
  123.5 31.1 all-gather.13
  172.9 31.6 all-gather.15
  401.7 34.7 reduce-scatter.8
  444.3 30.5 reduce-scatter.12
  477.7 28.8 reduce-scatter.10
  508.7 41.5 all-gather.17
  553.1 31.6 reduce-scatter.14

commit v2 on v1

--- a/solution.py
+++ b/solution.py
@@ -1433,10 +1433,12 @@
     for number in range(stage_count + 1):
         carry, boths = step["carry"], step["boths"]
         parts = {"first": sums[number].first()}
+        if number == 2:
+            finished[0] = sum_columns(sums.pop(0).total())
         if number >= 2:
             finished[number - 1] = sum_group(sums.pop(number - 1).total())
-        if number >= 2:
-            parts["finished"] = finished[number - 2]
+        if number >= 3:
+            parts["finished"] = {n: finished[n] for n in (number - 2, 0)}
         until = number + 1 if number == 0 else number + 2
         while done < min(until, stage_count):
             stage, layer_index = stages[done]
@@ -1450,12 +1452,9 @@
             entry_summed = entry_sums_of_group(entry_chunk.total())
         step = close(**parts)
         sums[number].met = step["first"]
-        if number >= 2:
-            finished[number - 2] = step["finished"]
+        finished.update(step.get("finished", {}))
         carry, boths = step["carry"], step["boths"]
         parts = {"last": sums[number].last()}
-        if number == 1:
-            finished[0] = sum_columns(sums.pop(0).total())
         if number == stage_count - 2:
             if layers[0].fetched:
                 entry_chunk = input_products(me, step["entry"])

time: 639 us -> 664 us (1.039)
  waiting for transfers between devices: 238 us -> 254 us
  starting transfers between devices: 86.4 us -> 93.3 us
    all_to_all x2, waiting for transfers between devices: 4.73 us -> 30.3 us  [sum_group_at_once(): lax.all_to_all(total, 'head', split_axis=axis, concat_axis=axis, tiled=True)]
    ppermute x103, waiting for transfers between devices: 178 us -> 167 us  [swap(): return lax.ppermute(v, 'dp', [(i, i ^ 1 << bit) for i in range(size)])]
    ppermute x103, starting transfers between devices: 62.5 us -> 69.3 us  [swap(): return lax.ppermute(v, 'dp', [(i, i ^ 1 << bit) for i in range(size)])]
    unnamed x378 -> x380, local copies, waits for them, and re-layouts: 69.7 us -> 73.2 us
  transfers between devices with their start and end apart: 118 -> 118, of which waited for: 41 -> 41; matrix products, arithmetic and copies ran while one was open for 14% -> 13% of each run, Pallas kernels for 21% -> 20%
where the time goes in v2:
time: 664 us; the launch traced here: 657 us
  waiting for transfers between devices  254 us (38%)
  Pallas kernels  137 us (21%)
  local copies, waits for them, and re-layouts  110 us (17%)
  starting transfers between devices  93.3 us (14%)
  other arithmetic  44.3 us (7%)
  between operations  16.5 us (2%)
    ppermute x103, waiting for transfers between devices, swap(): return lax.ppermute(v, 'dp', [(i, i ^ 1 << bit) for i in range(size)])  167 us
    pallas_call x8, Pallas kernels, whole_call(): pl.pallas_call(partial(kernel, plan), out_shape=[jax.ShapeDtypeStruct(sha...  76.6 us
    unnamed x380, local copies, waits for them, and re-layouts  73.2 us
    ppermute x103, starting transfers between devices, swap(): return lax.ppermute(v, 'dp', [(i, i ^ 1 << bit) for i in range(size)])  69.3 us
    all_gather x4, waiting for transfers between devices, gather_head(): held = lax.all_gather(own, 'head', axis=0, tiled=True)[None]  53.2 us
    pallas_call x5, Pallas kernels, pair_products(): pl.pallas_call(partial(product_kernel, count, outer), out_shape=[jax.Shap...  34.9 us
    all_to_all x2, waiting for transfers between devices, sum_group_at_once(): lax.all_to_all(total, 'head', split_axis=axis, concat_axis=axis, tiled=True)  30.3 us
    convert_element_type x12, other arithmetic, low_sum(): return total.astype(jnp.bfloat16)  23.4 us
  transfers between devices with their start and end apart: 118, of which 41 were waited for; matrix products, arithmetic and copies ran while one was open for 13% of the time, Pallas kernels for 20%

profile of v2, /device:TPU:0, one launch (start us, length us, event | category | flops | bytes accessed | tf_op | source)
XLA Modules:
  0.0 657.3 jit_solution(3318032257700257698)
XLA Ops:
  17.4 27.5 %all-gather.10.cloned.1.call-done = bf16[160,3968]{1,0:T(8,128)(2,1)} async-done(((bf16[40,3968]{1,0:T(8,128)(2,1)}), bf16[160,3968]{1,0:T(8,128)(2,1)}) %all-gather.10.cloned.1.call-update) | async-done | bytes 1269776 | tf_op jit(solution)/shard_map/all_gather | solution.py:214
  51.8 25.7 %all-gather.8.cloned.1.call-done = bf16[160,3840]{1,0:T(8,128)(2,1)} async-done(((bf16[40,3840]{1,0:T(8,128)(2,1)}), bf16[160,3840]{1,0:T(8,128)(2,1)}) %all-gather.8.cloned.1.call-update) | async-done | bytes 1228816 | tf_op jit(solution)/shard_map/all_gather | solution.py:214
  82.6 12.3 %collective-permute-done.2.refs_6_ = bf16[1,80,3968]{2,1,0:T(8,128)(2,1)S(1)} collective-permute-done((bf16[1,80,3968]{2,1,0:T(8,128)(2,1)S(1)}, bf16[1,80,3968]{2,1,0:T(8,128)(2,1)S(1)}, u32[]{:S(2)}, u32[]{:S(2)}) %collective-permute-start.2) | collective-permute-done | bytes 634912 | tf_op jit(solution)/shard_map/ppermute | solution.py:129
  96.5 23.0 %collective-permute-done.4.refs_2_ = bf16[1,160,3840]{2,1,0:T(8,128)(2,1)} collective-permute-done((bf16[1,160,3840]{2,1,0:T(8,128)(2,1)S(1)}, bf16[1,160,3840]{2,1,0:T(8,128)(2,1)}, u32[]{:S(2)}, u32[]{:S(2)}) %collective-permute-start.4) | collective-permute-done | bytes 1228832 | tf_op jit(solution)/shard_map/ppermute | solution.py:129
  129.2 10.7 %collective-permute-done.6.refs_6_ = bf16[1,80,3840]{2,1,0:T(8,128)(2,1)} collective-permute-done((bf16[1,80,3840]{2,1,0:T(8,128)(2,1)}, bf16[1,80,3840]{2,1,0:T(8,128)(2,1)}, u32[]{:S(2)}, u32[]{:S(2)}) %collective-permute-start.6) | collective-permute-done | bytes 614432 | tf_op jit(solution)/shard_map/ppermute | solution.py:129
  153.8 10.2 %shard_map.315 = (bf16[128,1280]{1,0:T(8,128)(2,1)S(1)}, bf16[128,1280]{1,0:T(8,128)(2,1)S(1)}, bf16[128,1280]{1,0:T(8,128)(2,1)S(1)}, bf16[128,1280]{1,0:T(8,12...) custom-call(s32[1]{0:T(128)} %bitcast.me_ref, f32[128,1280]{1,0:T(8,128)S(1)} %fusion.resid_ref, ...), custom_call_target="tpu_custom_call" | custom-call | flops 1 | bytes 1 | tf_op jit(solution)/shard_map/pallas_call | solution.py:983
  176.0 11.6 %collective-permute-done.15.refs_6_ = bf16[1,80,3840]{2,1,0:T(8,128)(2,1)} collective-permute-done((bf16[1,80,3840]{2,1,0:T(8,128)(2,1)}, bf16[1,80,3840]{2,1,0:T(8,128)(2,1)}, u32[]{:S(2)}, u32[]{:S(2)}) %collective-permute-start.15) | collective-permute-done | bytes 614432 | tf_op jit(solution)/shard_map/ppermute | solution.py:129
  187.6 3.0 collective-permute-done.16.refs_8_
  193.6 7.0 %shard_map.316 = (f32[128,1280]{1,0:T(8,128)S(1)}, f32[128,1280]{1,0:T(8,128)S(1)}, bf16[128,1280]{1,0:T(8,128)(2,1)}, f32[128,1280]{1,0:T(8,128)S(1)}) custom-call(s32[1]{0:T(128)} %bitcast.me_ref, f32[128,1280]{1,0:T(8,128)S(1)} %fusion.resid_ref, bf16[128,1280]{1,0:T(8,128)(2,1)S(1)} %copy-done.49, f32[1,1280]{1,0:T(1,128)S(1)} %get-tuple-element.729.gain_ref, ...), custom_call_target="tpu_custom_call" | custom-call | flops 1 | bytes 1 | tf_op jit(solution)/shard_map/pallas_call | solution.py:983
  203.2 10.4 %collective-permute-done.22.refs_2_ = bf16[1,160,3840]{2,1,0:T(8,128)(2,1)S(1)} collective-permute-done((bf16[1,160,3840]{2,1,0:T(8,128)(2,1)}, bf16[1,160,3840]{2,1,0:T(8,128)(2,1)S(1)}, u32[]{:S(2)}, u32[]{:S(2)}) %collective-permute-start.22) | collective-permute-done | bytes 1228832 | tf_op jit(solution)/shard_map/ppermute | solution.py:129
  213.6 2.6 collective-permute-done.23.refs_4_
  221.5 12.7 %collective-permute-done.24.refs_6_ = bf16[1,80,3840]{2,1,0:T(8,128)(2,1)S(1)} collective-permute-done((bf16[1,80,3840]{2,1,0:T(8,128)(2,1)S(1)}, bf16[1,80,3840]{2,1,0:T(8,128)(2,1)S(1)}, u32[]{:S(2)}, u32[]{:S(2)}) %collective-permute-start.24) | collective-permute-done | bytes 614432 | tf_op jit(solution)/shard_map/ppermute | solution.py:129
  240.9 4.1 all-to-all-start
  249.1 10.6 %shard_map.317 = (bf16[128,1280]{1,0:T(8,128)(2,1)}, bf16[128,1280]{1,0:T(8,128)(2,1)S(1)}, bf16[128,1280]{1,0:T(8,128)(2,1)S(1)}, bf16[128,1280]{1,0:T(8,128)(2...) custom-call(s32[1]{0:T(128)} %bitcast.me_ref, f32[128,1280]{1,0:T(8,128)S(1)} %copy-done.7, ...), custom_call_target="tpu_custom_call" | custom-call | flops 1 | bytes 1 | tf_op jit(solution)/shard_map/pallas_call | solution.py:983
  279.4 6.5 shard_map.318
  290.7 11.3 %shard_map.319 = (bf16[128,1280]{1,0:T(8,128)(2,1)S(1)}, bf16[4,128,320]{2,1,0:T(8,128)(2,1)S(1)}, bf16[128,1280]{1,0:T(8,128)(2,1)S(1)}, f32[128,1280]{1,0:T(8,128)S(1)}, f32[1,1280]{1,0:T(1,128)S(1)}) custom-call(s32[1]{0:T(128)} %bitcast.me_ref, bf16[128,1280]{1,0:T(8,128)(2,1)S(1)} %convert_element_type.630.top_ref.refs_0_.refs_1_, ...), custom_call_target="tpu_custom_call" | custom-call | flops 1 | bytes 1 | tf_op jit(solution)/shard_map/pallas_call | solution.py:505
  304.8 6.8 %shard_map.320 = (bf16[2,3,160,640]{3,2,1,0:T(8,128)(2,1)}, bf16[2,3,160,640]{3,2,1,0:T(8,128)(2,1)S(1)}, bf16[2,3,160,640]{3,2,1,0:T(8,128)(2,1)S(1)}, bf16[3,160,1280]{2,1,0:T(8,128)(2,1)S(1)}) custom-call(s32[1]{0:T(128)} %bitcast.me_ref, bf16[128,1280]{1,0:T(8,128)(2,1)S(1)} %convert_element_type.630.top_ref.refs_0_.refs_1_, ...), custom_call_target="tpu_custom_call" | custom-call | flops 1 | bytes 1 | tf_op jit(solution)/shard_map/pallas_call | solution.py:302
  316.0 10.5 %shard_map.321 = (f32[128,1280]{1,0:T(8,128)S(1)}, bf16[128,1280]{1,0:T(8,128)(2,1)S(1)}, bf16[128,1280]{1,0:T(8,128)(2,1)S(1)}, bf16[128,1280]{1,0:T(8,128)(2,1...) custom-call(s32[1]{0:T(128)} %bitcast.me_ref, ...), custom_call_target="tpu_custom_call" | custom-call | flops 1 | bytes 1 | tf_op jit(solution)/shard_map/pallas_call | solution.py:983
  329.8 12.6 %collective-permute-done.55 = bf16[2,3,160,640]{3,2,1,0:T(8,128)(2,1)} collective-permute-done((bf16[2,3,160,640]{3,2,1,0:T(8,128)(2,1)}, bf16[2,3,160,640]{3,2,1,0:T(8,128)(2,1)}, u32[]{:S(2)}, u32[]{:S(2)}) %collective-permute-start.55) | collective-permute-done | bytes 1228832 | tf_op jit(solution)/shard_map/ppermute | solution.py:129
  346.8 7.4 %shard_map.322 = (bf16[2,3,160,640]{3,2,1,0:T(8,128)(2,1)}, bf16[2,3,160,640]{3,2,1,0:T(8,128)(2,1)}, bf16[2,3,160,640]{3,2,1,0:T(8,128)(2,1)S(1)}, bf16[3,160,1280]{2,1,0:T(8,128)(2,1)S(1)}) custom-call(s32[1]{0:T(128)} %bitcast.me_ref, bf16[128,1280]{1,0:T(8,128)(2,1)S(1)} %copy-done.54, bf16[128,1280]{1,0:T(8,128)(2,1)S(1)} %copy-done.114, ...), custom_call_target="tpu_custom_call" | custom-call | flops 1 | bytes 1 | tf_op jit(solution)/shard_map/pallas_call | solution.py:302
  354.2 5.5 collective-permute-done.57
  364.0 10.7 %shard_map.323 = (f32[128,1280]{1,0:T(8,128)S(1)}, bf16[128,3840]{1,0:T(8,128)(2,1)S(1)}, f32[1,1280]{1,0:T(1,128)S(1)}) custom-call(s32[1]{0:T(128)} %bitcast.me_ref, f32[128,1280]{1,0:T(8,128)S(1)} %get-tuple-element.411.grad_middle_ref, bf16[128,1280]{1,0:T(8,128)(2,1)S(1)} %copy-done.116, f32[128,1280]{1,0:T(8,128)S(1)} %copy-done.9, ...), custom_call_target="tpu_custom_call" | custom-call | flops 1 | bytes 1 | tf_op jit(solution)/shard_map/pallas_call | solution.py:983
  376.1 10.5 %shard_map.324 = (f32[128,1280]{1,0:T(8,128)S(1)}, bf16[128,1280]{1,0:T(8,128)(2,1)S(1)}, bf16[128,1280]{1,0:T(8,128)(2,1)S(1)}, bf16[128,1280]{1,0:T(8,128)(2,1...) custom-call(s32[1]{0:T(128)} %bitcast.me_ref, ...), custom_call_target="tpu_custom_call" | custom-call | flops 1 | bytes 1 | tf_op jit(solution)/shard_map/pallas_call | solution.py:983
  395.1 5.6 shard_map.325
  400.7 7.9 %collective-permute-done.69 = bf16[3,160,640]{2,1,0:T(8,128)(2,1)S(1)} collective-permute-done((bf16[3,160,640]{2,1,0:T(8,128)(2,1)S(1)}, bf16[3,160,640]{2,1,0:T(8,128)(2,1)S(1)}, u32[]{:S(2)}, u32[]{:S(2)}) %collective-permute-start.69) | collective-permute-done | bytes 614432 | tf_op jit(solution)/shard_map/ppermute | solution.py:129
  422.3 10.8 %shard_map.326 = (f32[128,1280]{1,0:T(8,128)S(1)}, bf16[128,3840]{1,0:T(8,128)(2,1)}, f32[1,1280]{1,0:T(1,128)S(1)}) custom-call(s32[1]{0:T(128)} %bitcast.me_ref, f32[128,1280]{1,0:T(8,128)S(1)} %copy-done.67, bf16[128,1280]{1,0:T(8,128)(2,1)S(1)} %copy-done.88, f32[128,1280]{1,0:T(8,128)S(1)} %fusion.resid_ref, bf16[128,1280]{1,0:T(8,128)(2,1)S(1)} %copy-done.82, ...), custom_call_target="tpu_custom_call" | custom-call | flops 1 | bytes 1 | tf_op jit(solution)/shard_map/pallas_call | solution.py:983
  433.7 2.6 shard_map.327
  442.7 3.3 reshape.508
  454.1 3.2 shard_map.328
  459.0 7.8 %shard_map.329 = (bf16[2,3,160,640]{3,2,1,0:T(8,128)(2,1)}, bf16[2,3,160,640]{3,2,1,0:T(8,128)(2,1)S(1)}, bf16[2,3,160,640]{3,2,1,0:T(8,128)(2,1)S(1)}, bf16[3,160,1280]{2,1,0:T(8,128)(2,1)S(1)}) custom-call(s32[1]{0:T(128)} %bitcast.me_ref, bf16[128,1280]{1,0:T(8,128)(2,1)S(1)} %copy-done.51, bf16[128,1280]{1,0:T(8,128)(2,1)} %get-tuple-element.517.refs_1_, ...), custom_call_target="tpu_custom_call" | custom-call | flops 1 | bytes 1 | tf_op jit(solution)/shard_map/pallas_call | solution.py:302
  478.4 3.4 reduce-scatter.9.cloned.1.call-done
  481.9 16.3 %collective-permute-done.86 = bf16[2,3,160,640]{3,2,1,0:T(8,128)(2,1)} collective-permute-done((bf16[2,3,160,640]{3,2,1,0:T(8,128)(2,1)}, bf16[2,3,160,640]{3,2,1,0:T(8,128)(2,1)}, u32[]{:S(2)}, u32[]{:S(2)}) %collective-permute-start.86) | collective-permute-done | bytes 1228832 | tf_op jit(solution)/shard_map/ppermute | solution.py:129
  498.8 2.7 fusion.29
  503.3 6.0 collective-permute-done.84
  514.1 5.0 all-to-all-start.1
  522.2 7.3 %shard_map.330 = (bf16[2,1,160,1920]{3,2,1,0:T(8,128)(2,1)}, bf16[2,1,160,1920]{3,2,1,0:T(8,128)(2,1)}, bf16[2,1,160,1920]{3,2,1,0:T(8,128)(2,1)S(1)}, bf16[1,160,3840]{2,1,0:T(8,128)(2,1)S(1)}) custom-call(s32[1]{0:T(128)} %bitcast.me_ref, bf16[128,1280]{1,0:T(8,128)(2,1)S(1)} %copy-done.123, bf16[128,3840]{1,0:T(8,128)(2,1)} %get-tuple-element.555.refs_1_, ...), custom_call_target="tpu_custom_call" | custom-call | flops 1 | bytes 1 | tf_op jit(solution)/shard_map/pallas_call | solution.py:302
  539.3 5.1 all-to-all-start.2
  546.1 22.3 %all-to-all-done.2 = bf16[4,48,1280]{2,1,0:T(8,128)(2,1)S(1)} async-done(((bf16[4,48,1280]{2,1,0:T(8,128)(2,1)}), bf16[4,48,1280]{2,1,0:T(8,128)(2,1)S(1)}, u32[]{:S(2)}, u32[]{:S(2)}) %all-to-all-start.2) | async-done | bytes 491552 | tf_op jit(solution)/shard_map/all_to_all | solution.py:379
  569.2 3.6 all-to-all-start.3
  573.0 2.6 fusion.30
  575.6 3.3 collective-permute-start.101
  585.2 2.3 collective-permute-start.93
  587.5 4.3 collective-permute-done.102
  593.9 9.2 %collective-permute-done.93.refs_4_ = bf16[1,192,1280]{2,1,0:T(8,128)(2,1)S(1)} collective-permute-done((bf16[1,192,1280]{2,1,0:T(8,128)(2,1)S(1)}, bf16[1,192,1280]{2,1,0:T(8,128)(2,1)S(1)}, u32[]{:S(2)}, u32[]{:S(2)}) %collective-permute-start.93) | collective-permute-done | bytes 491552 | tf_op jit(solution)/shard_map/ppermute | solution.py:129
  607.9 4.9 all-to-all-start.4
  613.3 2.6 collective-permute-done.95.refs_6_
  623.4 6.8 %shard_map.331 = (f32[32,40,1280]{2,1,0:T(8,128)}, f32[32,8,1280]{2,1,0:T(8,128)S(1)}) custom-call(s32[1]{0:T(128)} %bitcast.me_ref, bf16[1,192,1280]{2,1,0:T(8,128)(2,1)S(1)} %bitcast.180, bf16[1,192,1280]{2,1,0:T(8,128)(2,1)S(1)} %collective-permute-done.90.refs_1_, bf16[1,192,1280]{2,1,0:T(8,128)(2,1)S(1)} %collective-permute-done.91.refs_2_, ...), custom_call_target="tpu_custom_call" | custom-call | flops 1 | bytes 1 | tf_op jit(solution)/shard_map/pallas_call | solution.py:741
  633.1 8.0 %all-to-all-done.4 = bf16[1,4,40,3840]{3,2,0,1:T(8,128)(2,1)} async-done(((bf16[1,4,40,3840]{3,2,0,1:T(8,128)(2,1)}), bf16[1,4,40,3840]{3,2,0,1:T(8,128)(2,1)}, u32[]{:S(2)}, u32[]{:S(2)}) %all-to-all-start.4) | async-done | bytes 1228832 | tf_op jit(solution)/shard_map/all_to_all | solution.py:379
  (698 shorter events, 231.1 us)
Async XLA Ops:
  7.2 37.7 %all-gather.10.cloned.1.call-start = ((), (), s32[]{:S(2)}) async-start(), calls=%async_computation.10 | async-start | bytes 1587200 | tf_op jit(solution)/shard_map/all_gather | solution.py:214
  10.1 67.3 %all-gather.8.cloned.1.call-start = ((), (), s32[]{:S(2)}) async-start(), calls=%async_computation.9 | async-start | bytes 1536000 | tf_op jit(solution)/shard_map/all_gather | solution.py:214
  12.3 108.5 %all-gather.12.cloned.1.call-start = ((), (), s32[]{:S(2)}) async-start(), calls=%async_computation.11 | async-start | bytes 1536000 | tf_op jit(solution)/shard_map/all_gather | solution.py:214
  44.9 32.5 %collective-permute-start = (bf16[1,160,3968]{2,1,0:T(8,128)(2,1)}, bf16[1,160,3968]{2,1,0:T(8,128)(2,1)S(1)}, u32[]{:S(2)}, u32[]{:S(2)}) collective-permute-start(bf16[1,160,3968]{2,1,0:T(8,128)(2,1)} %bitcast.20.refs_0_), channel_id=1, source_target_pairs={{0,8},{4,12},{8,0},{12,4},{16,24},{20,28},{24,16},{28,20},{1,9},{5... | collective-permute-start | bytes 3809288 | tf_op jit(solution)/shard_map/ppermute | solution.py:129
  46.4 31.0 %collective-permute-start.1 = (bf16[1,160,3968]{2,1,0:T(8,128)(2,1)}, bf16[1,160,3968]{2,1,0:T(8,128)(2,1)S(1)}, u32[]{:S(2)}, u32[]{:S(2)}) collective-permute-start(bf16[1,160,3968]{2,1,0:T(8,128)(2,1)} %bitcast.20.refs_0_), channel_id=1, source_target_pairs={{0,16},{4,20},{8,24},{12,28},{16,0},{20,4},{24,8},{28,12},{1,17},{... | collective-permute-start | bytes 3809288 | tf_op jit(solution)/shard_map/ppermute | solution.py:129
  77.5 90.9 %all-gather.14.cloned.1.call-start = ((), (), s32[]{:S(2)}) async-start(), calls=%async_computation.12 | async-start | bytes 1536000 | tf_op jit(solution)/shard_map/all_gather | solution.py:214
  80.7 38.8 %collective-permute-start.4 = (bf16[1,160,3840]{2,1,0:T(8,128)(2,1)S(1)}, bf16[1,160,3840]{2,1,0:T(8,128)(2,1)}, u32[]{:S(2)}, u32[]{:S(2)}) collective-permute-start(bf16[1,160,3840]{2,1,0:T(8,128)(2,1)S(1)} %bitcast.168), channel_id=1, source_target_pairs={{0,8},{4,12},{8,0},{12,4},{16,24},{20,28},{24,16},{28,20},{1,9},{5... | collective-permute-start | bytes 3686408 | tf_op jit(solution)/shard_map/ppermute | solution.py:129
  81.3 39.6 %collective-permute-start.5 = (bf16[1,160,3840]{2,1,0:T(8,128)(2,1)S(1)}, bf16[1,160,3840]{2,1,0:T(8,128)(2,1)}, u32[]{:S(2)}, u32[]{:S(2)}) collective-permute-start(bf16[1,160,3840]{2,1,0:T(8,128)(2,1)S(1)} %bitcast.169), channel_id=1, source_target_pairs={{0,16},{4,20},{8,24},{12,28},{16,0},{20,4},{24,8},{28,12},{1,17},{... | collective-permute-start | bytes 3686408 | tf_op jit(solution)/shard_map/ppermute | solution.py:129
  82.6 44.5 %collective-permute-start.8 = (bf16[1,160,3968]{2,1,0:T(8,128)(2,1)}, bf16[1,160,3968]{2,1,0:T(8,128)(2,1)}, u32[]{:S(2)}, u32[]{:S(2)}) collective-permute-start(bf16[1,160,3968]{2,1,0:T(8,128)(2,1)} %bitcast.20.refs_0_), channel_id=1, source_target_pairs={{0,4},{4,0},{8,12},{12,8},{16,20},{20,16},{24,28},{28,24},{1,5},{5... | collective-permute-start | bytes 3809288 | tf_op jit(solution)/shard_map/ppermute | solution.py:129
  94.9 32.2 %collective-permute-start.9 = (bf16[1,160,3968]{2,1,0:T(8,128)(2,1)S(1)}, bf16[1,160,3968]{2,1,0:T(8,128)(2,1)}, u32[]{:S(2)}, u32[]{:S(2)}) collective-permute-start(bf16[1,160,3968]{2,1,0:T(8,128)(2,1)S(1)} %collective-permute-done.refs_2_), channel_id=1, source_target_pairs={{0,4},{4,0},{8,12},{12,8},{16,20},{20,16},{24,28},{28,24},{1,5},{5... | collective-permute-start | bytes 3809288 | tf_op jit(solution)/shard_map/ppermute | solution.py:129
  96.5 31.2 %collective-permute-start.10 = (bf16[1,160,3968]{2,1,0:T(8,128)(2,1)S(1)}, bf16[1,160,3968]{2,1,0:T(8,128)(2,1)}, u32[]{:S(2)}, u32[]{:S(2)}) collective-permute-start(bf16[1,160,3968]{2,1,0:T(8,128)(2,1)S(1)} %collective-permute-done.1.refs_4_), channel_id=1, source_target_pairs={{0,4},{4,0},{8,12},{12,8},{16,20},{20,16},{24,28},{28,24},{1,5},{5... | collective-permute-start | bytes 3809288 | tf_op jit(solution)/shard_map/ppermute | solution.py:129
  123.3 92.8 %all-gather.16.cloned.1.call-start = ((), (), s32[]{:S(2)}) async-start(), calls=%async_computation.13 | async-start | bytes 1638400 | tf_op jit(solution)/shard_map/all_gather | solution.py:1275
  127.6 40.7 %collective-permute-start.13 = (bf16[1,160,3840]{2,1,0:T(8,128)(2,1)}, bf16[1,160,3840]{2,1,0:T(8,128)(2,1)}, u32[]{:S(2)}, u32[]{:S(2)}) collective-permute-start(bf16[1,160,3840]{2,1,0:T(8,128)(2,1)} %bitcast.172), channel_id=1, source_target_pairs={{0,8},{4,12},{8,0},{12,4},{16,24},{20,28},{24,16},{28,20},{1,9},{5... | collective-permute-start | bytes 3686408 | tf_op jit(solution)/shard_map/ppermute | solution.py:129
  139.9 28.5 %collective-permute-start.14 = (bf16[1,160,3840]{2,1,0:T(8,128)(2,1)}, bf16[1,160,3840]{2,1,0:T(8,128)(2,1)}, u32[]{:S(2)}, u32[]{:S(2)}) collective-permute-start(bf16[1,160,3840]{2,1,0:T(8,128)(2,1)} %bitcast.173), channel_id=1, source_target_pairs={{0,16},{4,20},{8,24},{12,28},{16,0},{20,4},{24,8},{28,12},{1,17},{... | collective-permute-start | bytes 3686408 | tf_op jit(solution)/shard_map/ppermute | solution.py:129
  141.9 33.3 %collective-permute-start.17 = (bf16[1,160,3840]{2,1,0:T(8,128)(2,1)}, bf16[1,160,3840]{2,1,0:T(8,128)(2,1)}, u32[]{:S(2)}, u32[]{:S(2)}) collective-permute-start(bf16[1,160,3840]{2,1,0:T(8,128)(2,1)} %bitcast.167), channel_id=1, source_target_pairs={{0,4},{4,0},{8,12},{12,8},{16,20},{20,16},{24,28},{28,24},{1,5},{5... | collective-permute-start | bytes 3686408 | tf_op jit(solution)/shard_map/ppermute | solution.py:129
  144.2 31.1 %collective-permute-start.18 = (bf16[1,160,3840]{2,1,0:T(8,128)(2,1)}, bf16[1,160,3840]{2,1,0:T(8,128)(2,1)}, u32[]{:S(2)}, u32[]{:S(2)}) collective-permute-start(bf16[1,160,3840]{2,1,0:T(8,128)(2,1)} %collective-permute-done.4.refs_2_), channel_id=1, source_target_pairs={{0,4},{4,0},{8,12},{12,8},{16,20},{20,16},{24,28},{28,24},{1,5},{5... | collective-permute-start | bytes 3686408 | tf_op jit(solution)/shard_map/ppermute | solution.py:129
  144.7 30.7 %collective-permute-start.19 = (bf16[1,160,3840]{2,1,0:T(8,128)(2,1)}, bf16[1,160,3840]{2,1,0:T(8,128)(2,1)}, u32[]{:S(2)}, u32[]{:S(2)}) collective-permute-start(bf16[1,160,3840]{2,1,0:T(8,128)(2,1)} %collective-permute-done.5.refs_4_), channel_id=1, source_target_pairs={{0,4},{4,0},{8,12},{12,8},{16,20},{20,16},{24,28},{28,24},{1,5},{5... | collective-permute-start | bytes 3686408 | tf_op jit(solution)/shard_map/ppermute | solution.py:129
  175.3 38.3 %collective-permute-start.22 = (bf16[1,160,3840]{2,1,0:T(8,128)(2,1)}, bf16[1,160,3840]{2,1,0:T(8,128)(2,1)S(1)}, u32[]{:S(2)}, u32[]{:S(2)}) collective-permute-start(bf16[1,160,3840]{2,1,0:T(8,128)(2,1)} %bitcast.26.refs_0_), channel_id=1, source_target_pairs={{0,8},{4,12},{8,0},{12,4},{16,24},{20,28},{24,16},{28,20},{1,9},{5... | collective-permute-start | bytes 3686408 | tf_op jit(solution)/shard_map/ppermute | solution.py:129
  175.4 40.7 %collective-permute-start.23 = (bf16[1,160,3840]{2,1,0:T(8,128)(2,1)}, bf16[1,160,3840]{2,1,0:T(8,128)(2,1)}, u32[]{:S(2)}, u32[]{:S(2)}) collective-permute-start(bf16[1,160,3840]{2,1,0:T(8,128)(2,1)} %bitcast.26.refs_0_), channel_id=1, source_target_pairs={{0,16},{4,20},{8,24},{12,28},{16,0},{20,4},{24,8},{28,12},{1,17},{... | collective-permute-start | bytes 3686408 | tf_op jit(solution)/shard_map/ppermute | solution.py:129
  190.6 28.6 %collective-permute-start.26 = (bf16[1,160,3840]{2,1,0:T(8,128)(2,1)}, bf16[1,160,3840]{2,1,0:T(8,128)(2,1)}, u32[]{:S(2)}, u32[]{:S(2)}) collective-permute-start(bf16[1,160,3840]{2,1,0:T(8,128)(2,1)} %bitcast.174), channel_id=1, source_target_pairs={{0,4},{4,0},{8,12},{12,8},{16,20},{20,16},{24,28},{28,24},{1,5},{5... | collective-permute-start | bytes 3686408 | tf_op jit(solution)/shard_map/ppermute | solution.py:129
  190.6 28.6 %collective-permute-start.27 = (bf16[1,160,3840]{2,1,0:T(8,128)(2,1)}, bf16[1,160,3840]{2,1,0:T(8,128)(2,1)}, u32[]{:S(2)}, u32[]{:S(2)}) collective-permute-start(bf16[1,160,3840]{2,1,0:T(8,128)(2,1)} %collective-permute-done.13.refs_2_), channel_id=1, source_target_pairs={{0,4},{4,0},{8,12},{12,8},{16,20},{20,16},{24,28},{28,24},{1,5},{5... | collective-permute-start | bytes 3686408 | tf_op jit(solution)/shard_map/ppermute | solution.py:129
  191.1 28.6 %collective-permute-start.28 = (bf16[1,160,3840]{2,1,0:T(8,128)(2,1)}, bf16[1,160,3840]{2,1,0:T(8,128)(2,1)}, u32[]{:S(2)}, u32[]{:S(2)}) collective-permute-start(bf16[1,160,3840]{2,1,0:T(8,128)(2,1)} %collective-permute-done.14.refs_4_), channel_id=1, source_target_pairs={{0,4},{4,0},{8,12},{12,8},{16,20},{20,16},{24,28},{28,24},{1,5},{5... | collective-permute-start | bytes 3686408 | tf_op jit(solution)/shard_map/ppermute | solution.py:129
  219.7 43.5 %collective-permute-start.31 = (bf16[4,160,960]{2,1,0:T(8,128)(2,1)}, bf16[4,160,960]{2,1,0:T(8,128)(2,1)}, u32[]{:S(2)}, u32[]{:S(2)}) collective-permute-start(bf16[4,160,960]{2,1,0:T(8,128)(2,1)} %all-gather.16.cloned.1.call-done.refs_0_), channel_id=1, source_target_pairs={{0,8},{4,12},{8,0},{12,4},{16,24},{20,28},{24,16},{28,20},{1,9},{5... | collective-permute-start | bytes 3686408 | tf_op jit(solution)/shard_map/ppermute | solution.py:129
  234.1 29.1 %collective-permute-start.32 = (bf16[4,160,960]{2,1,0:T(8,128)(2,1)}, bf16[4,160,960]{2,1,0:T(8,128)(2,1)}, u32[]{:S(2)}, u32[]{:S(2)}) collective-permute-start(bf16[4,160,960]{2,1,0:T(8,128)(2,1)} %all-gather.16.cloned.1.call-done.refs_0_), channel_id=1, source_target_pairs={{0,16},{4,20},{8,24},{12,28},{16,0},{20,4},{24,8},{28,12},{1,17},{... | collective-permute-start | bytes 3686408 | tf_op jit(solution)/shard_map/ppermute | solution.py:129
  235.7 32.1 %collective-permute-start.35 = (bf16[1,160,3840]{2,1,0:T(8,128)(2,1)}, bf16[1,160,3840]{2,1,0:T(8,128)(2,1)}, u32[]{:S(2)}, u32[]{:S(2)}) collective-permute-start(bf16[1,160,3840]{2,1,0:T(8,128)(2,1)} %bitcast.26.refs_0_), channel_id=1, source_target_pairs={{0,4},{4,0},{8,12},{12,8},{16,20},{20,16},{24,28},{28,24},{1,5},{5... | collective-permute-start | bytes 3686408 | tf_op jit(solution)/shard_map/ppermute | solution.py:129
  236.7 31.4 %collective-permute-start.36 = (bf16[1,160,3840]{2,1,0:T(8,128)(2,1)S(1)}, bf16[1,160,3840]{2,1,0:T(8,128)(2,1)}, u32[]{:S(2)}, u32[]{:S(2)}) collective-permute-start(bf16[1,160,3840]{2,1,0:T(8,128)(2,1)S(1)} %collective-permute-done.22.refs_2_), channel_id=1, source_target_pairs={{0,4},{4,0},{8,12},{12,8},{16,20},{20,16},{24,28},{28,24},{1,5},{5... | collective-permute-start | bytes 3686408 | tf_op jit(solution)/shard_map/ppermute | solution.py:129
  239.0 29.8 %collective-permute-start.37 = (bf16[1,160,3840]{2,1,0:T(8,128)(2,1)}, bf16[1,160,3840]{2,1,0:T(8,128)(2,1)}, u32[]{:S(2)}, u32[]{:S(2)}) collective-permute-start(bf16[1,160,3840]{2,1,0:T(8,128)(2,1)} %collective-permute-done.23.refs_4_), channel_id=1, source_target_pairs={{0,4},{4,0},{8,12},{12,8},{16,20},{20,16},{24,28},{28,24},{1,5},{5... | collective-permute-start | bytes 3686408 | tf_op jit(solution)/shard_map/ppermute | solution.py:129
  245.1 229.8 %reduce-scatter.13.cloned.1.call-start = ((), (), s32[]{:S(2)}) async-start(), calls=%async_computation.17 | async-start | bytes 1536000
  312.7 29.6 %collective-permute-start.55 = (bf16[2,3,160,640]{3,2,1,0:T(8,128)(2,1)}, bf16[2,3,160,640]{3,2,1,0:T(8,128)(2,1)}, u32[]{:S(2)}, u32[]{:S(2)}) collective-permute-start(bf16[2,3,160,640]{3,2,1,0:T(8,128)(2,1)} %get-tuple-element.385), channel_id=1, source_target_pairs={{0,8},{4,12},{8,0},{12,4},{16,24},{20,28},{24,16},{28,20},{1,9},{5... | collective-permute-start | bytes 3686408 | tf_op jit(solution)/shard_map/ppermute | solution.py:129
  314.0 29.1 %collective-permute-start.56 = (bf16[2,3,160,640]{3,2,1,0:T(8,128)(2,1)S(1)}, bf16[2,3,160,640]{3,2,1,0:T(8,128)(2,1)}, u32[]{:S(2)}, u32[]{:S(2)}) collective-permute-start(bf16[2,3,160,640]{3,2,1,0:T(8,128)(2,1)S(1)} %get-tuple-element.386), channel_id=1, source_target_pairs={{0,16},{4,20},{8,24},{12,28},{16,0},{20,4},{24,8},{28,12},{1,17},{... | collective-permute-start | bytes 3686408 | tf_op jit(solution)/shard_map/ppermute | solution.py:129
  346.8 28.5 %collective-permute-start.61 = (bf16[128,1280]{1,0:T(8,128)(2,1)S(1)}, bf16[128,1280]{1,0:T(8,128)(2,1)S(1)}, u32[]{:S(2)}, u32[]{:S(2)}) collective-permute-start(bf16[128,1280]{1,0:T(8,128)(2,1)S(1)} %copy-done.50), channel_id=1, source_target_pairs={{0,4},{4,0},{8,12},{12,8},{16,20},{20,16},{24,28},{28,24},{1,5},{5... | collective-permute-start | bytes 983048 | tf_op jit(solution)/shard_map/ppermute | solution.py:129
  361.0 29.6 %collective-permute-start.67 = (bf16[2,3,160,640]{3,2,1,0:T(8,128)(2,1)}, bf16[2,3,160,640]{3,2,1,0:T(8,128)(2,1)}, u32[]{:S(2)}, u32[]{:S(2)}) collective-permute-start(bf16[2,3,160,640]{3,2,1,0:T(8,128)(2,1)} %get-tuple-element.428), channel_id=1, source_target_pairs={{0,8},{4,12},{8,0},{12,4},{16,24},{20,28},{24,16},{28,20},{1,9},{5... | collective-permute-start | bytes 3686408 | tf_op jit(solution)/shard_map/ppermute | solution.py:129
  361.8 28.7 %collective-permute-start.68 = (bf16[2,3,160,640]{3,2,1,0:T(8,128)(2,1)}, bf16[2,3,160,640]{3,2,1,0:T(8,128)(2,1)}, u32[]{:S(2)}, u32[]{:S(2)}) collective-permute-start(bf16[2,3,160,640]{3,2,1,0:T(8,128)(2,1)} %get-tuple-element.429), channel_id=1, source_target_pairs={{0,16},{4,20},{8,24},{12,28},{16,0},{20,4},{24,8},{28,12},{1,17},{... | collective-permute-start | bytes 3686408 | tf_op jit(solution)/shard_map/ppermute | solution.py:129
  413.9 67.9 %reduce-scatter.9.cloned.1.call-start = ((), (), s32[]{:S(2)}) async-start(), calls=%async_computation.14 | async-start | bytes 1843200 | tf_op jit(solution)/shard_map/reduce_scatter | solution.py:389
  414.0 33.6 %collective-permute-start.78 = (bf16[2,1,160,1920]{3,2,1,0:T(8,128)(2,1)}, bf16[2,1,160,1920]{3,2,1,0:T(8,128)(2,1)}, u32[]{:S(2)}, u32[]{:S(2)}) collective-permute-start(bf16[2,1,160,1920]{3,2,1,0:T(8,128)(2,1)} %copy-done.150), channel_id=1, source_target_pairs={{0,8},{4,12},{8,0},{12,4},{16,24},{20,28},{24,16},{28,20},{1,9},{5... | collective-permute-start | bytes 3686408 | tf_op jit(solution)/shard_map/ppermute | solution.py:129
  415.2 32.3 %collective-permute-start.79 = (bf16[2,1,160,1920]{3,2,1,0:T(8,128)(2,1)}, bf16[2,1,160,1920]{3,2,1,0:T(8,128)(2,1)}, u32[]{:S(2)}, u32[]{:S(2)}) collective-permute-start(bf16[2,1,160,1920]{3,2,1,0:T(8,128)(2,1)} %copy-done.149), channel_id=1, source_target_pairs={{0,16},{4,20},{8,24},{12,28},{16,0},{20,4},{24,8},{28,12},{1,17},{... | collective-permute-start | bytes 3686408 | tf_op jit(solution)/shard_map/ppermute | solution.py:129
  447.4 125.5 %reduce-scatter.11.cloned.1.call-start = ((), (), s32[]{:S(2)}) async-start(), calls=%async_computation.15 | async-start | bytes 1536000 | tf_op jit(solution)/shard_map/reduce_scatter | solution.py:367
  467.9 30.3 %collective-permute-start.86 = (bf16[2,3,160,640]{3,2,1,0:T(8,128)(2,1)}, bf16[2,3,160,640]{3,2,1,0:T(8,128)(2,1)}, u32[]{:S(2)}, u32[]{:S(2)}) collective-permute-start(bf16[2,3,160,640]{3,2,1,0:T(8,128)(2,1)} %get-tuple-element.546), channel_id=1, source_target_pairs={{0,8},{4,12},{8,0},{12,4},{16,24},{20,28},{24,16},{28,20},{1,9},{5... | collective-permute-start | bytes 3686408 | tf_op jit(solution)/shard_map/ppermute | solution.py:129
  468.7 30.1 %collective-permute-start.87 = (bf16[2,3,160,640]{3,2,1,0:T(8,128)(2,1)S(1)}, bf16[2,3,160,640]{3,2,1,0:T(8,128)(2,1)}, u32[]{:S(2)}, u32[]{:S(2)}) collective-permute-start(bf16[2,3,160,640]{3,2,1,0:T(8,128)(2,1)S(1)} %get-tuple-element.547), channel_id=1, source_target_pairs={{0,16},{4,20},{8,24},{12,28},{16,0},{20,4},{24,8},{28,12},{1,17},{... | collective-permute-start | bytes 3686408 | tf_op jit(solution)/shard_map/ppermute | solution.py:129
  472.2 37.1 %collective-permute-start.84 = (bf16[2,1,192,640]{3,2,1,0:T(8,128)(2,1)}, bf16[2,1,192,640]{3,2,1,0:T(8,128)(2,1)}, u32[]{:S(2)}, u32[]{:S(2)}) collective-permute-start(bf16[2,1,192,640]{3,2,1,0:T(8,128)(2,1)} %copy-done.152), channel_id=1, source_target_pairs={{0,16},{4,20},{8,24},{12,28},{16,0},{20,4},{24,8},{28,12},{1,17},{... | collective-permute-start | bytes 1474568 | tf_op jit(solution)/shard_map/ppermute | solution.py:129
  473.7 35.6 %collective-permute-start.82 = (bf16[2,1,192,640]{3,2,1,0:T(8,128)(2,1)}, bf16[2,1,192,640]{3,2,1,0:T(8,128)(2,1)}, u32[]{:S(2)}, u32[]{:S(2)}) collective-permute-start(bf16[2,1,192,640]{3,2,1,0:T(8,128)(2,1)} %copy-done.151), channel_id=1, source_target_pairs={{0,8},{4,12},{8,0},{12,4},{16,24},{20,28},{24,16},{28,20},{1,9},{5... | collective-permute-start | bytes 1474568 | tf_op jit(solution)/shard_map/ppermute | solution.py:129
  519.0 98.8 %reduce-scatter.15.cloned.1.call-start = ((), (), s32[]{:S(2)}) async-start(), calls=%async_computation.18 | async-start | bytes 1536000
  529.6 43.4 %collective-permute-start.99 = (bf16[2,1,160,1920]{3,2,1,0:T(8,128)(2,1)}, bf16[2,1,160,1920]{3,2,1,0:T(8,128)(2,1)}, u32[]{:S(2)}, u32[]{:S(2)}) collective-permute-start(bf16[2,1,160,1920]{3,2,1,0:T(8,128)(2,1)} %get-tuple-element.570), channel_id=1, source_target_pairs={{0,8},{4,12},{8,0},{12,4},{16,24},{20,28},{24,16},{28,20},{1,9},{5... | collective-permute-start | bytes 3686408 | tf_op jit(solution)/shard_map/ppermute | solution.py:129
  530.4 42.6 %collective-permute-start.100 = (bf16[2,1,160,1920]{3,2,1,0:T(8,128)(2,1)}, bf16[2,1,160,1920]{3,2,1,0:T(8,128)(2,1)}, u32[]{:S(2)}, u32[]{:S(2)}) collective-permute-start(bf16[2,1,160,1920]{3,2,1,0:T(8,128)(2,1)} %get-tuple-element.571), channel_id=1, source_target_pairs={{0,16},{4,20},{8,24},{12,28},{16,0},{20,4},{24,8},{28,12},{1,17},{... | collective-permute-start | bytes 3686408 | tf_op jit(solution)/shard_map/ppermute | solution.py:129
  539.3 29.1 %all-to-all-start.2 = ((bf16[4,48,1280]{2,1,0:T(8,128)(2,1)}), bf16[4,48,1280]{2,1,0:T(8,128)(2,1)S(1)}, u32[]{:S(2)}, u32[]{:S(2)}) async-start(bf16[4,48,1280]{2,1,0:T(8,128)(2,1)} %bitcast.51), calls=%async_computation.3 | async-start | bytes 983040 | tf_op jit(solution)/shard_map/all_to_all | solution.py:379
  572.9 70.9 %all-gather.18.cloned.1.call-start = ((), (), s32[]{:S(2)}) async-start(), calls=%async_computation.16 | async-start | bytes 3317760 | tf_op jit(solution)/shard_map/all_gather | solution.py:396
  582.9 40.4 %collective-permute-start.90 = (bf16[1,192,1280]{2,1,0:T(8,128)(2,1)S(1)}, bf16[1,192,1280]{2,1,0:T(8,128)(2,1)S(1)}, u32[]{:S(2)}, u32[]{:S(2)}) collective-permute-start(bf16[1,192,1280]{2,1,0:T(8,128)(2,1)S(1)} %bitcast.177), channel_id=1, source_target_pairs={{0,4},{4,0},{8,12},{12,8},{16,20},{20,16},{24,28},{28,24},{1,5},{5... | collective-permute-start | bytes 1474568 | tf_op jit(solution)/shard_map/ppermute | solution.py:129
  607.9 33.3 %all-to-all-start.4 = ((bf16[1,4,40,3840]{3,2,0,1:T(8,128)(2,1)}), bf16[1,4,40,3840]{3,2,0,1:T(8,128)(2,1)}, u32[]{:S(2)}, u32[]{:S(2)}) async-start(bf16[1,4,40,3840]{3,2,0,1:T(8,128)(2,1)} %bitcast.189), calls=%async_computation.6 | async-start | bytes 2457600 | tf_op jit(solution)/shard_map/all_to_all | solution.py:379
  (251 other events, 2355.1 us)
Sparse Core Ops, SparseCore 0:
  10.2 34.6 all-gather.9
  47.1 30.3 all-gather.7
  79.6 30.3 all-gather.11
  123.5 31.1 all-gather.13
  172.7 31.6 all-gather.15
  414.0 30.3 reduce-scatter.12
  447.5 34.2 reduce-scatter.8
  484.8 28.9 reduce-scatter.10
  536.3 38.1 reduce-scatter.14
  583.0 39.0 all-gather.17
